TPU v7x, 32 devices: a whole 2x2x4 slice. The times are simulated.
32 devices in a mesh: dp: 8 (over y, x, core), mlp: 4 (over z).
Axes of the slice: x: 2, y: 2, z: 4, core: 2. Of those that a mesh axis runs over, the one named last changes fastest.
Arguments:
- pixels: bfloat16 [8, 12, 196, 768], P('dp'), may hold values from -6 to 6
- lengths: int32 [8], P('dp'), may hold values from 4 to 12
- frame_mask: int32 [8, 12], P('dp'), may hold values 0 or 1
- time_index: int32 [8, 12], P('dp'), may hold values from 0 to 7
- label_valid: int32 [8, 400], P('dp'), may hold values from 0 to 1
- targets: float32 [8, 400], P('dp'), may hold values from 0 to 1
- owners: int32 [272], replicated, may hold values from 0 to 31, as said below
- slot_weight: float32 [13824, 768], P(('dp', 'mlp')), may hold values from -0.21875 to 0.21875
- slot_moment1: float32 [13824, 768], P(('dp', 'mlp')), may hold values from -4.7683716e-07 to 4.7683716e-07
- slot_moment2: float32 [13824, 768], P(('dp', 'mlp')), may hold values from 9.520937e-17 to 3.8083747e-16
- tables: float32 [220, 768], replicated
- table_moment1: float32 [220, 768], replicated, may hold values from -1.4305115e-06 to 1.4305115e-06
- table_moment2: float32 [220, 768], replicated, may hold values from 9.520937e-16 to 3.808375e-15
- head_weight: float32 [768, 400], replicated, may hold values from -0.625 to 0.625
- head_moment1: float32 [768, 400], replicated, may hold values from -4.7683716e-07 to 4.7683716e-07
- head_moment2: float32 [768, 400], replicated, may hold values from 9.520937e-17 to 3.8083747e-16
Outputs:
- loss_sum: float32 [], replicated
- label_total: float32 [], replicated
- grad_norm: float32 [], replicated
- new_slot_weight: float32 [13824, 768], P(('dp', 'mlp'))
- new_slot_moment1: float32 [13824, 768], P(('dp', 'mlp'))
- new_slot_moment2: float32 [13824, 768], P(('dp', 'mlp'))
- new_tables: float32 [220, 768], replicated
- new_table_moment1: float32 [220, 768], replicated
- new_table_moment2: float32 [220, 768], replicated
- new_head: float32 [768, 400], replicated
- new_head_moment1: float32 [768, 400], replicated
- new_head_moment2: float32 [768, 400], replicated
Inputs may be any that keep to these rules, and one draw needn't show every extreme that they name: `owners`: No device owns more than 9 blocks and some device owns exactly 9.
All inputs are finite; a program needn't handle non-finite values. No bound on the sum of `frame_mask` on one device may be relied on, other than what follows from the above.
Results may differ from a plain program's by a relative error of at most 0.0065.
Values may be sent and summed in bfloat16 or wider, within the bound.
No kernel may reach another device: no remote copies, remote signals or barrier semaphores. Data moves between devices by JAX's collectives and lax.ppermute only.
A program may use at most 384 MiB of HBM per device.

v0:
```python
from functools import partial

import jax
import jax.numpy as jnp
from jax import lax
from jax.sharding import PartitionSpec as P

HEADS = 12
HEAD_DIM = 64
TROWS = 8
FRAME_BLOCK = 4
BR = 48
STEP = 10


ln_eps = 1e-06
beta_one = 0.9
beta_two = 0.999
learn_rate = 0.05
table_rate = 0.4
decay_rate = 0.05
adam_eps = 1e-08
clip_max = 0.001
highest = lax.Precision.HIGHEST
time_forms = ("cfphd,cgphd->cphfg", "cphfg,cgphd->cfphd", "cphfg,cfphd->cgphd")
space_forms = ("fphd,fqhd->fhpq", "fhpq,fqhd->fphd", "fhpq,fphd->fqhd")


def matmul(left, right):
    return jnp.dot(left, right, preferred_element_type=jnp.float32)


def matmul_tn(left, right):
    return lax.dot_general(
        left, right, (((0,), (0,)), ((), ())), preferred_element_type=jnp.float32
    )


def matmul_nt(left, right):
    return lax.dot_general(
        left, right, (((1,), (1,)), ((), ())), preferred_element_type=jnp.float32
    )


def rounded(values):
    return values.astype(jnp.bfloat16).astype(jnp.float32)


def layer_norm(values, gain, shift):
    centred = values - jnp.mean(values, axis=-1, keepdims=True)
    return (
        centred * lax.rsqrt(jnp.mean(centred * centred, axis=-1, keepdims=True) + ln_eps) * gain
        + shift
    )


def block_ranks(owners):
    total_blocks = owners.shape[0]
    same_owner = owners[:, None] == owners[None, :]
    earlier = jnp.arange(total_blocks)[None, :] < jnp.arange(total_blocks)[:, None]
    return jnp.sum((same_owner & earlier).astype(jnp.int32), axis=1)


def adamw(weight, gradient, moment_one, moment_two, weight_decay, rate):
    first_new = beta_one * moment_one + (1.0 - beta_one) * gradient
    second_new = beta_two * moment_two + (1.0 - beta_two) * gradient * gradient
    mean_hat = first_new / (1.0 - beta_one**STEP)
    var_hat = second_new / (1.0 - beta_two**STEP)
    updated = weight - rate * (mean_hat / (jnp.sqrt(var_hat) + adam_eps) + weight_decay * weight)
    return (updated, first_new, second_new)


def score_block(queries, key_rows, forms, allowed):
    scores = jnp.einsum(
        forms[0], queries, key_rows, preferred_element_type=jnp.float32
    ) * HEAD_DIM ** (-0.5)
    if allowed is None:
        return scores
    return jnp.where(allowed, scores, -1e30)


def forward_block(items, forms, allowed):
    queries, key_rows, valued = items
    scores = score_block(queries, key_rows, forms, allowed)
    logsum = jax.nn.logsumexp(scores, axis=-1)
    softmax_b = jnp.exp(scores - logsum[..., None]).astype(jnp.bfloat16)
    return (jnp.einsum(forms[1], softmax_b, valued, preferred_element_type=jnp.float32), logsum)


def backward_block(items, forms, allowed):
    queries, key_rows, valued, grad_out, logsum = items
    scores = score_block(queries, key_rows, forms, allowed)
    softmax_w = jnp.exp(scores - logsum[..., None])
    grad_weights = jnp.einsum(forms[0], grad_out, valued, preferred_element_type=jnp.float32)
    grad_value = jnp.einsum(
        forms[2], softmax_w.astype(jnp.bfloat16), grad_out, preferred_element_type=jnp.float32
    )
    inner = jnp.sum(grad_weights * softmax_w, axis=-1, keepdims=True)
    grad_scores = (softmax_w * (grad_weights - inner)).astype(jnp.bfloat16)
    grad_query = jnp.einsum(
        forms[1], grad_scores, key_rows, preferred_element_type=jnp.float32
    ) * HEAD_DIM ** (-0.5)
    grad_key = jnp.einsum(
        forms[2], grad_scores, queries, preferred_element_type=jnp.float32
    ) * HEAD_DIM ** (-0.5)
    return (
        grad_query.astype(jnp.bfloat16),
        grad_key.astype(jnp.bfloat16),
        grad_value.astype(jnp.bfloat16),
    )


def to_heads(tensors, temporal, layout):
    clips, frames, patches = layout
    headed = tuple((tensor.reshape(clips, frames, patches, HEADS, HEAD_DIM) for tensor in tensors))
    if temporal:
        return headed
    return tuple((tensor.reshape(-1, FRAME_BLOCK, patches, HEADS, HEAD_DIM) for tensor in headed))


def attend_forward(triple, temporal, allowed, layout):
    headed = to_heads(triple, temporal, layout)
    if temporal:
        merged, logsum = forward_block(headed, time_forms, allowed)
    else:
        merged, logsum = lax.map(partial(forward_block, forms=space_forms, allowed=None), headed)
    return (merged.reshape(-1, HEADS * HEAD_DIM), logsum)


def attend_backward(quad, logsum, temporal, allowed, layout):
    headed = to_heads(quad, temporal, layout) + (logsum,)
    if temporal:
        results = backward_block(headed, time_forms, allowed)
    else:
        results = lax.map(partial(backward_block, forms=space_forms, allowed=None), headed)
    return tuple((tensor.reshape(-1, HEADS * HEAD_DIM) for tensor in results))


def attn_forward(stream, tile_set, row_set, temporal, allowed, layout):
    hidden_b = layer_norm(stream, row_set[0], row_set[1]).astype(jnp.bfloat16)
    queries = (matmul(hidden_b, tile_set[0]) + row_set[2]).astype(jnp.bfloat16)
    key_rows = matmul(hidden_b, tile_set[1]).astype(jnp.bfloat16)
    valued = (matmul(hidden_b, tile_set[2]) + row_set[3]).astype(jnp.bfloat16)
    merged, logsum = attend_forward((queries, key_rows, valued), temporal, allowed, layout)
    merged_b = merged.astype(jnp.bfloat16)
    return (
        stream + matmul(merged_b, tile_set[3]) + row_set[4],
        (hidden_b, queries, key_rows, valued, merged_b, logsum),
    )


def attn_backward(grad_stream, stream, kept, tile_set, row_set, temporal, allowed, layout):
    hidden_b, queries, key_rows, valued, merged_b, logsum = kept
    grad_out_b = grad_stream.astype(jnp.bfloat16)
    grad_merged = matmul_nt(grad_out_b, tile_set[3]).astype(jnp.bfloat16)
    grad_query, grad_key, grad_value = attend_backward(
        (queries, key_rows, valued, grad_merged), logsum, temporal, allowed, layout
    )
    grad_hidden = (
        matmul_nt(grad_query, tile_set[0])
        + matmul_nt(grad_key, tile_set[1])
        + matmul_nt(grad_value, tile_set[2])
    )
    unused, pullback = jax.vjp(layer_norm, stream, row_set[0], row_set[1])
    grad_in, grad_gain, grad_shift = pullback(grad_hidden)
    tile_grads = [
        matmul_tn(hidden_b, grad_query),
        matmul_tn(hidden_b, grad_key),
        matmul_tn(hidden_b, grad_value),
        matmul_tn(merged_b, grad_out_b),
    ]
    row_grads = [
        grad_gain,
        grad_shift,
        jnp.sum(grad_query.astype(jnp.float32), axis=0),
        jnp.sum(grad_value.astype(jnp.float32), axis=0),
        jnp.sum(grad_stream, axis=0),
    ]
    return (grad_stream + grad_in, tile_grads, row_grads)


def local(
    pixels,
    lengths,
    frame_mask,
    time_index,
    label_valid,
    targets,
    owners,
    slot_weight,
    slot_moment1,
    slot_moment2,
    tables,
    table_moment1,
    table_moment2,
    head_weight,
    head_moment1,
    head_moment2,
):
    dp_count = lax.axis_size("dp")
    mlp_count = lax.axis_size("mlp")
    member = lax.axis_index("mlp")
    width = slot_weight.shape[1]
    per_tile = width // BR
    slots = slot_weight.shape[0] // BR
    shared_blocks = 9 * per_tile
    own_copy = slot_weight.astype(jnp.bfloat16)
    gathered = lax.all_gather(own_copy, ("dp", "mlp"), axis=0, tiled=True)
    slot_index = owners * slots + block_ranks(owners)
    view_ids = jnp.arange(11 * per_tile)
    global_ids = jnp.where(view_ids < shared_blocks, view_ids, view_ids + member * 2 * per_tile)
    tiles = gathered.reshape(-1, BR, width)[slot_index[global_ids]].reshape(11, width, width)
    clips, frames, patches = (pixels.shape[0], pixels.shape[1], pixels.shape[2])
    layout = (clips, frames, patches)
    row_count = clips * frames * patches
    pix_rows = pixels.reshape(row_count, width)
    slot_pos = jnp.arange(frames)
    frame_live = slot_pos[None, :] < lengths[:, None]
    key_ok = frame_live & (frame_mask == 1)
    allowed = (key_ok[:, None, :] | (slot_pos[:, None] == slot_pos[None, :])[None])[:, None, None]
    time_hot = (time_index[:, :, None] == jnp.arange(TROWS)[None, None, :]).astype(jnp.float32)
    pos_rows = tables[16 : 16 + patches]
    time_rows = tables[16 + patches :]
    frame_add = jnp.einsum("cft,td->cfd", time_hot, time_rows, precision=highest)
    offsets = tables[0] + pos_rows[None, None] + frame_add[:, :, None]
    stream_embed = matmul(pix_rows, tiles[0]) + offsets.reshape(row_count, width)
    stream_time, kept_time = attn_forward(
        stream_embed, tiles[1:5], tables[1:6], True, allowed, layout
    )
    stream_space, kept_space = attn_forward(
        stream_time, tiles[5:9], tables[6:11], False, None, layout
    )
    hidden_mlp = layer_norm(stream_space, tables[11], tables[12]).astype(jnp.bfloat16)
    upper = matmul(hidden_mlp, tiles[9])
    active = jax.nn.gelu(upper).astype(jnp.bfloat16)
    mlp_sum = lax.psum(rounded(matmul(active, tiles[10])).astype(jnp.bfloat16), "mlp").astype(
        jnp.float32
    )
    stream_mlp = stream_space + mlp_sum + tables[13]
    final = layer_norm(stream_mlp, tables[14], tables[15])
    frame_weight = jnp.where(
        frame_live, 1.0 / (lengths * patches).astype(jnp.float32)[:, None], 0.0
    )
    pooled = jnp.sum(
        final.reshape(clips, frames, patches, width) * frame_weight[:, :, None, None], axis=(1, 2)
    )
    pooled_b = pooled.astype(jnp.bfloat16)
    head_b = head_weight.astype(jnp.bfloat16)
    logits = matmul(pooled_b, head_b)
    valid_f = label_valid.astype(jnp.float32)
    label_total = lax.psum(jnp.sum(valid_f), "dp")
    loss_local = jnp.sum(valid_f * (jax.nn.softplus(logits) - targets * logits))
    grad_logits = (
        valid_f * (jax.nn.sigmoid(logits) - targets) / jnp.maximum(label_total, 1.0)
    ).astype(jnp.bfloat16)
    grad_head = matmul_tn(pooled_b, grad_logits)
    grad_pooled = matmul_nt(grad_logits, head_b)
    spread_grad = grad_pooled[:, None, None, :] * frame_weight[:, :, None, None]
    grad_final = jnp.broadcast_to(spread_grad, (clips, frames, patches, width)).reshape(
        row_count, width
    )
    unused, pullback = jax.vjp(layer_norm, stream_mlp, tables[14], tables[15])
    grad_top, gain_final, shift_final = pullback(grad_final)
    grad_top_b = grad_top.astype(jnp.bfloat16)
    grad_down = matmul_tn(active, grad_top_b)
    unused, gelu_pull = jax.vjp(jax.nn.gelu, upper)
    grad_upper = gelu_pull(matmul_nt(grad_top_b, tiles[10]))[0].astype(jnp.bfloat16)
    grad_up = matmul_tn(hidden_mlp, grad_upper)
    grad_hidden = lax.psum(
        rounded(matmul_nt(grad_upper, tiles[9])).astype(jnp.bfloat16), "mlp"
    ).astype(jnp.float32)
    unused, pullback = jax.vjp(layer_norm, stream_space, tables[11], tables[12])
    grad_in, gain_mlp, shift_mlp = pullback(grad_hidden)
    grad_mid = grad_top + grad_in
    grad_after_time, tiles_space, rows_space = attn_backward(
        grad_mid, stream_time, kept_space, tiles[5:9], tables[6:11], False, None, layout
    )
    grad_embed_out, tiles_time, rows_time = attn_backward(
        grad_after_time, stream_embed, kept_time, tiles[1:5], tables[1:6], True, allowed, layout
    )
    grad_embed = matmul_tn(pix_rows, grad_embed_out.astype(jnp.bfloat16))
    grad_frames = jnp.sum(grad_embed_out.reshape(clips, frames, patches, width), axis=2)
    grad_pos = jnp.sum(grad_embed_out.reshape(clips * frames, patches, width), axis=0)
    grad_time = jnp.einsum("cft,cfd->td", time_hot, grad_frames, precision=highest)
    vectors = (
        [jnp.sum(grad_embed_out, axis=0)]
        + rows_time
        + rows_space
        + [gain_mlp, shift_mlp, jnp.sum(grad_top, axis=0), gain_final, shift_final]
    )
    grad_tables = jnp.concatenate([jnp.stack(vectors), grad_pos, grad_time])
    grad_tiles = jnp.stack([grad_embed] + tiles_time + tiles_space + [grad_up, grad_down])
    grad_tables, grad_head, loss_sum = lax.psum((grad_tables, grad_head, loss_local), "dp")
    grad_blocks = grad_tiles.reshape(11 * per_tile, BR, width)
    group_slots = (
        (jnp.arange(dp_count)[:, None] * mlp_count + member) * slots + jnp.arange(slots)[None, :]
    ).reshape(-1)
    matches = (slot_index[:, None] == group_slots[None, :]).astype(jnp.int32)
    block_found = jnp.sum(matches * (jnp.arange(owners.shape[0])[:, None] + 1), axis=0) - 1
    view_of_slot = jnp.where(
        block_found < shared_blocks, block_found, block_found - member * 2 * per_tile
    )
    filled = block_found >= 0
    chosen = grad_blocks[jnp.maximum(view_of_slot, 0)] * filled[:, None, None].astype(jnp.float32)
    own_grad = lax.psum_scatter(
        chosen.reshape(slots * BR * lax.axis_size("dp"), width),
        "dp",
        scatter_dimension=0,
        tiled=True,
    )
    squares_own = lax.psum(jnp.sum(own_grad * own_grad), ("dp", "mlp"))
    grad_norm = jnp.sqrt(
        squares_own + jnp.sum(grad_tables * grad_tables) + jnp.sum(grad_head * grad_head)
    )
    factor = jnp.minimum(1.0, clip_max / (grad_norm + 1e-06))
    new_slots = adamw(
        slot_weight, own_grad * factor, slot_moment1, slot_moment2, decay_rate, learn_rate
    )
    new_tabs = adamw(tables, grad_tables * factor, table_moment1, table_moment2, 0.0, table_rate)
    new_heads = adamw(
        head_weight, grad_head * factor, head_moment1, head_moment2, decay_rate, learn_rate
    )
    return (
        loss_sum,
        label_total,
        grad_norm,
        new_slots[0],
        new_slots[1],
        new_slots[2],
        new_tabs[0],
        new_tabs[1],
        new_tabs[2],
        new_heads[0],
        new_heads[1],
        new_heads[2],
    )


def solution(mesh):
    return jax.shard_map(
        local,
        mesh=mesh,
        in_specs=(
            P("dp", None, None, None),
            P("dp"),
            P("dp", None),
            P("dp", None),
            P("dp", None),
            P("dp", None),
            P(),
            P(("dp", "mlp"), None),
            P(("dp", "mlp"), None),
            P(("dp", "mlp"), None),
            P(),
            P(),
            P(),
            P(),
            P(),
            P(),
        ),
        out_specs=(
            P(),
            P(),
            P(),
            P(("dp", "mlp"), None),
            P(("dp", "mlp"), None),
            P(("dp", "mlp"), None),
            P(),
            P(),
            P(),
            P(),
            P(),
            P(),
        ),
        check_vma=False,
    )
```

profile of v0, /device:TPU:0, one launch (start us, length us, event | category | flops | bytes accessed | tf_op | source)
XLA Modules:
  0.0 1617.2 jit_solution(1034030882156134481)
XLA Ops:
  35.6 114.4 %all-gather.2.cloned.1.call-done = bf16[13824,768]{1,0:T(8,128)(2,1)} async-done(((bf16[432,768]{1,0:T(8,128)(2,1)}), bf16[13824,768]{1,0:T(8,128)(2,1)}) %all-gather.2.cloned.1.call-update) | async-done | bytes 21233680 | tf_op jit(solution)/shard_map/all_gather | solution.py:208
  150.0 15.7 gather_fusion.1
  189.5 12.0 reshape.715
  208.4 11.8 reshape.716
  220.2 19.4 %fusion.55 = (f32[196,12,12]{2,1,0:T(8,128)S(1)}, f32[196,12,12,12]{2,3,1,0:T(8,128)}) fusion(pred[12,12]{0,1:T(8,128)(4,1)S(1)} %fusion.120, bf16[12,196,12,64]{3,2,1,0:T(8,128)(2,1)} %reshape.716, bf16[12,196,12,64]{3,2,1,0:T(8,128)(2,1)} %reshape.715), kind=kOutput, calls=%fused_computation.72 | convolution fusion | flops 44339904 | bytes 8693136 | tf_op jit(solution)/shard_map/cfphd,cgphd->cphfg/dot_general | solution.py:74
  256.0 11.9 reshape.714
  267.9 16.7 %convert_bitcast_fusion.1 = bf16[1,12,196,12,64]{4,1,3,2,0:T(8,128)(2,1)} fusion(bf16[12,196,12,64]{3,2,1,0:T(8,128)(2,1)} %reshape.714, f32[196,12,12,12]{2,3,1,0:T(8,128)} %get-tuple-element.256, f32[196,12,12]{2,1,0:T(8,128)S(1)} %log_add_fusion, pred[12,12]{0,1:T(8,128)(4,1)S(1)} %fusion.120), kind=kOutput, calls=%fused_computation.87 | convolution fusion | flops 46513152 | bytes 8693136 | tf_op jit(solution)/shard_map/cphfg,cgphd->cfphd/dot_general | solution.py:87
  284.6 16.6 %copy.97 = bf16[1,12,196,12,64]{2,1,4,3,0:T(8,128)(2,1)} copy(bf16[1,12,196,12,64]{4,1,3,2,0:T(8,128)(2,1)} %convert_bitcast_fusion.1) | data formatting | bytes 7225344 | tf_op jit(solution)/shard_map/convert_element_type | solution.py:145
  329.0 12.2 reshape.719
  341.2 12.5 copy.103
  372.3 12.4 copy.102
  403.5 12.4 copy.101
  415.9 30.6 %while.26 = (s32[]{:T(128)}, bf16[3,4,196,12,64]{2,4,3,1,0:T(8,128)(2,1)}, f32[3,4,12,196]{3,2,1,0:T(8,128)S(1)}, bf16[3,4,196,12,64]{2,4,3,1,0:T(8,128)(2,1)}, ...) while((s32[]{:T(128)}, ...), condition=%wide.region_10.11_spmd, body=%wide.region_7.10_spmd.sunk | while | flops 486882816 | bytes 30529360 | solution.py:126
  485.8 134.5 %all-reduce.6.cloned.1.call-done = bf16[2352,768]{1,0:T(8,128)(2,1)} async-done(((bf16[2352,768]{1,0:T(8,128)(2,1)}), bf16[2352,768]{1,0:T(8,128)(2,1)}) %all-reduce.6.cloned.1.call-update) | async-done | bytes 3612688 | tf_op jit(solution)/shard_map/psum | solution.py:236
  629.7 14.3 all-reduce
  692.0 130.1 %all-reduce.8.cloned.1.call-done = bf16[2352,768]{1,0:T(8,128)(2,1)} async-done(((bf16[2352,768]{1,0:T(8,128)(2,1)}), bf16[2352,768]{1,0:T(8,128)(2,1)}) %all-reduce.8.cloned.1.call-update) | async-done | bytes 3612688 | tf_op jit(solution)/shard_map/psum | solution.py:269
  863.1 12.4 copy.108
  875.5 127.0 %while.27 = (s32[]{:T(128)}, bf16[3,4,196,12,64]{2,4,3,1,0:T(8,128)(2,1)}, bf16[3,4,196,12,64]{2,1,0,4,3:T(4,128)(2,1)}, bf16[3,4,196,12,64]{2,4,3,1,0:T(8,128)(...) while((s32[]{:T(128)}, ...), condition=%wide.region_28.29_spmd, body=%wide.region_26.28_spmd.sunk | while | flops 1205268224 | bytes 135174112 | solution.py:135
  1058.5 16.0 multiply_reduce_fusion.4
  1096.5 12.0 reshape.720
  1108.5 25.1 %multiply_reduce_fusion.2 = (f32[196,12,12]{2,1,0:T(8,128)S(1)}, f32[196,12,12,12]{2,3,1,0:T(8,128)}) fusion(f32[196,12,12,12]{2,3,1,0:T(8,128)} %get-tuple-element.256, f32[196,12,12]{2,1,0:T(8,128)S(1)} %copy-done.11, pred[12,12]{0,1:T(8,128)(4,1)S(1)} %copy-done.78, bf16[12,196,12,64]{3,2,1,0:T(8,128)(2,1)} %reshape.714, ...), kind=kOutput, calls=%fused_computation.68 | convolution fusion | flops 45017280 | bytes 10160784 | tf_op jit(solution)/shard_map/cfphd,cgphd->cphfg/dot_general | solution.py:94
  1133.6 18.9 %multiply_convert_fusion.5 = bf16[196,12,12,12]{2,3,1,0:T(8,128)(2,1)} fusion(f32[196,12,12,12]{2,3,1,0:T(8,128)} %get-tuple-element.263, f32[196,12,12,12]{2,3,1,0:T(8,128)} %get-tuple-element.256, f32[196,12,12]{2,1,0:T(8,128)S(1)} %get-tuple-element.262, f32[196,12,12]{2,1,0:T(8,128)S(1)} %copy-done.11, pred[12,12]{0,1:T(8,128)(4,1)S(1)} %copy-done.78), kind=kLoop, calls=%fused_computation.67 | loop fusion | flops 2032128 | bytes 3612816 | tf_op jit(solution)/shard_map/convert_element_type | solution.py:99
  1164.0 12.5 convert_reduce_fusion.1
  1176.5 16.9 %convert_reduce_fusion = (f32[12,64]{1,0:T(8,128)S(1)}, bf16[1,12,196,12,64]{4,1,3,2,0:T(8,128)(2,1)}) fusion(f32[196,12,12,12]{2,3,1,0:T(8,128)} %get-tuple-element.256, f32[196,12,12]{2,1,0:T(8,128)S(1)} %copy-done.11, pred[12,12]{0,1:T(8,128)(4,1)S(1)} %copy-done.78, bf16[12,196,12,64]{3,2,1,0:T(8,128)(2,1)} %reshape.720), kind=kOutput, calls=%fused_computation.63 | convolution fusion | flops 50125056 | bytes 8696208 | tf_op jit(solution)/shard_map/cphfg,cfphd->cgphd/dot_general | solution.py:95
  1199.8 16.7 %copy.120 = bf16[1,12,196,12,64]{2,1,4,3,0:T(8,128)(2,1)} copy(bf16[1,12,196,12,64]{4,1,3,2,0:T(8,128)(2,1)} %fusion.58) | data formatting | bytes 7225344 | tf_op jit(solution)/shard_map/convert_element_type | solution.py:108
  1235.6 16.7 %copy.118 = bf16[1,12,196,12,64]{2,1,4,3,0:T(8,128)(2,1)} copy(bf16[1,12,196,12,64]{4,1,3,2,0:T(8,128)(2,1)} %get-tuple-element.266) | data formatting | bytes 7225344 | tf_op jit(solution)/shard_map/convert_element_type | solution.py:107
  1271.4 16.6 %copy.122 = bf16[1,12,196,12,64]{2,1,4,3,0:T(8,128)(2,1)} copy(bf16[1,12,196,12,64]{4,1,3,2,0:T(8,128)(2,1)} %get-tuple-element.268) | data formatting | bytes 7225344 | tf_op jit(solution)/shard_map/convert_element_type | solution.py:109
  1299.1 14.3 multiply_reduce_fusion.5
  1409.3 16.9 %gather_fusion.2 = f32[72,48,768]{2,1,0:T(8,128)} fusion(f32[176,48,768]{2,1,0:T(8,128)} %bitcast.278, s32[1024]{0:T(1024)} %get-tuple-element.269), kind=kCustom, calls=%fused_computation.2 | custom fusion | bytes 21233952 | tf_op jit(solution)/shard_map/gather | solution.py:304
  1435.0 34.2 %all-reduce.10.cloned.1.call-done = (f32[220,768]{1,0:T(8,128)}, f32[768,400]{0,1:T(8,128)}) async-done(((f32[220,768]{1,0:T(8,128)}, f32[768,400]{0,1:T(8,128)}), (f32[220,768]{1,0:T(8,128)}, f32[768,400]{0,1:T(8,128)})) %all-reduce.10.cloned.1.call-update) | async-done | bytes 1904656 | tf_op jit(solution)/shard_map/psum | solution.py:293
  1471.4 82.6 %reduce-scatter.2.cloned.1.call-done = f32[432,768]{1,0:T(8,128)} async-done(((f32[3456,768]{1,0:T(8,128)}), f32[432,768]{1,0:T(8,128)}) %reduce-scatter.2.cloned.1.call-update) | async-done | bytes 1327120 | tf_op jit(solution)/shard_map/reduce_scatter | solution.py:305
  1558.3 39.8 %psum.53 = f32[]{:T(128)} all-reduce(f32[]{:T(128)} %multiply_reduce_fusion.14), channel_id=1, replica_groups=mesh['dp'=8,'mlp'=4] {'dp','mlp'}, use_global_device_ids=true, to_apply=%region_37.38 | all-reduce | flops 1 | bytes 8 | tf_op jit(solution)/shard_map/psum | solution.py:311
  (489 shorter events, 698.1 us)
Async XLA Ops:
  7.2 142.8 %all-gather.2.cloned.1.call-start = ((), (), s32[]{:S(2)}) async-start(), calls=%async_computation.1 | async-start | bytes 21897216 | tf_op jit(solution)/shard_map/all_gather | solution.py:208
  9.5 610.8 %all-reduce.6.cloned.1.call-start = ((), (), s32[]{:S(2)}) async-start(), calls=%async_computation.2 | async-start | bytes 7225344 | tf_op jit(solution)/shard_map/psum | solution.py:236
  15.8 165.6 %copy-start.71 = (f32[768]{0:T(1024)}, f32[768]{0:T(1024)S(1)}, u32[]{:S(2)}) copy-start(f32[768]{0:T(1024)S(1)} %get-tuple-element.171) | copy-start | bytes 9220
  15.8 305.0 %copy-start.73 = (f32[768]{0:T(1024)}, f32[768]{0:T(1024)S(1)}, u32[]{:S(2)}) copy-start(f32[768]{0:T(1024)S(1)} %get-tuple-element.166) | copy-start | bytes 9220
  35.6 232.3 %copy-start.77 = (pred[12,12]{0,1:T(8,128)(4,1)}, pred[12,12]{0,1:T(8,128)(4,1)S(1)}, u32[]{:S(2)}) copy-start(pred[12,12]{0,1:T(8,128)(4,1)S(1)} %fusion.120) | copy-start | bytes 436
  150.0 25.2 %slice-start.19 = ((s8[7225344]{0:T(1024)(128)(4,1)}), s8[3031040]{0:T(1024)(128)(4,1)S(1)}, s32[]{:S(2)}) async-start(s8[7225344]{0:T(1024)(128)(4,1)} %bitcast.272), calls=%async_computation.25 | async-start | bytes 6062080
  251.5 16.4 %copy-start.10 = (f32[196,12,12]{2,1,0:T(8,128)}, f32[196,12,12]{2,1,0:T(8,128)S(1)}, u32[]{:S(2)}) copy-start(f32[196,12,12]{2,1,0:T(8,128)S(1)} %log_add_fusion) | copy-start | bytes 338692
  446.5 16.6 %copy-start.45 = (bf16[16,48,768]{2,1,0:T(8,128)(2,1)S(1)}, bf16[16,48,768]{2,1,0:T(8,128)(2,1)}, u32[]{:S(2)}) copy-start(bf16[16,48,768]{2,1,0:T(8,128)(2,1)} %get-tuple-element.240) | copy-start | bytes 3538948
  446.5 16.6 %copy-start.96 = (f32[768]{0:T(1024)S(1)}, f32[768]{0:T(1024)}, u32[]{:S(2)}) copy-start(f32[768]{0:T(1024)} %get-tuple-element.162) | copy-start | bytes 9220
  470.9 365.8 %copy-start.57 = (f32[2352]{0:T(1024)}, f32[2352]{0:T(1024)S(1)}, u32[]{:S(2)}) copy-start(f32[2352]{0:T(1024)S(1)} %broadcast_multiply_fusion.3) | copy-start | bytes 28228
  471.9 364.8 %copy-start.67 = (f32[2352]{0:T(1024)}, f32[2352]{0:T(1024)S(1)}, u32[]{:S(2)}) copy-start(f32[2352]{0:T(1024)S(1)} %fusion.117) | copy-start | bytes 28228
  479.7 140.6 %copy-start.82 = (f32[768]{0:T(1024)S(1)}, f32[768]{0:T(1024)}, u32[]{:S(2)}) copy-start(f32[768]{0:T(1024)} %get-tuple-element.159) | copy-start | bytes 9220
  485.5 336.6 %all-reduce.8.cloned.1.call-start = ((), (), s32[]{:S(2)}) async-start(), calls=%async_computation.3 | async-start | bytes 7225344 | tf_op jit(solution)/shard_map/psum | solution.py:269
  671.5 165.2 %copy-start.79 = (f32[2352]{0:T(1024)}, f32[2352]{0:T(1024)S(1)}, u32[]{:S(2)}) copy-start(f32[2352]{0:T(1024)S(1)} %negate_multiply_fusion.3) | copy-start | bytes 28228
  688.3 780.9 %all-reduce.10.cloned.1.call-start = ((), (), s32[]{:S(2)}) async-start(), calls=%async_computation.5 | async-start | bytes 3833856 | tf_op jit(solution)/shard_map/psum | solution.py:293
  822.1 14.6 slice-start.3
  1002.5 17.1 %slice-start.17 = ((s8[4718592]{0:T(1024)(128)(4,1)}), s8[524288]{0:T(1024)(128)(4,1)S(1)}, s32[]{:S(2)}) async-start(s8[4718592]{0:T(1024)(128)(4,1)} %bitcast.269), calls=%async_computation.23 | async-start | bytes 1048576
  1041.9 16.5 %copy-start.56 = (f32[2352]{0:T(1024)S(1)}, f32[2352]{0:T(1024)}, u32[]{:S(2)}) copy-start(f32[2352]{0:T(1024)} %copy-done.55) | copy-start | bytes 28228
  1041.9 16.5 %copy-start.62 = (f32[2352]{0:T(1024)S(1)}, f32[2352]{0:T(1024)}, u32[]{:S(2)}) copy-start(f32[2352]{0:T(1024)} %copy-done.61) | copy-start | bytes 28228
  1041.9 16.5 %copy-start.74 = (f32[768]{0:T(1024)S(1)}, f32[768]{0:T(1024)}, u32[]{:S(2)}) copy-start(f32[768]{0:T(1024)} %copy-done.73) | copy-start | bytes 9220
  1050.1 24.4 %slice-start.9 = ((s8[7225344]{0:T(1024)(128)(4,1)}), s8[3031040]{0:T(1024)(128)(4,1)S(1)}, s32[]{:S(2)}) async-start(s8[7225344]{0:T(1024)(128)(4,1)} %bitcast.261), calls=%async_computation.15 | async-start | bytes 6062080
  1058.5 16.0 copy-start.66
  1058.5 16.0 slice-start.10
  1288.0 25.4 %slice-start.7 = ((s8[7225344]{0:T(1024)(128)(4,1)}), s8[3031040]{0:T(1024)(128)(4,1)S(1)}, s32[]{:S(2)}) async-start(s8[7225344]{0:T(1024)(128)(4,1)} %bitcast.259), calls=%async_computation.13 | async-start | bytes 6062080
  1299.1 14.3 copy-start.64
  1299.1 14.3 slice-start.8
  1380.4 15.5 slice-start.11
  1409.2 144.8 %reduce-scatter.2.cloned.1.call-start = ((), (), s32[]{:S(2)}) async-start(), calls=%async_computation.4 | async-start | bytes 11943936 | tf_op jit(solution)/shard_map/reduce_scatter | solution.py:305
  1409.3 16.9 %copy-start.75 = (f32[3456]{0:T(1024)S(1)}, f32[3456]{0:T(1024)}, u32[]{:S(2)}) copy-start(f32[3456]{0:T(1024)} %mul.643) | copy-start | bytes 41476
  1434.9 165.2 %copy-start.15 = (f32[768,400]{0,1:T(8,128)S(1)}, f32[768,400]{0,1:T(8,128)}, u32[]{:S(2)}) copy-start(f32[768,400]{0,1:T(8,128)} %param.33) | copy-start | bytes 3686404
  1435.0 169.8 %copy-start.31 = (f32[220,768]{1,0:T(8,128)S(1)}, f32[220,768]{1,0:T(8,128)}, u32[]{:S(2)}) copy-start(f32[220,768]{1,0:T(8,128)} %param.30) | copy-start | bytes 2027524
  1556.3 50.1 %copy-start.16 = (f32[432,768]{1,0:T(8,128)S(1)}, f32[432,768]{1,0:T(8,128)}, u32[]{:S(2)}) copy-start(f32[432,768]{1,0:T(8,128)} %reduce-scatter.2.cloned.1.call-done) | copy-start | bytes 3981316
  (107 other events, 694.9 us)
Sparse Core Ops, SparseCore 0:
  11.4 138.5 all-gather.1
  485.6 134.5 all-reduce.5
  688.4 133.6 all-reduce.7
  1409.3 59.8 all-reduce.9
  1472.6 81.4 reduce-scatter.1
where the time goes:
time: 1630 us; the launch traced here: 1620 us
  waiting for transfers between devices  496 us (30%)
  matrix products  427 us (26%)
  local copies, waits for them, and re-layouts  422 us (26%)
  other arithmetic  197 us (12%)
  blocking collectives  54 us (3%)
  between operations  20.1 us (1%)
    psum x1, waiting for transfers between devices, local(): lax.psum(rounded(matmul(active, tiles[10])).astype(jnp.bfloat16), 'mlp')  134 us
    psum x1, waiting for transfers between devices, local(): lax.psum(rounded(matmul_nt(grad_upper, tiles[9])).astype(jnp.bfloat16), '...  130 us
    all_gather x1, waiting for transfers between devices, local(): gathered = lax.all_gather(own_copy, ('dp', 'mlp'), axis=0, tiled=True)  114 us
    dot_general x11, matrix products, matmul_nt(): lax.dot_general(left, right, (((1,), (1,)), ((), ())), preferred_element_...  87.7 us
    reduce_scatter x1, waiting for transfers between devices, local(): lax.psum_scatter(chosen.reshape(slots * BR * lax.axis_size('dp'), width),...  82.6 us
    dot_general x11, matrix products, matmul_tn(): lax.dot_general(left, right, (((0,), (0,)), ((), ())), preferred_element_...  65 us
    dot_general x12, matrix products, matmul(): return jnp.dot(left, right, preferred_element_type=jnp.float32)  62.4 us
    reshape x6, local copies, waits for them, and re-layouts, attend_backward(): return tuple((tensor.reshape(-1, HEADS * HEAD_DIM) for tensor in results))  58.1 us
  transfers between devices with their start and end apart: 5, of which 5 were waited for; matrix products, arithmetic and copies ran while one was open for 4% of the time, Pallas kernels for 0%

commit v1 on v0

v1 whole, which is shorter than its diff:
```python
from functools import partial

import jax
import jax.numpy as jnp
from jax import lax
from jax.experimental import pallas as pl
from jax.experimental.pallas import tpu as pltpu
from jax.sharding import PartitionSpec as P

HEADS = 12
HEAD_DIM = 64
TROWS = 8
BR = 48
STEP = 10
GROUP = 16
PAIR = 2 * HEAD_DIM
GROUPS_AT_ONCE = 2
FRAMES_AT_ONCE = 2
VMEM_BYTES = 58 * 2**20

ln_eps = 1e-06
beta_one = 0.9
beta_two = 0.999
learn_rate = 0.05
table_rate = 0.4
decay_rate = 0.05
adam_eps = 1e-08
clip_max = 0.001
highest = lax.Precision.HIGHEST
f32 = jnp.float32
bf16 = jnp.bfloat16
gelu_a = 0.7978845608028654
gelu_b = 0.044715
masked = -1e30


def mm(left, right):
    return jnp.dot(left, right, preferred_element_type=f32)


def mm_nt(left, right):
    return lax.dot_general(left, right, (((1,), (1,)), ((), ())), preferred_element_type=f32)


def mm_tn(left, right):
    return lax.dot_general(left, right, (((0,), (0,)), ((), ())), preferred_element_type=f32)


def normed(values):
    centred = values - jnp.mean(values, axis=-1, keepdims=True)
    rstd = lax.rsqrt(jnp.mean(centred * centred, axis=-1, keepdims=True) + ln_eps)
    return centred * rstd, rstd


def norm_back(grad, xhat, rstd, gain):
    scaled = grad * gain
    return rstd * (
        scaled
        - jnp.mean(scaled, axis=-1, keepdims=True)
        - xhat * jnp.mean(scaled * xhat, axis=-1, keepdims=True)
    )


def fold(values):
    return jnp.sum(values.reshape(-1, 8, values.shape[-1]), axis=0)


def low_lanes():
    lane = lax.broadcasted_iota(jnp.int32, (1, PAIR), 1)
    low = jnp.where(lane < HEAD_DIM, 1.0, 0.0)
    return low.astype(bf16), (1.0 - low).astype(bf16)


def pick_half(stacked):
    rows = stacked.shape[0] // 2
    lane = lax.broadcasted_iota(jnp.int32, (rows, PAIR), 1)
    return jnp.where(lane < HEAD_DIM, stacked[:rows], stacked[rows:])


def fetch(slots_ref, source, target, sem, first, across):
    width = source.shape[2]
    per_tile = width // BR

    def one(i, carry):
        tile, row = i // per_tile, pl.multiple_of((i % per_tile) * BR, 16)
        place = pl.ds(row, BR)
        if across:
            into = target.at[place, pl.ds(pl.multiple_of(tile * width, width), width)]
        else:
            into = target.at[pl.ds(pl.multiple_of(tile * width, 16) + row, BR)]
        block = first(tile) * per_tile + i % per_tile
        pltpu.make_async_copy(source.at[slots_ref[block]], into, sem).start()
        return carry

    count = target.shape[0] * target.shape[1] // (width * width)
    lax.fori_loop(0, count * per_tile, one, 0)


def arrive(target, sem):
    pltpu.make_async_copy(target, target, sem).wait()


def attend(load, store, extra_q, extra_k):
    low, high = low_lanes()
    for pair in range(HEADS // 2):
        lanes = slice(pair * PAIR, (pair + 1) * PAIR)
        queries, keys, values = load(lanes)
        both = jnp.concatenate([queries * low, queries * high], axis=0)
        scores = mm_nt(
            jnp.concatenate([both, extra_q[...]], axis=1),
            jnp.concatenate([keys, extra_k[: keys.shape[0]]], axis=1),
        )
        top = jnp.max(scores, axis=-1, keepdims=True)
        weights = jnp.exp(scores - top).astype(bf16)
        summed = mm(weights, jnp.concatenate([values, jnp.ones_like(values)], axis=1))
        merged = pick_half(summed[:, :PAIR]) / pick_half(summed[:, PAIR:])
        store(lanes, merged.astype(bf16))


def attend_back(load, store, extra_q, extra_k):
    low, high = low_lanes()
    for pair in range(HEADS // 2):
        lanes = slice(pair * PAIR, (pair + 1) * PAIR)
        queries, keys, values, grads = load(lanes)
        rows = queries.shape[0]
        both_k = jnp.concatenate([keys * low, keys * high], axis=0)
        both_v = jnp.concatenate([values * low, values * high], axis=0)
        scores = mm_nt(
            jnp.concatenate([both_k, extra_k[...]], axis=1),
            jnp.concatenate([queries, extra_q[:rows]], axis=1),
        )
        back = mm_nt(both_v, grads)
        soft, inner = [], []
        for half in (slice(0, rows), slice(rows, 2 * rows)):
            part = scores[half]
            weights = jnp.exp(part - jnp.max(part, axis=0, keepdims=True))
            weights = weights * (1.0 / jnp.sum(weights, axis=0, keepdims=True))
            delta = back[half] - jnp.sum(weights * back[half], axis=0, keepdims=True)
            soft.append(weights.astype(bf16))
            inner.append((weights * delta).astype(bf16))
        soft = jnp.concatenate(soft, axis=0)
        inner = jnp.concatenate(inner, axis=0)
        store(
            lanes,
            (mm_tn(inner, both_k) * HEAD_DIM ** (-0.5)).astype(bf16),
            pick_half(mm(inner, queries)).astype(bf16),
            pick_half(mm(soft, grads)).astype(bf16),
        )


def project(hidden, rows, tiles):
    width = hidden.shape[1]
    joint = mm(hidden, tiles[...])
    queries = (joint[:, :width] + rows[2:3]).astype(bf16) * jnp.asarray(HEAD_DIM ** (-0.5), bf16)
    keys = joint[:, width : 2 * width].astype(bf16)
    values = (joint[:, 2 * width :] + rows[3:4]).astype(bf16)
    return queries, keys, values


def keep_norm(stream, rows, at, hid_ref, hat_ref, rstd_ref, here, cut):
    xhat, rstd = normed(stream)
    hat_ref[here] = xhat.astype(bf16).reshape(cut)
    rstd_ref[here] = jnp.broadcast_to(rstd, (rstd.shape[0], 128)).reshape(cut[:-1] + (128,))
    hidden = (xhat * rows[at : at + 1] + rows[at + 1 : at + 2]).astype(bf16)
    if hid_ref is not None:
        hid_ref[here] = hidden.reshape(cut)
    return xhat, hidden


def by_groups(block, total, work):
    step = pl.program_id(0)
    full, rest = total // block, total % block
    if rest == 0:
        work(block)
    else:
        pl.when(step < full)(lambda: work(block))
        pl.when(step == full)(lambda: work(rest))


def time_forward(
    total, slots, gathered, pixels, pos, trow, rows, extra_q, extra_k,
    x1_ref, hid_ref, hat_ref, rstd_ref, q_ref, k_ref, v_ref, o_ref,
    embed, joint, out, base, sems,
):
    frames, span, width = x1_ref.shape

    @pl.when(pl.program_id(0) == 0)
    def _():
        fetch(slots, gathered, embed, sems.at[0], lambda t: t, False)
        fetch(slots, gathered, joint, sems.at[1], lambda t: t + 1, True)
        fetch(slots, gathered, out, sems.at[2], lambda t: t + 4, False)
        arrive(embed, sems.at[0])
        arrive(joint, sems.at[1])
        arrive(out, sems.at[2])

    def work(count):
        cut = (frames, count * GROUP, width)
        flat = (frames * count * GROUP, width)
        here = slice(0, count * GROUP)
        every = (slice(None), here)
        offset = (pos[here][None] + trow[...][:, None]).reshape(flat)
        stream = mm(pixels[:, here].reshape(flat), embed[...]) + offset
        base[: flat[0]] = stream
        rows_now = rows[...]
        unused, hidden = keep_norm(stream, rows_now, 0, hid_ref, hat_ref, rstd_ref, every, cut)
        queries, keys, values = project(hidden, rows_now, joint)
        q_ref[:, here] = queries.reshape(cut)
        k_ref[:, here] = keys.reshape(cut)
        v_ref[:, here] = values.reshape(cut)
        for g in range(count):
            part = slice(g * GROUP, (g + 1) * GROUP)

            def load(lanes):
                return tuple(
                    ref[:, part, lanes].reshape(frames * GROUP, PAIR)
                    for ref in (q_ref, k_ref, v_ref)
                )

            def store(lanes, merged):
                o_ref[:, part, lanes] = merged.reshape(frames, GROUP, PAIR)

            attend(load, store, extra_q, extra_k)
        merged = o_ref[:, here].reshape(flat)
        stream = base[: flat[0]] + mm(merged, out[...]) + rows_now[4:5]
        x1_ref[:, here] = stream.reshape(cut)

    by_groups(span // GROUP, total, work)


def space_forward(
    slots, frame_weight, member, patches, gathered, x1, rows, low_rows, extra_q, extra_k,
    hid1_ref, hat1_ref, rstd1_ref, q_ref, k_ref, v_ref, o_ref,
    hid2_ref, hat2_ref, rstd2_ref, hat3_ref, rstd3_ref, gp_ref, act_ref, pool_ref,
    joint, out, ups, downs, acts, sems,
):
    step = pl.program_id(0)
    members = gp_ref.shape[0]
    cut = x1.shape
    span, count, width = cut
    flat = (span * count, width)
    every = (slice(None),)

    @pl.when(step == 0)
    def _():
        fetch(slots, gathered, joint, sems.at[0], lambda t: t + 5, True)
        fetch(slots, gathered, out, sems.at[1], lambda t: t + 8, False)
        fetch(slots, gathered, ups, sems.at[2], lambda t: 2 * t + 9, True)
        fetch(slots, gathered, downs, sems.at[3], lambda t: 2 * t + 10, False)
        pool_ref[...] = jnp.zeros_like(pool_ref)
        arrive(joint, sems.at[0])
        arrive(out, sems.at[1])

    rows_now = rows[...]
    unused, hidden = keep_norm(
        x1[...].reshape(flat), rows_now, 0, hid1_ref, hat1_ref, rstd1_ref, every, cut
    )
    queries, keys, values = project(hidden, rows_now, joint)
    q_ref[...] = queries.reshape(cut)
    k_ref[...] = keys.reshape(cut)
    v_ref[...] = values.reshape(cut)
    for f in range(span):

        def load(lanes):
            return q_ref[f, :, lanes], k_ref[f, :, lanes], v_ref[f, :, lanes]

        def store(lanes, merged):
            o_ref[f, :, lanes] = merged

        attend(load, store, extra_q, extra_k)
    merged = o_ref[...].reshape(flat)
    stream = x1[...].reshape(flat) + mm(merged, out[...]) + rows_now[4:5]
    low_now = low_rows[...]
    unused, hidden = keep_norm(stream, low_now, 0, hid2_ref, hat2_ref, rstd2_ref, every, cut)

    @pl.when(step == 0)
    def _():
        arrive(ups, sems.at[2])
        arrive(downs, sems.at[3])

    for j in range(members):
        lanes = slice(j * width, (j + 1) * width)
        upper = mm(hidden, ups[:, lanes])
        cubic = gelu_a * gelu_b * (upper * upper)
        gate = 0.5 + 0.5 * jnp.tanh(upper * (gelu_a + cubic))
        active = upper * gate
        slope = gate + active * (1.0 - gate) * (2.0 * gelu_a + 6.0 * cubic)
        gp_ref[j] = slope.astype(bf16).reshape(cut)
        acts[:, lanes] = active.astype(bf16)
        stream = stream + mm(acts[:, lanes], downs[lanes])
    own = pl.ds(pl.multiple_of(member[0] * width, 128), width)
    act_ref[...] = acts[:, own].reshape(cut)
    stream = stream + low_now[2:3]
    xhat, rstd = normed(stream)
    hat3_ref[...] = xhat.astype(bf16).reshape(cut)
    rstd3_ref[...] = jnp.broadcast_to(rstd, (flat[0], 128)).reshape(span, count, 128)
    final = xhat * low_now[3:4] + low_now[4:5]
    row = lax.broadcasted_iota(jnp.int32, (count, 1), 0)
    for f in range(span):
        part = jnp.where(row < patches, final[f * count : (f + 1) * count], 0.0)
        pool_ref[...] += fold(part) * frame_weight[step * span + f]


def mlp_backward(
    slots, frame_weight, member, patches, gathered, pool, head, valid, targets, total,
    hid2, hat2, rstd2, hat3, rstd3, gp, act, low_rows,
    dx2_ref, up_ref, down_ref, rows_ref, small_ref,
    ups, downs, dus, spread, up_sum, down_sum, row_sums, sems,
):
    step = pl.program_id(0)
    members = gp.shape[0]
    cut = hid2.shape
    span, count, width = cut
    flat = (span * count, width)

    @pl.when(step == 0)
    def _():
        fetch(slots, gathered, downs, sems.at[1], lambda t: 2 * t + 10, False)
        fetch(slots, gathered, ups, sems.at[0], lambda t: 2 * t + 9, True)
        pooled = jnp.sum(pool[...], axis=0, keepdims=True).astype(bf16)
        pooled8 = jnp.broadcast_to(pooled, (8, width))
        logits = mm(pooled8, head[...])
        valid_f = valid[...]
        target = targets[...]
        soft = jnp.maximum(logits, 0.0) + jnp.log(1.0 + jnp.exp(-jnp.abs(logits)))
        loss = jnp.sum(valid_f * (soft - target * logits), axis=1, keepdims=True)
        sig = 1.0 / (1.0 + jnp.exp(-logits))
        grad = (valid_f * (sig - target) / jnp.maximum(total[0], 1.0)).astype(bf16)
        spread[...] = mm_nt(grad, head[...])
        small_ref[...] = jnp.zeros_like(small_ref)
        small_ref[0:1, :] = pooled.astype(f32)
        small_ref[1:2, 0 : grad.shape[1]] = grad[0:1].astype(f32)
        small_ref[2:3, 0:128] = jnp.broadcast_to(loss[0:1], (1, 128))
        up_sum[...] = jnp.zeros_like(up_sum)
        down_sum[...] = jnp.zeros_like(down_sum)
        row_sums[...] = jnp.zeros_like(row_sums)
        arrive(downs, sems.at[1])

    low_now = low_rows[...]
    row = lax.broadcasted_iota(jnp.int32, (count, 1), 0)
    weight = jnp.concatenate(
        [jnp.where(row < patches, frame_weight[step * span + f], 0.0) for f in range(span)]
    )
    grad_final = spread[0:1] * weight
    xhat = hat3[...].reshape(flat).astype(f32)
    rstd = rstd3[...].reshape(flat[0], 128)[:, 0:1]
    row_sums[3] += fold(grad_final * xhat)
    row_sums[4] += fold(grad_final)
    grad_top = norm_back(grad_final, xhat, rstd, low_now[3:4])
    row_sums[2] += fold(grad_top)
    grad_b = grad_top.astype(bf16)

    for j in range(members):
        lanes = slice(j * width, (j + 1) * width)
        du = mm_nt(grad_b, downs[lanes]) * gp[j].reshape(flat).astype(f32)
        dus[:, lanes] = du.astype(bf16)

    @pl.when(step == 0)
    def _():
        arrive(ups, sems.at[0])

    grad_hidden = mm_nt(dus[...], ups[...])
    own = pl.ds(pl.multiple_of(member[0] * width, 128), width)
    up_sum[...] += mm_tn(hid2[...].reshape(flat), dus[:, own])
    down_sum[...] += mm_tn(act[...].reshape(flat), grad_b)
    xhat = hat2[...].reshape(flat).astype(f32)
    rstd = rstd2[...].reshape(flat[0], 128)[:, 0:1]
    row_sums[0] += fold(grad_hidden * xhat)
    row_sums[1] += fold(grad_hidden)
    dx2_ref[...] = (grad_top + norm_back(grad_hidden, xhat, rstd, low_now[0:1])).reshape(cut)

    @pl.when(step == pl.num_programs(0) - 1)
    def _():
        up_ref[...] = up_sum[...].astype(bf16)
        down_ref[...] = down_sum[...].astype(bf16)
        rows_ref[...] = jnp.zeros_like(rows_ref)
        for i in range(5):
            rows_ref[i : i + 1] = jnp.sum(row_sums[i], axis=0, keepdims=True)


def close_attention(
    grad_stream, grad_b, hidden, xhat, rstd, grads, merged, rows_now, picked, ones, joint,
    joint_sum, out_sum, row_sums,
):
    grad_hidden = mm_nt(grads, joint[...])
    hidden_t = mm_nt(picked, hidden).astype(bf16) + ones
    merged_t = mm_nt(picked, merged).astype(bf16) + ones
    joint_sum[...] += mm(hidden_t, grads)
    out_sum[...] += mm(merged_t, grad_b)
    xhat = xhat.astype(f32)
    row_sums[0] += fold(grad_hidden * xhat)
    row_sums[1] += fold(grad_hidden)
    return grad_stream + norm_back(grad_hidden, xhat, rstd[:, 0:1], rows_now[0:1])


def ones_row(picked):
    row = lax.broadcasted_iota(jnp.int32, (picked.shape[0], 1), 0)
    return jnp.where(row == picked.shape[0] - 16, 1.0, 0.0).astype(bf16)


def clear(*refs):
    for ref in refs:
        ref[...] = jnp.zeros_like(ref)


def finish_attention(tile_ref, at, rows_ref, joint_sum, out_sum, row_sums):
    share = tile_ref.shape[1]
    width = tile_ref.shape[2]
    rows_ref[...] = jnp.zeros_like(rows_ref)
    for i in range(3):
        tile_ref[at + i] = joint_sum[:share, i * width : (i + 1) * width].astype(bf16)
    tile_ref[at + 3] = out_sum[:share].astype(bf16)
    for i in range(2):
        rows_ref[i : i + 1] = jnp.sum(row_sums[i], axis=0, keepdims=True)
    rows_ref[2:3] = joint_sum[share : share + 1, :width]
    rows_ref[3:4] = joint_sum[share : share + 1, 2 * width :]
    rows_ref[4:5] = out_sum[share : share + 1]


def space_backward(
    slots, gathered, dx2, hid1, hat1, rstd1, q, k, v, o, rows, picked, extra_q, extra_k,
    dx1_ref, tile_ref, rows_ref, joint, out, joint_sum, out_sum, row_sums, grads, outer, sems,
):
    step = pl.program_id(0)
    cut = hid1.shape
    span, count, width = cut
    flat = (span * count, width)

    @pl.when(step == 0)
    def _():
        fetch(slots, gathered, out, sems.at[1], lambda t: t + 8, False)
        fetch(slots, gathered, joint, sems.at[0], lambda t: t + 5, True)
        clear(joint_sum, out_sum, row_sums)
        arrive(out, sems.at[1])
        arrive(joint, sems.at[0])

    grad_b = dx2[...].reshape(flat).astype(bf16)
    outer[...] = mm_nt(grad_b, out[...]).astype(bf16)
    for f in range(span):
        here = slice(f * count, (f + 1) * count)

        def load(lanes):
            return q[f, :, lanes], k[f, :, lanes], v[f, :, lanes], outer[here, lanes]

        def store(lanes, *parts):
            for i, part in enumerate(parts):
                grads[here, i * width + lanes.start : i * width + lanes.stop] = part

        attend_back(load, store, extra_q, extra_k)
    picked_now = picked[...]
    dx1_ref[...] = close_attention(
        dx2[...].reshape(flat), grad_b, hid1[...].reshape(flat), hat1[...].reshape(flat),
        rstd1[...].reshape(flat[0], 128), grads[...], o[...].reshape(flat), rows[...],
        picked_now, ones_row(picked_now), joint, joint_sum, out_sum, row_sums,
    ).reshape(cut)

    @pl.when(step == pl.num_programs(0) - 1)
    def _():
        finish_attention(tile_ref, 0, rows_ref, joint_sum, out_sum, row_sums)


def time_backward(
    total, slots, gathered, dx1, hid0, hat0, rstd0, q, k, v, o, pixels, rows, picked,
    extra_q, extra_k,
    tile_ref, rows_ref, pos_ref, frame_ref,
    joint, out, joint_sum, out_sum, embed_sum, row_sums, grads, outer, sems,
):
    step = pl.program_id(0)
    frames, span, width = hid0.shape

    @pl.when(step == 0)
    def _():
        fetch(slots, gathered, out, sems.at[1], lambda t: t + 4, False)
        fetch(slots, gathered, joint, sems.at[0], lambda t: t + 1, True)
        clear(joint_sum, out_sum, embed_sum, row_sums, frame_ref)
        arrive(out, sems.at[1])
        arrive(joint, sems.at[0])

    def work(groups):
        cut = (frames, groups * GROUP, width)
        flat = (frames * groups * GROUP, width)
        small = (frames, GROUP, PAIR)
        here = slice(0, groups * GROUP)
        grad_b = dx1[:, here].reshape(flat).astype(bf16)
        outer[:, here] = mm_nt(grad_b, out[...]).astype(bf16).reshape(cut)
        for g in range(groups):
            part = slice(g * GROUP, (g + 1) * GROUP)

            def load(lanes):
                return tuple(
                    ref[:, part, lanes].reshape(frames * GROUP, PAIR)
                    for ref in (q, k, v, outer)
                )

            def store(lanes, *parts):
                for i, value in enumerate(parts):
                    span_now = slice(i * width + lanes.start, i * width + lanes.stop)
                    grads[:, part, span_now] = value.reshape(small)

            attend_back(load, store, extra_q, extra_k)
        picked_now = picked[...]
        grad = close_attention(
            dx1[:, here].reshape(flat), grad_b, hid0[:, here].reshape(flat),
            hat0[:, here].reshape(flat), rstd0[:, here].reshape(flat[0], 128),
            grads[:, here].reshape(flat[0], 3 * width), o[:, here].reshape(flat), rows[...],
            picked_now, ones_row(picked_now), joint, joint_sum, out_sum, row_sums,
        )
        pix_t = mm_nt(picked_now, pixels[:, here].reshape(flat)).astype(bf16)
        embed_sum[...] += mm(pix_t, grad.astype(bf16))
        cube = grad.reshape(cut)
        pos_ref[here] = jnp.sum(cube, axis=0)
        frame_ref[...] += jnp.sum(cube, axis=1)

    by_groups(span // GROUP, total, work)

    @pl.when(step == pl.num_programs(0) - 1)
    def _():
        finish_attention(tile_ref, 1, rows_ref, joint_sum, out_sum, row_sums)
        tile_ref[0] = embed_sum[: tile_ref.shape[1]].astype(bf16)


def pack(dests, core, *refs):
    sources, table_ref, keep_ref, send_ref, sems = refs[:-4], refs[-4], refs[-3], refs[-2], refs[-1]
    slots = (keep_ref.shape[1] - table_ref.shape[1]) // BR

    def route(source, chunk, place, sem):
        mine = chunk % 2 == core[0]

        @pl.when(mine)
        def _():
            pltpu.make_async_copy(source, keep_ref.at[chunk // 2, place], sem).start()

        @pl.when(jnp.logical_not(mine))
        def _():
            pltpu.make_async_copy(source, send_ref.at[chunk // 2, place], sem).start()

    first = 0
    for n, source in enumerate(sources):

        def one(i, carry, source=source, first=first, n=n):
            dest = dests[first + i]
            row = pl.multiple_of((dest % slots) * BR, 16)
            route(source.at[i], dest // slots, pl.ds(row, BR), sems.at[n])
            return carry

        lax.fori_loop(0, source.shape[0], one, 0)
        first += source.shape[0]

    def one_table(i, carry):
        place = pl.ds(slots * BR, table_ref.shape[1])
        route(table_ref.at[i], i, place, sems.at[len(sources)])
        return carry

    lax.fori_loop(0, table_ref.shape[0], one_table, 0)
    for n, source in enumerate(sources + (table_ref,)):
        pltpu.make_async_copy(source, source, sems.at[n]).wait()


def swap(value, axis, hop):
    size = lax.axis_size(axis)
    return lax.ppermute(value, axis, [(i, i ^ hop) for i in range(size)])


def halve(kept, sent, axis):
    size = lax.axis_size(axis)
    place = lax.axis_index(axis)
    bits = size.bit_length() - 1
    rows, width = kept.shape[1:]
    middle = (width // 256) * 128
    met = swap(sent, axis, 1)
    cut = (2,) * (bits - 1) + (rows, width)
    kept, met = kept.reshape(cut), met.reshape(cut)
    ascending = list(range(1, bits))
    parts = [
        [kept[..., :middle], met[..., :middle], ascending],
        [kept[..., middle:], met[..., middle:], ascending[::-1]],
    ]
    parts = [(left.astype(f32) + right.astype(f32), order) for left, right, order in parts]
    for stage in range(bits - 1):
        outgoing, staying = [], []
        for value, order in parts:
            alive = sorted(order[stage:], reverse=True)
            at = alive.index(order[stage])
            bit = (place >> order[stage]) & 1
            outgoing.append(lax.dynamic_index_in_dim(value, 1 - bit, at, False).astype(bf16))
            staying.append(lax.dynamic_index_in_dim(value, bit, at, False))
        arrived = [
            swap(value, axis, 1 << order[stage]) for value, (unused, order) in zip(outgoing, parts)
        ]
        parts = [
            (stay + come.astype(f32), order)
            for stay, come, (unused, order) in zip(staying, arrived, parts)
        ]
    return jnp.concatenate([parts[0][0], parts[1][0]], axis=-1)


def block_ranks(owners):
    total_blocks = owners.shape[0]
    same_owner = owners[:, None] == owners[None, :]
    earlier = jnp.arange(total_blocks)[None, :] < jnp.arange(total_blocks)[:, None]
    return jnp.sum((same_owner & earlier).astype(jnp.int32), axis=1)


def adamw(weight, gradient, moment_one, moment_two, weight_decay, rate):
    first_new = beta_one * moment_one + (1.0 - beta_one) * gradient
    second_new = beta_two * moment_two + (1.0 - beta_two) * gradient * gradient
    mean_hat = first_new / (1.0 - beta_one**STEP)
    var_hat = second_new / (1.0 - beta_two**STEP)
    updated = weight - rate * (mean_hat / (jnp.sqrt(var_hat) + adam_eps) + weight_decay * weight)
    return (updated, first_new, second_new)


def local(
    pixels,
    lengths,
    frame_mask,
    time_index,
    label_valid,
    targets,
    owners,
    slot_weight,
    slot_moment1,
    slot_moment2,
    tables,
    table_moment1,
    table_moment2,
    head_weight,
    head_moment1,
    head_moment2,
):
    dp_count = lax.axis_size("dp")
    mlp_count = lax.axis_size("mlp")
    member = lax.axis_index("mlp").astype(jnp.int32)
    width = slot_weight.shape[1]
    per_tile = width // BR
    slots = slot_weight.shape[0] // BR
    shared_blocks = 9 * per_tile
    frames, patches = pixels.shape[1], pixels.shape[2]
    padded = -(-patches // GROUP) * GROUP
    groups = padded // GROUP
    classes = head_weight.shape[1]
    class_pad = -(-classes // 128) * 128
    params = pltpu.CompilerParams(vmem_limit_bytes=VMEM_BYTES)
    any_spec = pl.BlockSpec(memory_space=pl.ANY)

    gathered = lax.all_gather(slot_weight.astype(bf16), ("dp", "mlp"), axis=0, tiled=True)
    gathered = gathered.reshape(-1, BR, width)
    slot_index = (owners * slots + block_ranks(owners)).astype(jnp.int32)

    pix = jnp.pad(pixels[0], ((0, 0), (0, padded - patches), (0, 0)))
    slot_pos = jnp.arange(frames)
    frame_live = slot_pos < lengths[0]
    key_ok = frame_live & (frame_mask[0] == 1)
    allowed = key_ok[None, :] | (slot_pos[:, None] == slot_pos[None, :])
    extra_lane = jnp.arange(HEAD_DIM)
    flat_id = jnp.arange(frames * GROUP)
    frame_id, patch_id = flat_id // GROUP, flat_id % GROUP
    lane_frame = jnp.clip(extra_lane - GROUP, 0, frames - 1)
    in_patch = (extra_lane < GROUP)[None, :]
    in_frame = ((extra_lane >= GROUP) & (extra_lane < GROUP + frames))[None, :]
    same_patch = patch_id[:, None] == extra_lane[None, :]
    same_frame = frame_id[:, None] == lane_frame[None, :]
    time_q = (in_patch & same_patch) | (in_frame & same_frame)
    time_k = (in_patch & ~same_patch) | (in_frame & ~allowed.T[frame_id][:, lane_frame])
    is_pad = (jnp.arange(padded) >= patches)[:, None]
    space_q = jnp.broadcast_to(extra_lane[None, :] == 0, (padded, HEAD_DIM))
    space_k = is_pad & (extra_lane[None, :] == 0)

    def widen(flags, value):
        block = jnp.where(flags, value, 0.0).astype(bf16)
        block = jnp.pad(block, ((0, 0), (0, PAIR - HEAD_DIM)))
        return jnp.concatenate([block, block])

    time_q, time_k = widen(time_q, 1.0), widen(time_k, masked)
    space_q, space_k = widen(space_q, 1.0), widen(space_k, masked)
    time_hot = (time_index[0][:, None] == jnp.arange(TROWS)[None, :]).astype(f32)
    trow = jnp.einsum("ft,td->fd", time_hot, tables[16 + patches :], precision=highest)
    pos = jnp.pad(tables[16 : 16 + patches] + tables[0], ((0, padded - patches), (0, 0)))
    frame_weight = jnp.where(
        frame_live, 1.0 / (lengths[0] * patches).astype(f32), 0.0
    ).astype(f32)
    valid_f = label_valid.astype(f32)
    label_total = lax.psum(jnp.sum(valid_f), "dp")
    share = width // mlp_count
    pick_row = jnp.arange(share)
    pick_feature = (pick_row // BR) * (BR * mlp_count) + member * BR + pick_row % BR
    picked = (pick_feature[:, None] == jnp.arange(width)[None, :]).astype(bf16)
    picked = jnp.pad(picked, ((0, 16), (0, 0)))
    member_s = member[None]
    time_rows = jnp.pad(tables[1:6], ((0, 3), (0, 0)))
    space_rows = jnp.pad(tables[6:11], ((0, 3), (0, 0)))
    low_rows = jnp.pad(tables[11:16], ((0, 3), (0, 0)))

    cube32 = jax.ShapeDtypeStruct((frames, padded, width), f32)
    cube16 = jax.ShapeDtypeStruct((frames, padded, width), bf16)
    thin32 = jax.ShapeDtypeStruct((frames, padded, 128), f32)
    row32 = jax.ShapeDtypeStruct((8, width), f32)
    group_rows = GROUPS_AT_ONCE * GROUP
    frame_rows = FRAMES_AT_ONCE * padded
    group_spec = pl.BlockSpec((frames, group_rows, width), lambda g, *_: (0, g, 0))
    group_thin = pl.BlockSpec((frames, group_rows, 128), lambda g, *_: (0, g, 0))
    patch_spec = pl.BlockSpec((group_rows, width), lambda g, *_: (g, 0))
    frame_spec = pl.BlockSpec((FRAMES_AT_ONCE, padded, width), lambda f, *_: (f, 0, 0))
    frame_thin = pl.BlockSpec((FRAMES_AT_ONCE, padded, 128), lambda f, *_: (f, 0, 0))
    gp_spec = pl.BlockSpec(
        (mlp_count, FRAMES_AT_ONCE, padded, width), lambda f, *_: (0, f, 0, 0)
    )
    time_grid = (-(-groups // GROUPS_AT_ONCE),)
    space_grid = (frames // FRAMES_AT_ONCE,)

    def whole(*shape):
        return pl.BlockSpec(shape, lambda i, *_: (0,) * len(shape))

    rows_spec = whole(8, width)
    time_extra = whole(2 * frames * GROUP, PAIR)
    space_extra = whole(2 * padded, PAIR)
    pick_spec = whole(share + 16, width)

    def call(kernel, name, scalars, grid, ins, in_specs, outs, out_specs, scratch):
        return pl.pallas_call(
            kernel,
            grid_spec=pltpu.PrefetchScalarGridSpec(
                num_scalar_prefetch=len(scalars),
                grid=grid,
                in_specs=[any_spec] + in_specs,
                out_specs=out_specs,
                scratch_shapes=scratch,
            ),
            out_shape=outs,
            compiler_params=params,
            name=name,
        )(*scalars, gathered, *ins)

    def tile_bufs(*shapes):
        return [pltpu.VMEM((rows * width, cols * width), bf16) for rows, cols in shapes]

    x1, hid0, hat0, rstd0, q_t, k_t, v_t, o_t = call(
        partial(time_forward, groups),
        "time_forward",
        [slot_index],
        time_grid,
        [pix, pos, trow, time_rows, time_q, time_k],
        [group_spec, patch_spec, whole(frames, width), rows_spec, time_extra, time_extra],
        [cube32, cube16, cube16, thin32] + [cube16] * 4,
        [group_spec] * 3 + [group_thin] + [group_spec] * 4,
        tile_bufs((1, 1), (1, 3), (1, 1))
        + [pltpu.VMEM((frames * group_rows, width), f32), pltpu.SemaphoreType.DMA((3,))],
    )
    (hid1, hat1, rstd1, q_s, k_s, v_s, o_s, hid2, hat2, rstd2, hat3, rstd3, gp, act, pool) = call(
        lambda s, fw, m, *refs: space_forward(s, fw, m, patches, *refs),
        "space_forward",
        [slot_index, frame_weight, member_s],
        space_grid,
        [x1, space_rows, low_rows, space_q, space_k],
        [frame_spec, rows_spec, rows_spec, space_extra, space_extra],
        [cube16, cube16, thin32]
        + [cube16] * 4
        + [cube16, cube16, thin32, cube16, thin32]
        + [jax.ShapeDtypeStruct((mlp_count, frames, padded, width), bf16), cube16, row32],
        [frame_spec, frame_spec, frame_thin]
        + [frame_spec] * 4
        + [frame_spec, frame_spec, frame_thin, frame_spec, frame_thin]
        + [gp_spec, frame_spec, rows_spec],
        tile_bufs((1, 3), (1, 1), (1, mlp_count), (mlp_count, 1))
        + [pltpu.VMEM((frame_rows, mlp_count * width), bf16), pltpu.SemaphoreType.DMA((4,))],
    )

    head_b = jnp.pad(head_weight.astype(bf16), ((0, 0), (0, class_pad - classes)))
    valid_p = jnp.pad(valid_f, ((0, 0), (0, class_pad - classes)))
    targets_p = jnp.pad(targets, ((0, 0), (0, class_pad - classes)))
    square16 = jax.ShapeDtypeStruct((width, width), bf16)
    dx2, grad_up, grad_down, rows_low, small = call(
        lambda s, fw, m, *refs: mlp_backward(s, fw, m, patches, *refs),
        "mlp_backward",
        [slot_index, frame_weight, member_s],
        space_grid,
        [
            pool, head_b, valid_p, targets_p, label_total[None],
            hid2, hat2, rstd2, hat3, rstd3, gp, act, low_rows,
        ],
        [
            rows_spec, whole(width, class_pad), whole(1, class_pad), whole(1, class_pad),
            pl.BlockSpec(memory_space=pltpu.SMEM),
            frame_spec, frame_spec, frame_thin, frame_spec, frame_thin, gp_spec, frame_spec,
            rows_spec,
        ],
        [cube32, square16, square16, row32, row32],
        [frame_spec, whole(width, width), whole(width, width), rows_spec, rows_spec],
        tile_bufs((1, mlp_count), (mlp_count, 1))
        + [
            pltpu.VMEM((frame_rows, mlp_count * width), bf16),
            pltpu.VMEM((8, width), f32),
            pltpu.VMEM((width, width), f32),
            pltpu.VMEM((width, width), f32),
            pltpu.VMEM((5, 8, width), f32),
            pltpu.SemaphoreType.DMA((2,)),
        ],
    )

    sums = [
        pltpu.VMEM((share + 16, 3 * width), f32),
        pltpu.VMEM((share + 16, width), f32),
    ]
    dx1, tiles_space, rows_space = call(
        space_backward,
        "space_backward",
        [slot_index],
        space_grid,
        [dx2, hid1, hat1, rstd1, q_s, k_s, v_s, o_s, space_rows, picked, space_q, space_k],
        [frame_spec] * 3
        + [frame_thin]
        + [frame_spec] * 4
        + [rows_spec, pick_spec, space_extra, space_extra],
        [cube32, jax.ShapeDtypeStruct((4, share, width), bf16), row32],
        [frame_spec, whole(4, share, width), rows_spec],
        tile_bufs((1, 3), (1, 1))
        + sums
        + [
            pltpu.VMEM((2, 8, width), f32),
            pltpu.VMEM((frame_rows, 3 * width), bf16),
            pltpu.VMEM((frame_rows, width), bf16),
            pltpu.SemaphoreType.DMA((2,)),
        ],
    )
    tiles_time, rows_time, grad_pos, grad_frames = call(
        partial(time_backward, groups),
        "time_backward",
        [slot_index],
        time_grid,
        [dx1, hid0, hat0, rstd0, q_t, k_t, v_t, o_t, pix, time_rows, picked, time_q, time_k],
        [group_spec] * 3
        + [group_thin]
        + [group_spec] * 5
        + [rows_spec, pick_spec, time_extra, time_extra],
        [
            jax.ShapeDtypeStruct((5, share, width), bf16),
            row32,
            jax.ShapeDtypeStruct((padded, width), f32),
            jax.ShapeDtypeStruct((frames, width), f32),
        ],
        [whole(5, share, width), rows_spec, patch_spec, whole(frames, width)],
        tile_bufs((1, 3), (1, 1))
        + sums
        + [
            pltpu.VMEM((share + 16, width), f32),
            pltpu.VMEM((2, 8, width), f32),
            pltpu.VMEM((frames, group_rows, 3 * width), bf16),
            pltpu.VMEM((frames, group_rows, width), bf16),
            pltpu.SemaphoreType.DMA((2,)),
        ],
    )

    grad_time = jnp.einsum("ft,fd->td", time_hot, grad_frames, precision=highest)
    table_rows = tables.shape[0]
    table_part = jnp.concatenate(
        [
            jnp.sum(grad_frames, axis=0, keepdims=True),
            rows_time[:5],
            rows_space[:5],
            rows_low[:5],
            grad_pos[:patches],
            grad_time,
        ]
    )
    rows_each = -(-table_rows // (dp_count * mlp_count))
    table_part = jnp.pad(
        table_part, ((0, rows_each * dp_count * mlp_count - table_rows), (0, 0))
    ).reshape(dp_count, mlp_count, rows_each, width)
    table_part = lax.dynamic_index_in_dim(table_part, member, 1, False).astype(bf16)
    table_part = jnp.pad(table_part, ((0, 0), (0, 16 - rows_each), (0, 0)))

    sources = [
        part.reshape(-1, BR, width) for part in (tiles_time, tiles_space, grad_up, grad_down)
    ]
    shared_here = shared_blocks // mlp_count
    here_ids = jnp.arange(shared_here + 2 * per_tile)
    block_of = jnp.where(
        here_ids < shared_here,
        here_ids * mlp_count + member,
        here_ids - shared_here + shared_blocks + member * 2 * per_tile,
    )
    here_slots = slot_index[block_of]
    dests = (here_slots // (slots * mlp_count)) * slots + here_slots % slots
    place = lax.axis_index("dp").astype(jnp.int32)
    chunk = jax.ShapeDtypeStruct((dp_count // 2, slots * BR + 16, width), bf16)
    kept, sent = pl.pallas_call(
        pack,
        grid_spec=pltpu.PrefetchScalarGridSpec(
            num_scalar_prefetch=2,
            grid=(1,),
            in_specs=[pl.BlockSpec(memory_space=pltpu.VMEM)] * 5,
            out_specs=[any_spec] * 2,
            scratch_shapes=[pltpu.SemaphoreType.DMA((5,))],
        ),
        out_shape=[chunk, chunk],
        compiler_params=params,
        name="pack",
    )(dests, (place % 2)[None], *sources, table_part)
    summed = halve(kept, sent, "dp")
    my_slots = (place * mlp_count + member) * slots + jnp.arange(slots)
    filled = jnp.any(slot_index[:, None] == my_slots[None, :], axis=0)
    filled = jnp.repeat(filled, BR)[:, None]
    own_grad = jnp.where(filled, summed[: slots * BR], 0.0)
    squares_own = jnp.sum(own_grad * own_grad)
    block = jnp.concatenate(
        [
            jnp.pad(summed[slots * BR : slots * BR + rows_each], ((0, 7 - rows_each), (0, 0))),
            jnp.broadcast_to(squares_own, (1, width)),
            small,
        ]
    )
    blocks = lax.all_gather(block, "dp", axis=0)
    grad_head = jnp.einsum("cd,ck->dk", blocks[:, 8], blocks[:, 9, :classes], precision=highest)
    loss_sum = jnp.sum(blocks[:, 10, 0])
    blocks = lax.all_gather(blocks[:, :8], "mlp", axis=1)
    grad_tables = blocks[:, :, :rows_each].reshape(-1, width)[:table_rows]
    grad_norm = jnp.sqrt(
        jnp.sum(blocks[:, :, 7, 0])
        + jnp.sum(grad_tables * grad_tables)
        + jnp.sum(grad_head * grad_head)
    )
    factor = jnp.minimum(1.0, clip_max / (grad_norm + 1e-06))
    new_slots = adamw(
        slot_weight, own_grad * factor, slot_moment1, slot_moment2, decay_rate, learn_rate
    )
    new_tabs = adamw(tables, grad_tables * factor, table_moment1, table_moment2, 0.0, table_rate)
    new_heads = adamw(
        head_weight, grad_head * factor, head_moment1, head_moment2, decay_rate, learn_rate
    )
    return (
        loss_sum,
        label_total,
        grad_norm,
        new_slots[0],
        new_slots[1],
        new_slots[2],
        new_tabs[0],
        new_tabs[1],
        new_tabs[2],
        new_heads[0],
        new_heads[1],
        new_heads[2],
    )


def solution(mesh):
    return jax.shard_map(
        local,
        mesh=mesh,
        in_specs=(
            P("dp", None, None, None),
            P("dp"),
            P("dp", None),
            P("dp", None),
            P("dp", None),
            P("dp", None),
            P(),
            P(("dp", "mlp"), None),
            P(("dp", "mlp"), None),
            P(("dp", "mlp"), None),
            P(),
            P(),
            P(),
            P(),
            P(),
            P(),
        ),
        out_specs=(
            P(),
            P(),
            P(),
            P(("dp", "mlp"), None),
            P(("dp", "mlp"), None),
            P(("dp", "mlp"), None),
            P(),
            P(),
            P(),
            P(),
            P(),
            P(),
        ),
        check_vma=False,
    )
```

time: 1630 us -> 566 us (0.35)
  matrix products: 427 us -> 3.78 us
  local copies, waits for them, and re-layouts: 422 us -> 23.4 us
  waiting for transfers between devices: 496 us -> 132 us
  Pallas kernels: 0 us -> 305 us
  other arithmetic: 197 us -> 28.2 us
    dot_general x63 -> x3, matrix products: 427 us -> 3.78 us  [the longest x1 1.88 us: local(): jnp.einsum('cd,ck->dk', blocks[:, 8], blocks[:, 9, :classes], precision=h...]
    pallas_call x0 -> x6, Pallas kernels: none -> 305 us  [the longest x5 300 us: call(): pl.pallas_call(kernel, grid_spec=pltpu.PrefetchScalarGridSpec(num_scalar_...]
    psum x3 -> x0, waiting for transfers between devices: 299 us -> none  [the longest x1 134 us: local(): lax.psum(rounded(matmul(active, tiles[10])).astype(jnp.bfloat16), 'mlp')]
    reduce_sum x26 -> x4, other arithmetic: 109 us -> 3.1 us  [the longest x1 1.03 us: local(): squares_own = jnp.sum(own_grad * own_grad)]
    another operation x16 -> x0, local copies, waits for them, and re-layouts: 95.7 us -> none  [the longest x4 47.7 us: to_heads(): tensor.reshape(-1, FRAME_BLOCK, patches, HEADS, HEAD_DIM)]
    convert_element_type x8 -> x6, local copies, waits for them, and re-layouts: 94 us -> 2.22 us  [the longest x4 1.93 us: halve(): lax.dynamic_index_in_dim(value, 1 - bit, at, False).astype(bf16)]
    reduce_scatter x1 -> x0, waiting for transfers between devices: 82.6 us -> none  [local(): lax.psum_scatter(chosen.reshape(slots * BR * lax.axis_size('dp'), width),...]
    reshape x16 -> x2, local copies, waits for them, and re-layouts: 72.9 us -> 0.21 us  [the longest x1 0.12 us: local(): table_part = jnp.pad(table_part, ((0, rows_each * dp_count * mlp_count -...]
  transfers between devices with their start and end apart: 5 -> 6, of which waited for: 5 -> 5; matrix products, arithmetic and copies ran while one was open for 4% -> 4% of each run, Pallas kernels for 0% -> 0%
where the time goes in v1:
time: 566 us; the launch traced here: 558 us
  Pallas kernels  305 us (54%)
  waiting for transfers between devices  132 us (23%)
  blocking collectives  42.4 us (7%)
  other arithmetic  28.2 us (5%)
  local copies, waits for them, and re-layouts  23.4 us (4%)
  between operations  18.7 us (3%)
    pallas_call x5, Pallas kernels, call(): pl.pallas_call(kernel, grid_spec=pltpu.PrefetchScalarGridSpec(num_scalar_...  300 us
    all_gather x1, waiting for transfers between devices, local(): lax.all_gather(slot_weight.astype(bf16), ('dp', 'mlp'), axis=0, tiled=True)  105 us
    ppermute x5, waiting for transfers between devices, swap(): return lax.ppermute(value, axis, [(i, i ^ hop) for i in range(size)])  26.9 us
    all_gather x1, blocking collectives, local(): blocks = lax.all_gather(blocks[:, :8], 'mlp', axis=1)  18 us
    psum x1, blocking collectives, local(): label_total = lax.psum(jnp.sum(valid_f), 'dp')  15.7 us
  transfers between devices with their start and end apart: 6, of which 5 were waited for; matrix products, arithmetic and copies ran while one was open for 4% of the time, Pallas kernels for 0%

profile of v1, /device:TPU:0, one launch (start us, length us, event | category | flops | bytes accessed | tf_op | source)
XLA Modules:
  0.0 558.0 jit_solution(16122610623820505886)
XLA Ops:
  7.2 2.2 convert_element_type.110
  10.1 15.7 %psum.7 = f32[]{:T(128)} all-reduce(f32[]{:T(128)} %convert_reduce_fusion.1), channel_id=1, replica_groups=mesh['dp'=8,'mlp'=4] {'dp'}, use_global_device_ids=true, to_apply=%region_2.3 | all-reduce | flops 1 | bytes 8 | tf_op jit(solution)/shard_map/psum | solution.py:682
  28.5 4.4 pad.59.pixels
  38.7 1.3 gather_fusion
  44.9 105.1 %all-gather.4.cloned.1.call-done = bf16[13824,768]{1,0:T(8,128)(2,1)} async-done(((bf16[432,768]{1,0:T(8,128)(2,1)}), bf16[13824,768]{1,0:T(8,128)(2,1)}) %all-gather.4.cloned.1.call-update) | async-done | bytes 21233680 | tf_op jit(solution)/shard_map/all_gather | solution.py:645
  150.0 36.2 %time_forward.1 = (f32[12,208,768]{2,1,0:T(8,128)}, bf16[12,208,768]{2,1,0:T(8,128)(2,1)}, bf16[12,208,768]{2,1,0:T(8,128)(2,1)}, f32[12,208,128]{2,1,0:T(8,128)...) custom-call(s32[272]{0:T(512)} %copy-done, ...), custom_call_target="tpu_custom_call" | custom-call | tf_op jit(solution)/shard_map/time_forward/pallas_call | solution.py:719
  186.2 69.1 %space_forward.1 = (bf16[12,208,768]{2,1,0:T(8,128)(2,1)}, bf16[12,208,768]{2,1,0:T(8,128)(2,1)}, f32[12,208,128]{2,1,0:T(8,128)}, bf16[12,208,768]{2,1,0:T(8,12...) custom-call(s32[272]{0:T(512)} %copy-done, ...), custom_call_target="tpu_custom_call" | custom-call | tf_op jit(solution)/shard_map/space_forward/pallas_call | solution.py:719
  255.3 49.2 %mlp_backward.1 = (f32[12,208,768]{2,1,0:T(8,128)}, bf16[768,768]{1,0:T(8,128)(2,1)}, bf16[768,768]{1,0:T(8,128)(2,1)}, f32[8,768]{1,0:T(8,128)}, f32[8,768]{1,0:T(8,128)}) custom-call(s32[272]{0:T(512)} %copy-done, f32[12]{0:T(128)} %compare_select_fusion.3.fw, s32[1]{0:T(128)} %bitcast.4.m, bf16[288,48,768]{2,1,0:T(8,128)(2,1)} %bitcast.64, ...), custom_call_target="tpu_custom_call" | custom-call | tf_op jit(solution)/shard_map/mlp_backward/pallas_call | solution.py:719
  304.5 69.6 %space_backward.1 = (f32[12,208,768]{2,1,0:T(8,128)}, bf16[4,192,768]{2,1,0:T(8,128)(2,1)}, f32[8,768]{1,0:T(8,128)}) custom-call(s32[272]{0:T(512)} %copy-done, bf16[288,48,768]{2,1,0:T(8,128)(2,1)} %bitcast.65, f32[12,208,768]{2,1,0:T(8,128)} %get-tuple-element.58.dx2, bf16[12,208,768]{2,1,0:T(8,128)(2,1)} %get-tuple-element.59.hid1, ...), custom_call_target="tpu_custom_call" | custom-call | tf_op jit(solution)/shard_map/space_backward/pallas_call | solution.py:719
  374.2 75.5 %time_backward.1 = (bf16[5,192,768]{2,1,0:T(8,128)(2,1)}, f32[8,768]{1,0:T(8,128)}, f32[208,768]{1,0:T(8,128)}, f32[12,768]{1,0:T(8,128)}) custom-call(s32[272]{0:T(512)} %copy-done, bf16[288,48,768]{2,1,0:T(8,128)(2,1)} %bitcast.66, f32[12,208,768]{2,1,0:T(8,128)} %get-tuple-element.66.dx1, bf16[12,208,768]{2,1,0:T(8,128)(2,1)} %get-tuple-element.67.hid0, ...), custom_call_target="tpu_custom_call" | custom-call | tf_op jit(solution)/shard_map/time_backward/pallas_call | solution.py:719
  449.7 1.1 fusion.24
  451.6 1.1 slice.78
  454.8 5.4 pack.1
  460.4 5.1 collective-permute-done
  465.6 1.6 copy-done.10
  467.2 3.1 convert_add_fusion.1
  470.3 1.5 copy-done.2
  472.7 1.4 collective-permute-start.1
  475.7 14.8 %collective-permute-done.1 = bf16[2,448,384]{2,1,0:T(8,128)(2,1)S(1)} collective-permute-done((bf16[2,448,384]{2,1,0:T(8,128)(2,1)}, bf16[2,448,384]{2,1,0:T(8,128)(2,1)S(1)}, u32[]{:S(2)}, u32[]{:S(2)}) %collective-permute-start.1) | collective-permute-done | bytes 688160 | tf_op jit(solution)/shard_map/ppermute | solution.py:560
  490.5 1.5 bitcast_add_fusion.1
  491.9 1.1 copy-done.6
  493.1 1.5 collective-permute-start.2
  494.6 1.2 bitcast_add_fusion
  497.1 5.5 collective-permute-done.2
  502.6 1.2 bitcast_add_fusion.3
  503.8 1.5 collective-permute-done.4
  508.1 8.6 %all-gather = f32[128,768]{1,0:T(8,128)S(1)} all-gather(f32[16,768]{1,0:T(8,128)S(1)} %fusion.16), channel_id=2, replica_groups=mesh['dp'=8,'mlp'=4] {'dp'}, dimensions={0}, use_global_device_ids=true | all-gather | bytes 442368 | tf_op jit(solution)/shard_map/all_gather | solution.py:911
  517.4 18.0 %all-gather.1 = f32[8,32,768]{2,1,0:T(8,128)S(1)} all-gather(f32[8,8,768]{2,1,0:T(8,128)S(1)} %slice.103), channel_id=3, replica_groups=mesh['dp'=8,'mlp'=4] {'mlp'}, dimensions={1}, use_global_device_ids=true | all-gather | bytes 983040 | tf_op jit(solution)/shard_map/all_gather | solution.py:914
  536.9 1.9 multiply_reduce_fusion.1
  540.9 3.3 multiply_subtract_fusion.2
  544.2 2.8 multiply_subtract_fusion
  547.4 2.5 multiply_subtract_fusion.1
  (128 shorter events, 25.3 us)
Async XLA Ops:
  7.2 2.3 copy-start.17
  7.2 19.3 %copy-start.22 = (s32[1,12]{1,0:T(1,128)S(1)}, s32[1,12]{1,0:T(1,128)}, u32[]{:S(2)}) copy-start(s32[1,12]{1,0:T(1,128)} %param.18) | copy-start | bytes 148
  7.2 142.8 %all-gather.4.cloned.1.call-start = ((), (), s32[]{:S(2)}) async-start(), calls=%async_computation | async-start | bytes 21897216 | tf_op jit(solution)/shard_map/all_gather | solution.py:645
  28.5 4.4 copy-start.9
  33.5 2.3 copy-start.4
  35.9 1.9 copy-start.20
  36.0 2.5 copy-start.16
  36.2 7.8 %copy-start.21 = (s32[1,12]{1,0:T(1,128)S(1)}, s32[1,12]{1,0:T(1,128)}, u32[]{:S(2)}) copy-start(s32[1,12]{1,0:T(1,128)} %param.19) | copy-start | bytes 148
  38.7 111.3 %copy-start = (s32[272]{0:T(512)}, s32[272]{0:T(512)S(1)}, u32[]{:S(2)}) copy-start(s32[272]{0:T(512)S(1)} %multiply_add_fusion.3.slots.s) | copy-start | bytes 3268
  374.2 79.3 %copy-start.19 = (f32[8,768]{1,0:T(8,128)S(1)}, f32[8,768]{1,0:T(8,128)}, u32[]{:S(2)}) copy-start(f32[8,768]{1,0:T(8,128)} %get-tuple-element.80) | copy-start | bytes 73732
  374.2 79.3 %copy-start.18 = (f32[8,768]{1,0:T(8,128)S(1)}, f32[8,768]{1,0:T(8,128)}, u32[]{:S(2)}) copy-start(f32[8,768]{1,0:T(8,128)} %get-tuple-element.81) | copy-start | bytes 73732
  460.2 5.4 collective-permute-start
  465.6 1.6 copy-start.10
  470.3 1.5 copy-start.2
  472.7 17.7 %collective-permute-start.1 = (bf16[2,448,384]{2,1,0:T(8,128)(2,1)}, bf16[2,448,384]{2,1,0:T(8,128)(2,1)S(1)}, u32[]{:S(2)}, u32[]{:S(2)}) collective-permute-start(bf16[2,448,384]{2,1,0:T(8,128)(2,1)} %fusion.4), channel_id=1, source_target_pairs={{0,8},{4,12},{8,0},{12,4},{16,24},{20,28},{24,16},{28,20},{1,9},{5... | collective-permute-start | bytes 2064392 | tf_op jit(solution)/shard_map/ppermute | solution.py:560
  475.1 19.6 %collective-permute-start.3 = (bf16[2,448,384]{2,1,0:T(8,128)(2,1)}, bf16[2,448,384]{2,1,0:T(8,128)(2,1)}, u32[]{:S(2)}, u32[]{:S(2)}) collective-permute-start(bf16[2,448,384]{2,1,0:T(8,128)(2,1)} %fusion.5), channel_id=1, source_target_pairs={{0,16},{4,20},{8,24},{12,28},{16,0},{20,4},{24,8},{28,12},{1,17},{... | collective-permute-start | bytes 2064392 | tf_op jit(solution)/shard_map/ppermute | solution.py:560
  491.9 1.1 copy-start.6
  493.1 3.5 copy-start.1
  493.1 9.5 %collective-permute-start.2 = (bf16[448,384]{1,0:T(8,128)(2,1)S(1)}, bf16[448,384]{1,0:T(8,128)(2,1)S(1)}, u32[]{:S(2)}, u32[]{:S(2)}) collective-permute-start(bf16[448,384]{1,0:T(8,128)(2,1)S(1)} %fusion.7), channel_id=1, source_target_pairs={{0,16},{4,20},{8,24},{12,28},{16,0},{20,4},{24,8},{28,12},{1,17},{... | collective-permute-start | bytes 1032200 | tf_op jit(solution)/shard_map/ppermute | solution.py:560
  495.9 1.1 copy-start.7
  495.9 9.3 %collective-permute-start.4 = (bf16[448,384]{1,0:T(8,128)(2,1)S(1)}, bf16[448,384]{1,0:T(8,128)(2,1)}, u32[]{:S(2)}, u32[]{:S(2)}) collective-permute-start(bf16[448,384]{1,0:T(8,128)(2,1)S(1)} %fusion.8), channel_id=1, source_target_pairs={{0,8},{4,12},{8,0},{12,4},{16,24},{20,28},{24,16},{28,20},{1,9},{5... | collective-permute-start | bytes 1032200 | tf_op jit(solution)/shard_map/ppermute | solution.py:560
  497.0 8.2 %copy-start.8 = (f32[2,448,384]{2,1,0:T(8,128)S(1)}, f32[2,448,384]{2,1,0:T(8,128)}, u32[]{:S(2)}) copy-start(f32[2,448,384]{2,1,0:T(8,128)} %copy-done.7) | copy-start | bytes 4128772
  503.7 4.3 copy-start.15
  540.9 3.3 copy-start.3
  540.9 3.3 copy-start.11
  540.9 3.3 copy-start.12
  544.2 2.8 copy-start.5
  544.2 2.8 copy-start.13
  544.2 3.1 copy-start.14
Sparse Core Ops, SparseCore 0:
  11.4 138.5 all-gather.3

commit v2 on v1

--- a/solution.py
+++ b/solution.py
@@ -287,8 +287,9 @@
         gp_ref[j] = slope.astype(bf16).reshape(cut)
         acts[:, lanes] = active.astype(bf16)
         stream = stream + mm(acts[:, lanes], downs[lanes])
-    own = pl.ds(pl.multiple_of(member[0] * width, 128), width)
-    act_ref[...] = acts[:, own].reshape(cut)
+    for i in range(2):
+        own = pl.ds(pl.multiple_of((member[0] ^ i) * width, 128), width)
+        act_ref[i] = acts[:, own].reshape(cut)
     stream = stream + low_now[2:3]
     xhat, rstd = normed(stream)
     hat3_ref[...] = xhat.astype(bf16).reshape(cut)
@@ -301,9 +302,9 @@
 
 
 def mlp_backward(
-    slots, frame_weight, member, patches, gathered, pool, head, valid, targets, total,
+    slots, frame_weight, member, patches, gathered, pool, pool_other, head, valid, targets, total,
     hid2, hat2, rstd2, hat3, rstd3, gp, act, low_rows,
-    dx2_ref, up_ref, down_ref, rows_ref, small_ref,
+    dx2_ref, own_ref, other_ref, rows_ref, small_ref,
     ups, downs, dus, spread, up_sum, down_sum, row_sums, sems,
 ):
     step = pl.program_id(0)
@@ -316,7 +317,7 @@
     def _():
         fetch(slots, gathered, downs, sems.at[1], lambda t: 2 * t + 10, False)
         fetch(slots, gathered, ups, sems.at[0], lambda t: 2 * t + 9, True)
-        pooled = jnp.sum(pool[...], axis=0, keepdims=True).astype(bf16)
+        pooled = jnp.sum(pool[...] + pool_other[...], axis=0, keepdims=True).astype(bf16)
         pooled8 = jnp.broadcast_to(pooled, (8, width))
         logits = mm(pooled8, head[...])
         valid_f = valid[...]
@@ -359,9 +360,10 @@
         arrive(ups, sems.at[0])
 
     grad_hidden = mm_nt(dus[...], ups[...])
-    own = pl.ds(pl.multiple_of(member[0] * width, 128), width)
-    up_sum[...] += mm_tn(hid2[...].reshape(flat), dus[:, own])
-    down_sum[...] += mm_tn(act[...].reshape(flat), grad_b)
+    for i in range(2):
+        own = pl.ds(pl.multiple_of((member[0] ^ i) * width, 128), width)
+        up_sum[i] += mm_tn(hid2[...].reshape(flat), dus[:, own])
+        down_sum[i] += mm_tn(act[i].reshape(flat), grad_b)
     xhat = hat2[...].reshape(flat).astype(f32)
     rstd = rstd2[...].reshape(flat[0], 128)[:, 0:1]
     row_sums[0] += fold(grad_hidden * xhat)
@@ -370,8 +372,9 @@
 
     @pl.when(step == pl.num_programs(0) - 1)
     def _():
-        up_ref[...] = up_sum[...].astype(bf16)
-        down_ref[...] = down_sum[...].astype(bf16)
+        for i, ref in enumerate((own_ref, other_ref)):
+            ref[0] = up_sum[i].astype(bf16)
+            ref[1] = down_sum[i].astype(bf16)
         rows_ref[...] = jnp.zeros_like(rows_ref)
         for i in range(5):
             rows_ref[i : i + 1] = jnp.sum(row_sums[i], axis=0, keepdims=True)
@@ -402,23 +405,26 @@
         ref[...] = jnp.zeros_like(ref)
 
 
-def finish_attention(tile_ref, at, rows_ref, joint_sum, out_sum, row_sums):
-    share = tile_ref.shape[1]
-    width = tile_ref.shape[2]
+def finish_attention(tile_refs, at, rows_ref, joint_sum, out_sum, row_sums):
+    share, width = tile_refs[0].shape[1:]
     rows_ref[...] = jnp.zeros_like(rows_ref)
-    for i in range(3):
-        tile_ref[at + i] = joint_sum[:share, i * width : (i + 1) * width].astype(bf16)
-    tile_ref[at + 3] = out_sum[:share].astype(bf16)
+    for n, tile_ref in enumerate(tile_refs):
+        here = slice(n * share, (n + 1) * share)
+        for i in range(3):
+            tile_ref[at + i] = joint_sum[here, i * width : (i + 1) * width].astype(bf16)
+        tile_ref[at + 3] = out_sum[here].astype(bf16)
+    last = slice(2 * share, 2 * share + 1)
     for i in range(2):
         rows_ref[i : i + 1] = jnp.sum(row_sums[i], axis=0, keepdims=True)
-    rows_ref[2:3] = joint_sum[share : share + 1, :width]
-    rows_ref[3:4] = joint_sum[share : share + 1, 2 * width :]
-    rows_ref[4:5] = out_sum[share : share + 1]
+    rows_ref[2:3] = joint_sum[last, :width]
+    rows_ref[3:4] = joint_sum[last, 2 * width :]
+    rows_ref[4:5] = out_sum[last]
 
 
 def space_backward(
     slots, gathered, dx2, hid1, hat1, rstd1, q, k, v, o, rows, picked, extra_q, extra_k,
-    dx1_ref, tile_ref, rows_ref, joint, out, joint_sum, out_sum, row_sums, grads, outer, sems,
+    g1_ref, own_ref, other_ref, rows_ref,
+    joint, out, joint_sum, out_sum, row_sums, grads, outer, sems,
 ):
     step = pl.program_id(0)
     cut = hid1.shape
@@ -447,21 +453,21 @@
 
         attend_back(load, store, extra_q, extra_k)
     picked_now = picked[...]
-    dx1_ref[...] = close_attention(
+    g1_ref[...] = close_attention(
         dx2[...].reshape(flat), grad_b, hid1[...].reshape(flat), hat1[...].reshape(flat),
         rstd1[...].reshape(flat[0], 128), grads[...], o[...].reshape(flat), rows[...],
         picked_now, ones_row(picked_now), joint, joint_sum, out_sum, row_sums,
-    ).reshape(cut)
+    ).astype(bf16).reshape(cut)
 
     @pl.when(step == pl.num_programs(0) - 1)
     def _():
-        finish_attention(tile_ref, 0, rows_ref, joint_sum, out_sum, row_sums)
+        finish_attention((own_ref, other_ref), 0, rows_ref, joint_sum, out_sum, row_sums)
 
 
 def time_backward(
-    total, slots, gathered, dx1, hid0, hat0, rstd0, q, k, v, o, pixels, rows, picked,
+    rest, slots, member, gathered, near, far, hid0, hat0, rstd0, q, k, v, o, pixels, rows, picked,
     extra_q, extra_k,
-    tile_ref, rows_ref, pos_ref, frame_ref,
+    own_ref, other_ref, rows_ref, pos_ref, frame_ref,
     joint, out, joint_sum, out_sum, embed_sum, row_sums, grads, outer, sems,
 ):
     step = pl.program_id(0)
@@ -480,7 +486,11 @@
         flat = (frames * groups * GROUP, width)
         small = (frames, GROUP, PAIR)
         here = slice(0, groups * GROUP)
-        grad_b = dx1[:, here].reshape(flat).astype(bf16)
+        first = member[0] % 2 == 0
+        near_now, far_now = near[:, here], far[:, here]
+        grad_b = jnp.concatenate(
+            [jnp.where(first, near_now, far_now), jnp.where(first, far_now, near_now)]
+        ).reshape(flat)
         outer[:, here] = mm_nt(grad_b, out[...]).astype(bf16).reshape(cut)
         for g in range(groups):
             part = slice(g * GROUP, (g + 1) * GROUP)
@@ -499,7 +509,7 @@
             attend_back(load, store, extra_q, extra_k)
         picked_now = picked[...]
         grad = close_attention(
-            dx1[:, here].reshape(flat), grad_b, hid0[:, here].reshape(flat),
+            grad_b.astype(f32), grad_b, hid0[:, here].reshape(flat),
             hat0[:, here].reshape(flat), rstd0[:, here].reshape(flat[0], 128),
             grads[:, here].reshape(flat[0], 3 * width), o[:, here].reshape(flat), rows[...],
             picked_now, ones_row(picked_now), joint, joint_sum, out_sum, row_sums,
@@ -510,17 +520,32 @@
         pos_ref[here] = jnp.sum(cube, axis=0)
         frame_ref[...] += jnp.sum(cube, axis=1)
 
-    by_groups(span // GROUP, total, work)
-
-    @pl.when(step == pl.num_programs(0) - 1)
+    last = step == pl.num_programs(0) - 1
+    if rest == 0:
+        work(span // GROUP)
+    else:
+        odd = member[0] % 2 == 1
+        pl.when(jnp.logical_not(last))(lambda: work(span // GROUP))
+        pl.when(jnp.logical_and(last, jnp.logical_not(odd)))(lambda: work(rest))
+
+        @pl.when(jnp.logical_and(last, odd))
+        def _():
+            pos_ref[...] = jnp.zeros_like(pos_ref)
+
+    @pl.when(last)
     def _():
-        finish_attention(tile_ref, 1, rows_ref, joint_sum, out_sum, row_sums)
-        tile_ref[0] = embed_sum[: tile_ref.shape[1]].astype(bf16)
+        finish_attention((own_ref, other_ref), 1, rows_ref, joint_sum, out_sum, row_sums)
+        share = own_ref.shape[1]
+        own_ref[0] = embed_sum[:share].astype(bf16)
+        other_ref[0] = embed_sum[share : 2 * share].astype(bf16)
 
 
 def pack(dests, core, *refs):
-    sources, table_ref, keep_ref, send_ref, sems = refs[:-4], refs[-4], refs[-3], refs[-2], refs[-1]
-    slots = (keep_ref.shape[1] - table_ref.shape[1]) // BR
+    count = (len(refs) - 3) // 3
+    owns, others, sums = refs[:count], refs[count : 2 * count], refs[-1 - count : -1]
+    keep_ref, send_ref, sems = refs[2 * count], refs[2 * count + 1], refs[-1]
+    table_rows = sums[-1].shape[1]
+    slots = (keep_ref.shape[1] - table_rows) // BR
 
     def route(source, chunk, place, sem):
         mine = chunk % 2 == core[0]
@@ -534,24 +559,22 @@
             pltpu.make_async_copy(source, send_ref.at[chunk // 2, place], sem).start()
 
     first = 0
-    for n, source in enumerate(sources):
-
-        def one(i, carry, source=source, first=first, n=n):
-            dest = dests[first + i]
-            row = pl.multiple_of((dest % slots) * BR, 16)
-            route(source.at[i], dest // slots, pl.ds(row, BR), sems.at[n])
+    for n, (own, other, source) in enumerate(zip(owns, others, sums)):
+        table = n == count - 1
+
+        def one(i, carry, own=own, other=other, source=source, first=first, n=n, table=table):
+            source[i] = (own[i].astype(f32) + other[i].astype(f32)).astype(bf16)
+            if table:
+                route(source.at[i], i, pl.ds(slots * BR, table_rows), sems.at[n])
+            else:
+                dest = dests[first + i]
+                row = pl.multiple_of((dest % slots) * BR, 16)
+                route(source.at[i], dest // slots, pl.ds(row, BR), sems.at[n])
             return carry
 
         lax.fori_loop(0, source.shape[0], one, 0)
         first += source.shape[0]
-
-    def one_table(i, carry):
-        place = pl.ds(slots * BR, table_ref.shape[1])
-        route(table_ref.at[i], i, place, sems.at[len(sources)])
-        return carry
-
-    lax.fori_loop(0, table_ref.shape[0], one_table, 0)
-    for n, source in enumerate(sources + (table_ref,)):
+    for n, source in enumerate(sums):
         pltpu.make_async_copy(source, source, sems.at[n]).wait()
 
 
@@ -680,9 +703,13 @@
     ).astype(f32)
     valid_f = label_valid.astype(f32)
     label_total = lax.psum(jnp.sum(valid_f), "dp")
+    pix, label_total = lax.optimization_barrier((pix, label_total))
     share = width // mlp_count
-    pick_row = jnp.arange(share)
-    pick_feature = (pick_row // BR) * (BR * mlp_count) + member * BR + pick_row % BR
+    half = member % 2
+    pick_row = jnp.arange(2 * share)
+    pick_member = jnp.where(pick_row < share, member, member ^ 1)
+    pick_row = pick_row % share
+    pick_feature = (pick_row // BR) * (BR * mlp_count) + pick_member * BR + pick_row % BR
     picked = (pick_feature[:, None] == jnp.arange(width)[None, :]).astype(bf16)
     picked = jnp.pad(picked, ((0, 16), (0, 0)))
     member_s = member[None]
@@ -705,7 +732,29 @@
         (mlp_count, FRAMES_AT_ONCE, padded, width), lambda f, *_: (0, f, 0, 0)
     )
     time_grid = (-(-groups // GROUPS_AT_ONCE),)
-    space_grid = (frames // FRAMES_AT_ONCE,)
+    half_frames = frames // 2
+    space_grid = (half_frames // FRAMES_AT_ONCE,)
+    half_blocks = groups // 2 // GROUPS_AT_ONCE
+    rest = groups - 2 * half_blocks * GROUPS_AT_ONCE
+    half_rows = (half_blocks * GROUPS_AT_ONCE + rest) * GROUP
+    back_grid = (half_blocks + (1 if rest else 0),)
+
+    def half_index(s, m):
+        ending = jnp.where(m[0] % 2 == 0, 2 * half_blocks, 2 * half_blocks - 1)
+        return jnp.where(s < half_blocks, (m[0] % 2) * half_blocks + s, ending)
+
+    back_spec = pl.BlockSpec((frames, group_rows, width), lambda s, i, m: (0, half_index(s, m), 0))
+    back_thin = pl.BlockSpec((frames, group_rows, 128), lambda s, i, m: (0, half_index(s, m), 0))
+    near_spec = pl.BlockSpec((half_frames, group_rows, width), lambda s, *_: (0, s, 0))
+    my_frame_spec = pl.BlockSpec(
+        (FRAMES_AT_ONCE, padded, width),
+        lambda f, s, w, m: ((m[0] % 2) * (half_frames // FRAMES_AT_ONCE) + f, 0, 0),
+    )
+    act_spec = pl.BlockSpec((2, FRAMES_AT_ONCE, padded, width), lambda f, *_: (0, f, 0, 0))
+    half16 = jax.ShapeDtypeStruct((half_frames, padded, width), bf16)
+    half32 = jax.ShapeDtypeStruct((half_frames, padded, width), f32)
+    half_thin = jax.ShapeDtypeStruct((half_frames, padded, 128), f32)
+    frame_weight = lax.dynamic_slice_in_dim(frame_weight, half * half_frames, half_frames)
 
     def whole(*shape):
         return pl.BlockSpec(shape, lambda i, *_: (0,) * len(shape))
@@ -713,9 +762,9 @@
     rows_spec = whole(8, width)
     time_extra = whole(2 * frames * GROUP, PAIR)
     space_extra = whole(2 * padded, PAIR)
-    pick_spec = whole(share + 16, width)
-
-    def call(kernel, name, scalars, grid, ins, in_specs, outs, out_specs, scratch):
+    pick_spec = whole(2 * share + 16, width)
+
+    def call(kernel, name, units, scalars, grid, ins, in_specs, outs, out_specs, scratch):
         return pl.pallas_call(
             kernel,
             grid_spec=pltpu.PrefetchScalarGridSpec(
@@ -727,6 +776,11 @@
             ),
             out_shape=outs,
             compiler_params=params,
+            cost_estimate=pl.CostEstimate(
+                flops=units * 2 * frames * padded * width * width,
+                bytes_accessed=16 * width * width,
+                transcendentals=0,
+            ),
             name=name,
         )(*scalars, gathered, *ins)
 
@@ -736,6 +790,7 @@
     x1, hid0, hat0, rstd0, q_t, k_t, v_t, o_t = call(
         partial(time_forward, groups),
         "time_forward",
+        14,
         [slot_index],
         time_grid,
         [pix, pos, trow, time_rows, time_q, time_k],
@@ -748,18 +803,23 @@
     (hid1, hat1, rstd1, q_s, k_s, v_s, o_s, hid2, hat2, rstd2, hat3, rstd3, gp, act, pool) = call(
         lambda s, fw, m, *refs: space_forward(s, fw, m, patches, *refs),
         "space_forward",
+        15,
         [slot_index, frame_weight, member_s],
         space_grid,
         [x1, space_rows, low_rows, space_q, space_k],
-        [frame_spec, rows_spec, rows_spec, space_extra, space_extra],
-        [cube16, cube16, thin32]
-        + [cube16] * 4
-        + [cube16, cube16, thin32, cube16, thin32]
-        + [jax.ShapeDtypeStruct((mlp_count, frames, padded, width), bf16), cube16, row32],
+        [my_frame_spec, rows_spec, rows_spec, space_extra, space_extra],
+        [half16, half16, half_thin]
+        + [half16] * 4
+        + [half16, half16, half_thin, half16, half_thin]
+        + [
+            jax.ShapeDtypeStruct((mlp_count, half_frames, padded, width), bf16),
+            jax.ShapeDtypeStruct((2, half_frames, padded, width), bf16),
+            row32,
+        ],
         [frame_spec, frame_spec, frame_thin]
         + [frame_spec] * 4
         + [frame_spec, frame_spec, frame_thin, frame_spec, frame_thin]
-        + [gp_spec, frame_spec, rows_spec],
+        + [gp_spec, act_spec, rows_spec],
         tile_bufs((1, 3), (1, 1), (1, mlp_count), (mlp_count, 1))
         + [pltpu.VMEM((frame_rows, mlp_count * width), bf16), pltpu.SemaphoreType.DMA((4,))],
     )
@@ -767,42 +827,46 @@
     head_b = jnp.pad(head_weight.astype(bf16), ((0, 0), (0, class_pad - classes)))
     valid_p = jnp.pad(valid_f, ((0, 0), (0, class_pad - classes)))
     targets_p = jnp.pad(targets, ((0, 0), (0, class_pad - classes)))
-    square16 = jax.ShapeDtypeStruct((width, width), bf16)
-    dx2, grad_up, grad_down, rows_low, small = call(
+    pool_other = swap(pool, "mlp", 1)
+    squares16 = jax.ShapeDtypeStruct((2, width, width), bf16)
+    dx2, own_mlp, other_mlp, rows_low, small = call(
         lambda s, fw, m, *refs: mlp_backward(s, fw, m, patches, *refs),
         "mlp_backward",
+        13,
         [slot_index, frame_weight, member_s],
         space_grid,
         [
-            pool, head_b, valid_p, targets_p, label_total[None],
+            pool, pool_other, head_b, valid_p, targets_p, label_total[None],
             hid2, hat2, rstd2, hat3, rstd3, gp, act, low_rows,
         ],
         [
-            rows_spec, whole(width, class_pad), whole(1, class_pad), whole(1, class_pad),
+            rows_spec, rows_spec, whole(width, class_pad), whole(1, class_pad), whole(1, class_pad),
             pl.BlockSpec(memory_space=pltpu.SMEM),
-            frame_spec, frame_spec, frame_thin, frame_spec, frame_thin, gp_spec, frame_spec,
+            frame_spec, frame_spec, frame_thin, frame_spec, frame_thin, gp_spec, act_spec,
             rows_spec,
         ],
-        [cube32, square16, square16, row32, row32],
-        [frame_spec, whole(width, width), whole(width, width), rows_spec, rows_spec],
+        [half32, squares16, squares16, row32, row32],
+        [frame_spec, whole(2, width, width), whole(2, width, width), rows_spec, rows_spec],
         tile_bufs((1, mlp_count), (mlp_count, 1))
         + [
             pltpu.VMEM((frame_rows, mlp_count * width), bf16),
             pltpu.VMEM((8, width), f32),
-            pltpu.VMEM((width, width), f32),
-            pltpu.VMEM((width, width), f32),
+            pltpu.VMEM((2, width, width), f32),
+            pltpu.VMEM((2, width, width), f32),
             pltpu.VMEM((5, 8, width), f32),
             pltpu.SemaphoreType.DMA((2,)),
         ],
     )
 
     sums = [
-        pltpu.VMEM((share + 16, 3 * width), f32),
-        pltpu.VMEM((share + 16, width), f32),
+        pltpu.VMEM((2 * share + 16, 3 * width), f32),
+        pltpu.VMEM((2 * share + 16, width), f32),
     ]
-    dx1, tiles_space, rows_space = call(
+    met_mlp = swap(other_mlp, "mlp", 1)
+    g1, own_space, other_space, rows_space = call(
         space_backward,
         "space_backward",
+        16,
         [slot_index],
         space_grid,
         [dx2, hid1, hat1, rstd1, q_s, k_s, v_s, o_s, space_rows, picked, space_q, space_k],
@@ -810,8 +874,8 @@
         + [frame_thin]
         + [frame_spec] * 4
         + [rows_spec, pick_spec, space_extra, space_extra],
-        [cube32, jax.ShapeDtypeStruct((4, share, width), bf16), row32],
-        [frame_spec, whole(4, share, width), rows_spec],
+        [half16] + [jax.ShapeDtypeStruct((4, share, width), bf16)] * 2 + [row32],
+        [frame_spec] + [whole(4, share, width)] * 2 + [rows_spec],
         tile_bufs((1, 3), (1, 1))
         + sums
         + [
@@ -821,27 +885,40 @@
             pltpu.SemaphoreType.DMA((2,)),
         ],
     )
-    tiles_time, rows_time, grad_pos, grad_frames = call(
-        partial(time_backward, groups),
+
+
+    def patches_of(which):
+        main = half_blocks * group_rows
+        here = lax.dynamic_slice_in_dim(g1, which * main, main, 1)
+        return jnp.concatenate([here, g1[:, 2 * main :]], axis=1)
+
+    far = swap(patches_of(1 - half), "mlp", 1)
+    near = patches_of(half)
+    near, met_mlp = lax.optimization_barrier((near, met_mlp))
+    met_space = swap(other_space, "mlp", 1)
+    own_time, other_time, rows_time, grad_pos, grad_frames = call(
+        partial(time_backward, rest),
         "time_backward",
-        [slot_index],
-        time_grid,
-        [dx1, hid0, hat0, rstd0, q_t, k_t, v_t, o_t, pix, time_rows, picked, time_q, time_k],
-        [group_spec] * 3
-        + [group_thin]
-        + [group_spec] * 5
+        18,
+        [slot_index, member_s],
+        back_grid,
+        [near, far, hid0, hat0, rstd0, q_t, k_t, v_t, o_t, pix, time_rows, picked, time_q, time_k],
+        [near_spec] * 2
+        + [back_spec] * 2
+        + [back_thin]
+        + [back_spec] * 5
         + [rows_spec, pick_spec, time_extra, time_extra],
-        [
-            jax.ShapeDtypeStruct((5, share, width), bf16),
+        [jax.ShapeDtypeStruct((5, share, width), bf16)] * 2
+        + [
             row32,
-            jax.ShapeDtypeStruct((padded, width), f32),
+            jax.ShapeDtypeStruct((half_rows, width), f32),
             jax.ShapeDtypeStruct((frames, width), f32),
         ],
-        [whole(5, share, width), rows_spec, patch_spec, whole(frames, width)],
+        [whole(5, share, width)] * 2 + [rows_spec, patch_spec, whole(frames, width)],
         tile_bufs((1, 3), (1, 1))
         + sums
         + [
-            pltpu.VMEM((share + 16, width), f32),
+            pltpu.VMEM((2 * share + 16, width), f32),
             pltpu.VMEM((2, 8, width), f32),
             pltpu.VMEM((frames, group_rows, 3 * width), bf16),
             pltpu.VMEM((frames, group_rows, width), bf16),
@@ -850,6 +927,12 @@
     )
 
     grad_time = jnp.einsum("ft,fd->td", time_hot, grad_frames, precision=highest)
+    other_time, met_space = lax.optimization_barrier((other_time, met_space))
+    met_time = swap(other_time, "mlp", 1)
+    main = half_blocks * group_rows
+    all_pos = jnp.concatenate(
+        [jnp.where(half == i, grad_pos[:main], 0.0) for i in range(2)] + [grad_pos[main:]]
+    )
     table_rows = tables.shape[0]
     table_part = jnp.concatenate(
         [
@@ -857,7 +940,7 @@
             rows_time[:5],
             rows_space[:5],
             rows_low[:5],
-            grad_pos[:patches],
+            all_pos[:patches],
             grad_time,
         ]
     )
@@ -865,12 +948,18 @@
     table_part = jnp.pad(
         table_part, ((0, rows_each * dp_count * mlp_count - table_rows), (0, 0))
     ).reshape(dp_count, mlp_count, rows_each, width)
-    table_part = lax.dynamic_index_in_dim(table_part, member, 1, False).astype(bf16)
-    table_part = jnp.pad(table_part, ((0, 0), (0, 16 - rows_each), (0, 0)))
-
-    sources = [
-        part.reshape(-1, BR, width) for part in (tiles_time, tiles_space, grad_up, grad_down)
-    ]
+
+    def table_of(which):
+        rows_now = lax.dynamic_index_in_dim(table_part, which, 1, False).astype(bf16)
+        return jnp.pad(rows_now, ((0, 0), (0, 16 - rows_each), (0, 0)))
+
+    met_table = swap(table_of(member ^ 1), "mlp", 1)
+
+    def blocks_of(*parts):
+        return [part.reshape(-1, BR, width) for part in parts]
+
+    sources = blocks_of(own_time, own_space, own_mlp) + [table_of(member)]
+    sources = sources + blocks_of(met_time, met_space, met_mlp) + [met_table]
     shared_here = shared_blocks // mlp_count
     here_ids = jnp.arange(shared_here + 2 * per_tile)
     block_of = jnp.where(
@@ -887,14 +976,15 @@
         grid_spec=pltpu.PrefetchScalarGridSpec(
             num_scalar_prefetch=2,
             grid=(1,),
-            in_specs=[pl.BlockSpec(memory_space=pltpu.VMEM)] * 5,
+            in_specs=[pl.BlockSpec(memory_space=pltpu.VMEM)] * 8,
             out_specs=[any_spec] * 2,
-            scratch_shapes=[pltpu.SemaphoreType.DMA((5,))],
+            scratch_shapes=[pltpu.VMEM(part.shape, bf16) for part in sources[:4]]
+            + [pltpu.SemaphoreType.DMA((4,))],
         ),
         out_shape=[chunk, chunk],
         compiler_params=params,
         name="pack",
-    )(dests, (place % 2)[None], *sources, table_part)
+    )(dests, (place % 2)[None], *sources)
     summed = halve(kept, sent, "dp")
     my_slots = (place * mlp_count + member) * slots + jnp.arange(slots)
     filled = jnp.any(slot_index[:, None] == my_slots[None, :], axis=0)
@@ -908,10 +998,13 @@
             small,
         ]
     )
-    blocks = lax.all_gather(block, "dp", axis=0)
-    grad_head = jnp.einsum("cd,ck->dk", blocks[:, 8], blocks[:, 9, :classes], precision=highest)
-    loss_sum = jnp.sum(blocks[:, 10, 0])
-    blocks = lax.all_gather(blocks[:, :8], "mlp", axis=1)
+    blocks = jnp.concatenate(
+        [lax.all_gather(block[:8], "mlp", axis=0), block[None, 8:]], axis=0
+    )
+    blocks = lax.all_gather(blocks, "dp", axis=0)
+    heads, blocks = blocks[:, mlp_count], blocks[:, :mlp_count]
+    grad_head = jnp.einsum("cd,ck->dk", heads[:, 0], heads[:, 1, :classes], precision=highest)
+    loss_sum = jnp.sum(heads[:, 2, 0])
     grad_tables = blocks[:, :, :rows_each].reshape(-1, width)[:table_rows]
     grad_norm = jnp.sqrt(
         jnp.sum(blocks[:, :, 7, 0])

time: 566 us -> 537 us (0.949)
  Pallas kernels: 305 us -> 208 us
  waiting for transfers between devices: 132 us -> 186 us
  local copies, waits for them, and re-layouts: 23.4 us -> 32.7 us
    pallas_call x5, Pallas kernels: 300 us -> 201 us  [call(): pl.pallas_call(kernel, grid_spec=pltpu.PrefetchScalarGridSpec(num_scalar_...]
    ppermute x5 -> x11, waiting for transfers between devices: 26.9 us -> 76.7 us  [swap(): return lax.ppermute(value, axis, [(i, i ^ hop) for i in range(size)])]
  transfers between devices with their start and end apart: 6 -> 12, of which waited for: 5 -> 9; matrix products, arithmetic and copies ran while one was open for 4% -> 7% of each run, Pallas kernels for 0% -> 17%
where the time goes in v2:
time: 537 us; the launch traced here: 529 us
  Pallas kernels  208 us (39%)
  waiting for transfers between devices  186 us (35%)
  blocking collectives  38.9 us (7%)
  local copies, waits for them, and re-layouts  32.7 us (6%)
  other arithmetic  31.3 us (6%)
  between operations  18.8 us (4%)
  starting transfers between devices  9.93 us (2%)
    pallas_call x5, Pallas kernels, call(): pl.pallas_call(kernel, grid_spec=pltpu.PrefetchScalarGridSpec(num_scalar_...  201 us
    all_gather x1, waiting for transfers between devices, local(): lax.all_gather(slot_weight.astype(bf16), ('dp', 'mlp'), axis=0, tiled=True)  110 us
    ppermute x11, waiting for transfers between devices, swap(): return lax.ppermute(value, axis, [(i, i ^ hop) for i in range(size)])  76.7 us
    psum x1, blocking collectives, local(): label_total = lax.psum(jnp.sum(valid_f), 'dp')  15.7 us
    all_gather x1, blocking collectives, local(): lax.all_gather(block[:8], 'mlp', axis=0)  13.2 us
  transfers between devices with their start and end apart: 12, of which 9 were waited for; matrix products, arithmetic and copies ran while one was open for 7% of the time, Pallas kernels for 17%

profile of v2, /device:TPU:0, one launch (start us, length us, event | category | flops | bytes accessed | tf_op | source)
XLA Modules:
  0.0 529.3 jit_solution(15169604341562389899)
XLA Ops:
  7.2 2.2 convert_element_type.117
  10.1 15.7 %psum.7 = f32[]{:T(128)} all-reduce(f32[]{:T(128)} %convert_reduce_fusion.1), channel_id=1, replica_groups=mesh['dp'=8,'mlp'=4] {'dp'}, use_global_device_ids=true, to_apply=%region_2.3 | all-reduce | flops 1 | bytes 8 | tf_op jit(solution)/shard_map/psum | solution.py:705
  28.5 4.2 pad.63.pixels
  40.3 109.7 %all-gather.4.cloned.1.call-done = bf16[13824,768]{1,0:T(8,128)(2,1)} async-done(((bf16[432,768]{1,0:T(8,128)(2,1)}), bf16[13824,768]{1,0:T(8,128)(2,1)}) %all-gather.4.cloned.1.call-update) | async-done | bytes 21233680 | tf_op jit(solution)/shard_map/all_gather | solution.py:668
  150.0 36.1 %time_forward.1 = (f32[12,208,768]{2,1,0:T(8,128)}, bf16[12,208,768]{2,1,0:T(8,128)(2,1)}, bf16[12,208,768]{2,1,0:T(8,128)(2,1)}, f32[12,208,128]{2,1,0:T(8,128)...) custom-call(s32[272]{0:T(512)} %multiply_add_fusion.3.slots.s, ...), custom_call_target="tpu_custom_call" | custom-call | flops 41221619712 | bytes 9437184 | tf_op jit(solution)/shard_map/time_forward/pallas_call | solution.py:768
  186.1 39.4 %space_forward.1 = (bf16[6,208,768]{2,1,0:T(8,128)(2,1)}, bf16[6,208,768]{2,1,0:T(8,128)(2,1)}, f32[6,208,128]{2,1,0:T(8,128)}, bf16[6,208,768]{2,1,0:T(8,128)(2...) custom-call(s32[272]{0:T(512)} %multiply_add_fusion.3.slots.s, ...), custom_call_target="tpu_custom_call" | custom-call | flops 44166021120 | bytes 9437184 | tf_op jit(solution)/shard_map/space_forward/pallas_call | solution.py:768
  230.3 34.4 %mlp_backward.1 = (f32[6,208,768]{2,1,0:T(8,128)}, bf16[2,768,768]{2,1,0:T(8,128)(2,1)}, bf16[2,768,768]{2,1,0:T(8,128)(2,1)}, f32[8,768]{1,0:T(8,128)}, f32[8,768]{1,0:T(8,128)}) custom-call(s32[272]{0:T(512)} %multiply_add_fusion.3.slots.s, f32[6]{0:T(128)} %dynamic_slice.43.fw, s32[1]{0:T(128)} %bitcast.2.m.member, bf16[288,48,768]{2,1,0:T(8,128)(2,1)} %bitcast.90, ...), custom_call_target="tpu_custom_call" | custom-call | flops 38277218304 | bytes 9437184 | tf_op jit(solution)/shard_map/mlp_backward/pallas_call | solution.py:768
  266.1 41.9 %space_backward.1 = (bf16[6,208,768]{2,1,0:T(8,128)(2,1)}, bf16[4,192,768]{2,1,0:T(8,128)(2,1)}, bf16[4,192,768]{2,1,0:T(8,128)(2,1)}, f32[8,768]{1,0:T(8,128)}) custom-call(s32[272]{0:T(512)} %multiply_add_fusion.3.slots.s, bf16[288,48,768]{2,1,0:T(8,128)(2,1)} %bitcast.91, f32[6,208,768]{2,1,0:T(8,128)} %get-tuple-element.68.dx2, ...), custom_call_target="tpu_custom_call" | custom-call | flops 47110422528 | bytes 9437184 | tf_op jit(solution)/shard_map/space_backward/pallas_call | solution.py:768
  308.9 1.6 constant_dynamic-slice_fusion
  313.6 5.5 %collective-permute-done.1 = bf16[2,768,768]{2,1,0:T(8,128)(2,1)S(1)} collective-permute-done((bf16[2,768,768]{2,1,0:T(8,128)(2,1)}, bf16[2,768,768]{2,1,0:T(8,128)(2,1)S(1)}, u32[]{:S(2)}, u32[]{:S(2)}) %collective-permute-start.1) | collective-permute-done | bytes 2359328 | tf_op jit(solution)/shard_map/ppermute | solution.py:583
  319.2 22.1 %collective-permute-done.2.far = bf16[6,112,768]{2,1,0:T(8,128)(2,1)S(1)} collective-permute-done((bf16[6,112,768]{2,1,0:T(8,128)(2,1)S(1)}, bf16[6,112,768]{2,1,0:T(8,128)(2,1)S(1)}, u32[]{:S(2)}, u32[]{:S(2)}) %collective-permute-start.2) | collective-permute-done | bytes 1032224 | tf_op jit(solution)/shard_map/ppermute | solution.py:583
  342.2 49.5 %time_backward.1 = (bf16[5,192,768]{2,1,0:T(8,128)(2,1)}, bf16[5,192,768]{2,1,0:T(8,128)(2,1)}, f32[8,768]{1,0:T(8,128)}, f32[112,768]{1,0:T(8,128)}, f32[12,768]{1,0:T(8,128)}) custom-call(s32[272]{0:T(512)} %multiply_add_fusion.3.slots.s, s32[1]{0:T(128)} %bitcast.2.m.member, bf16[288,48,768]{2,1,0:T(8,128)(2,1)} %bitcast.92, ...), custom_call_target="tpu_custom_call" | custom-call | flops 52999225344 | bytes 9437184 | tf_op jit(solution)/shard_map/time_backward/pallas_call | solution.py:768
  391.9 1.8 gather_fusion
  403.0 2.0 collective-permute-start.5
  406.3 21.5 %collective-permute-done.5.refs_7_ = bf16[8,16,768]{2,1,0:T(8,128)(2,1)S(1)} collective-permute-done((bf16[8,16,768]{2,1,0:T(8,128)(2,1)S(1)}, bf16[8,16,768]{2,1,0:T(8,128)(2,1)S(1)}, u32[]{:S(2)}, u32[]{:S(2)}) %collective-permute-start.5) | collective-permute-done | bytes 196640 | tf_op jit(solution)/shard_map/ppermute | solution.py:583
  429.1 7.1 %pack.1 = (bf16[4,448,768]{2,1,0:T(8,128)(2,1)}, bf16[4,448,768]{2,1,0:T(8,128)(2,1)}) custom-call(s32[68]{0:T(128)} %fusion.35.dests, s32[1]{0:T(128)} %bitcast.1.core, bf16[20,48,768]{2,1,0:T(8,128)(2,1)} %bitcast.79, bf16[16,48,768]{2,1,0:T(8,128)(2,1)} %bitcast.81, bf16[32,48,768]{2,1,0:T(8,128)(2,1)} %bitcast.77, bf16[8,16,768]{2,1,0:T(8,128)(2,1)} %pad.79.refs_3_, ...), custom_call_target="tpu_custom_call" | custom-call | tf_op jit(solution)/shard_map/pack/pallas_call | solution.py:974
  436.2 5.3 collective-permute-done.6
  441.5 1.5 copy-done.9
  443.1 3.1 convert_add_fusion.1
  446.2 1.5 copy-done.1
  448.7 1.4 collective-permute-start.7
  451.6 14.7 %collective-permute-done.7 = bf16[2,448,384]{2,1,0:T(8,128)(2,1)S(1)} collective-permute-done((bf16[2,448,384]{2,1,0:T(8,128)(2,1)}, bf16[2,448,384]{2,1,0:T(8,128)(2,1)S(1)}, u32[]{:S(2)}, u32[]{:S(2)}) %collective-permute-start.7) | collective-permute-done | bytes 688160 | tf_op jit(solution)/shard_map/ppermute | solution.py:583
  466.3 1.5 bitcast_add_fusion.1
  467.9 1.5 collective-permute-start.8
  472.0 5.4 %collective-permute-done.8 = bf16[448,384]{1,0:T(8,128)(2,1)S(1)} collective-permute-done((bf16[448,384]{1,0:T(8,128)(2,1)S(1)}, bf16[448,384]{1,0:T(8,128)(2,1)S(1)}, u32[]{:S(2)}, u32[]{:S(2)}) %collective-permute-start.8) | collective-permute-done | bytes 344096 | tf_op jit(solution)/shard_map/ppermute | solution.py:583
  478.5 1.5 collective-permute-done.10
  482.8 13.2 %all-gather = f32[32,768]{1,0:T(8,128)S(1)} all-gather(f32[8,768]{1,0:T(8,128)S(1)} %select_maximum_fusion), channel_id=2, replica_groups=mesh['dp'=8,'mlp'=4] {'mlp'}, dimensions={0}, use_global_device_ids=true | all-gather | bytes 122880 | tf_op jit(solution)/shard_map/all_gather | solution.py:1002
  496.1 9.9 %all-gather.1 = f32[40,8,768]{2,1,0:T(8,128)S(1)} all-gather(f32[5,8,768]{2,1,0:T(8,128)S(1)} %pad_maximum_fusion.5), channel_id=3, replica_groups=mesh['dp'=8,'mlp'=4] {'dp'}, dimensions={0}, use_global_device_ids=true | all-gather | bytes 1105920 | tf_op jit(solution)/shard_map/all_gather | solution.py:1004
  508.2 1.9 multiply_reduce_fusion.1
  512.2 3.3 multiply_subtract_fusion.2
  515.5 2.8 multiply_subtract_fusion
  518.7 2.5 multiply_subtract_fusion.1
  (162 shorter events, 44.6 us)
Async XLA Ops:
  7.2 19.3 %copy-start.29 = (s32[1,12]{1,0:T(1,128)S(1)}, s32[1,12]{1,0:T(1,128)}, u32[]{:S(2)}) copy-start(s32[1,12]{1,0:T(1,128)} %param.18) | copy-start | bytes 148
  7.2 142.8 %all-gather.4.cloned.1.call-start = ((), (), s32[]{:S(2)}) async-start(), calls=%async_computation | async-start | bytes 21897216 | tf_op jit(solution)/shard_map/all_gather | solution.py:668
  28.5 4.3 copy-start.8
  33.5 4.9 copy-start.20
  33.5 5.7 %copy-start.23 = (s32[1,12]{1,0:T(1,128)S(1)}, s32[1,12]{1,0:T(1,128)}, u32[]{:S(2)}) copy-start(s32[1,12]{1,0:T(1,128)} %param.19) | copy-start | bytes 148
  186.1 40.4 %copy-start.3 = (f32[768,400]{0,1:T(8,128)S(1)}, f32[768,400]{0,1:T(8,128)}, u32[]{:S(2)}) copy-start(f32[768,400]{0,1:T(8,128)} %param.29) | copy-start | bytes 3686404
  225.5 4.1 collective-permute-start
  264.7 54.4 %collective-permute-start.1 = (bf16[2,768,768]{2,1,0:T(8,128)(2,1)}, bf16[2,768,768]{2,1,0:T(8,128)(2,1)S(1)}, u32[]{:S(2)}, u32[]{:S(2)}) collective-permute-start(bf16[2,768,768]{2,1,0:T(8,128)(2,1)} %get-tuple-element.77), channel_id=1, source_target_pairs={{0,1},{1,0},{2,3},{3,2},{4,5},{5,4},{6,7},{7,6},{8,9},{9,8},{10,11... | collective-permute-start | bytes 7077896 | tf_op jit(solution)/shard_map/ppermute | solution.py:583
  311.6 29.7 %collective-permute-start.2 = (bf16[6,112,768]{2,1,0:T(8,128)(2,1)S(1)}, bf16[6,112,768]{2,1,0:T(8,128)(2,1)S(1)}, u32[]{:S(2)}, u32[]{:S(2)}) collective-permute-start(bf16[6,112,768]{2,1,0:T(8,128)(2,1)S(1)} %get-tuple-element.122), channel_id=1, source_target_pairs={{0,1},{1,0},{2,3},{3,2},{4,5},{5,4},{6,7},{7,6},{8,9},{9,8},{10,11... | collective-permute-start | bytes 3096584 | tf_op jit(solution)/shard_map/ppermute | solution.py:583
  312.3 79.4 %collective-permute-start.3 = (bf16[4,192,768]{2,1,0:T(8,128)(2,1)S(1)}, bf16[4,192,768]{2,1,0:T(8,128)(2,1)S(1)}, u32[]{:S(2)}, u32[]{:S(2)}) collective-permute-start(bf16[4,192,768]{2,1,0:T(8,128)(2,1)S(1)} %copy-done.26), channel_id=1, source_target_pairs={{0,1},{1,0},{2,3},{3,2},{4,5},{5,4},{6,7},{7,6},{8,9},{9,8},{10,11... | collective-permute-start | bytes 3538952 | tf_op jit(solution)/shard_map/ppermute | solution.py:583
  319.2 72.6 %copy-start.10 = (bf16[2,768,768]{2,1,0:T(8,128)(2,1)}, bf16[2,768,768]{2,1,0:T(8,128)(2,1)S(1)}, u32[]{:S(2)}) copy-start(bf16[2,768,768]{2,1,0:T(8,128)(2,1)S(1)} %collective-permute-done.1) | copy-start | bytes 7077892
  342.2 49.7 %copy-start = (s32[272]{0:T(512)S(1)}, s32[272]{0:T(512)}, u32[]{:S(2)}) copy-start(s32[272]{0:T(512)} %multiply_add_fusion.3.slots.s) | copy-start | bytes 3268
  391.7 9.4 %copy-start.16 = (bf16[4,192,768]{2,1,0:T(8,128)(2,1)}, bf16[4,192,768]{2,1,0:T(8,128)(2,1)S(1)}, u32[]{:S(2)}) copy-start(bf16[4,192,768]{2,1,0:T(8,128)(2,1)S(1)} %collective-permute-done.3) | copy-start | bytes 3538948
  391.7 8.0 %copy-start.18 = (f32[12,768]{1,0:T(8,128)S(1)}, f32[12,768]{1,0:T(8,128)}, u32[]{:S(2)}) copy-start(f32[12,768]{1,0:T(8,128)} %get-tuple-element.89) | copy-start | bytes 110596
  391.7 8.0 %copy-start.24 = (s32[1,12]{1,0:T(1,128)S(1)}, s32[1,12]{1,0:T(1,128)}, u32[]{:S(2)}) copy-start(s32[1,12]{1,0:T(1,128)} %param.19) | copy-start | bytes 148
  391.8 36.0 %collective-permute-start.4 = (bf16[5,192,768]{2,1,0:T(8,128)(2,1)}, bf16[5,192,768]{2,1,0:T(8,128)(2,1)S(1)}, u32[]{:S(2)}, u32[]{:S(2)}) collective-permute-start(bf16[5,192,768]{2,1,0:T(8,128)(2,1)} %get-tuple-element.96), channel_id=1, source_target_pairs={{0,1},{1,0},{2,3},{3,2},{4,5},{5,4},{6,7},{7,6},{8,9},{9,8},{10,11... | collective-permute-start | bytes 4423688 | tf_op jit(solution)/shard_map/ppermute | solution.py:583
  400.0 5.0 copy-start.25
  403.0 24.8 %collective-permute-start.5 = (bf16[8,16,768]{2,1,0:T(8,128)(2,1)S(1)}, bf16[8,16,768]{2,1,0:T(8,128)(2,1)S(1)}, u32[]{:S(2)}, u32[]{:S(2)}) collective-permute-start(bf16[8,16,768]{2,1,0:T(8,128)(2,1)S(1)} %pad.80), channel_id=1, source_target_pairs={{0,1},{1,0},{2,3},{3,2},{4,5},{5,4},{6,7},{7,6},{8,9},{9,8},{10,11... | collective-permute-start | bytes 589832 | tf_op jit(solution)/shard_map/ppermute | solution.py:583
  436.2 5.4 %collective-permute-start.6 = (bf16[4,448,768]{2,1,0:T(8,128)(2,1)}, bf16[4,448,768]{2,1,0:T(8,128)(2,1)S(1)}, u32[]{:S(2)}, u32[]{:S(2)}) collective-permute-start(bf16[4,448,768]{2,1,0:T(8,128)(2,1)} %get-tuple-element.100), channel_id=1, source_target_pairs={{0,4},{4,0},{8,12},{12,8},{16,20},{20,16},{24,28},{28,24},{1,5},{5... | collective-permute-start | bytes 8257544 | tf_op jit(solution)/shard_map/ppermute | solution.py:583
  448.7 17.7 %collective-permute-start.7 = (bf16[2,448,384]{2,1,0:T(8,128)(2,1)}, bf16[2,448,384]{2,1,0:T(8,128)(2,1)S(1)}, u32[]{:S(2)}, u32[]{:S(2)}) collective-permute-start(bf16[2,448,384]{2,1,0:T(8,128)(2,1)} %fusion.4), channel_id=1, source_target_pairs={{0,8},{4,12},{8,0},{12,4},{16,24},{20,28},{24,16},{28,20},{1,9},{5... | collective-permute-start | bytes 2064392 | tf_op jit(solution)/shard_map/ppermute | solution.py:583
  451.0 18.4 %collective-permute-start.9 = (bf16[2,448,384]{2,1,0:T(8,128)(2,1)}, bf16[2,448,384]{2,1,0:T(8,128)(2,1)}, u32[]{:S(2)}, u32[]{:S(2)}) collective-permute-start(bf16[2,448,384]{2,1,0:T(8,128)(2,1)} %fusion.5), channel_id=1, source_target_pairs={{0,16},{4,20},{8,24},{12,28},{16,0},{20,4},{24,8},{28,12},{1,17},{... | collective-permute-start | bytes 2064392 | tf_op jit(solution)/shard_map/ppermute | solution.py:583
  467.9 2.9 copy-start.5
  467.9 9.4 %collective-permute-start.8 = (bf16[448,384]{1,0:T(8,128)(2,1)S(1)}, bf16[448,384]{1,0:T(8,128)(2,1)S(1)}, u32[]{:S(2)}, u32[]{:S(2)}) collective-permute-start(bf16[448,384]{1,0:T(8,128)(2,1)S(1)} %fusion.7), channel_id=1, source_target_pairs={{0,16},{4,20},{8,24},{12,28},{16,0},{20,4},{24,8},{28,12},{1,17},{... | collective-permute-start | bytes 1032200 | tf_op jit(solution)/shard_map/ppermute | solution.py:583
  470.8 9.3 %collective-permute-start.10 = (bf16[448,384]{1,0:T(8,128)(2,1)S(1)}, bf16[448,384]{1,0:T(8,128)(2,1)}, u32[]{:S(2)}, u32[]{:S(2)}) collective-permute-start(bf16[448,384]{1,0:T(8,128)(2,1)S(1)} %fusion.8), channel_id=1, source_target_pairs={{0,8},{4,12},{8,0},{12,4},{16,24},{20,28},{24,16},{28,20},{1,9},{5... | collective-permute-start | bytes 1032200 | tf_op jit(solution)/shard_map/ppermute | solution.py:583
  471.9 8.2 %copy-start.7 = (f32[2,448,384]{2,1,0:T(8,128)S(1)}, f32[2,448,384]{2,1,0:T(8,128)}, u32[]{:S(2)}) copy-start(f32[2,448,384]{2,1,0:T(8,128)} %copy-done.6) | copy-start | bytes 4128772
  481.1 14.9 %copy-start.19 = (f32[8,768]{1,0:T(8,128)S(1)}, f32[8,768]{1,0:T(8,128)}, u32[]{:S(2)}) copy-start(f32[8,768]{1,0:T(8,128)} %get-tuple-element.101) | copy-start | bytes 73732
  512.2 3.3 copy-start.2
  512.2 3.3 copy-start.12
  512.2 3.3 copy-start.13
  515.5 2.8 copy-start.4
  515.5 2.8 copy-start.14
  515.5 3.1 copy-start.15
  (10 other events, 13.6 us)
Sparse Core Ops, SparseCore 0:
  11.4 138.5 all-gather.3

commit v3 on v2

--- a/solution.py
+++ b/solution.py
@@ -100,36 +100,58 @@
     pltpu.make_async_copy(target, target, sem).wait()
 
 
-def attend(load, store, extra_q, extra_k):
+def jobs_of(count):
+    pairs = [slice(p * PAIR, (p + 1) * PAIR) for p in range(HEADS // 2)]
+    return [(i, lanes) for i in range(count) for lanes in pairs]
+
+
+def in_flight(jobs, begin, finish):
+    waiting = None
+    for job in jobs:
+        started = begin(*job)
+        if waiting is not None:
+            finish(*waiting)
+        waiting = job + started
+    finish(*waiting)
+
+
+def attend(count, load, store, extra_q, extra_k):
     low, high = low_lanes()
-    for pair in range(HEADS // 2):
-        lanes = slice(pair * PAIR, (pair + 1) * PAIR)
-        queries, keys, values = load(lanes)
+
+    def begin(i, lanes):
+        queries, keys, values = load(i, lanes)
         both = jnp.concatenate([queries * low, queries * high], axis=0)
         scores = mm_nt(
             jnp.concatenate([both, extra_q[...]], axis=1),
             jnp.concatenate([keys, extra_k[: keys.shape[0]]], axis=1),
         )
+        return values, scores
+
+    def finish(i, lanes, values, scores):
         top = jnp.max(scores, axis=-1, keepdims=True)
         weights = jnp.exp(scores - top).astype(bf16)
         summed = mm(weights, jnp.concatenate([values, jnp.ones_like(values)], axis=1))
         merged = pick_half(summed[:, :PAIR]) / pick_half(summed[:, PAIR:])
-        store(lanes, merged.astype(bf16))
-
-
-def attend_back(load, store, extra_q, extra_k):
+        store(i, lanes, merged.astype(bf16))
+
+    in_flight(jobs_of(count), begin, finish)
+
+
+def attend_back(count, load, store, extra_q, extra_k):
     low, high = low_lanes()
-    for pair in range(HEADS // 2):
-        lanes = slice(pair * PAIR, (pair + 1) * PAIR)
-        queries, keys, values, grads = load(lanes)
-        rows = queries.shape[0]
+
+    def begin(i, lanes):
+        queries, keys, values, grads = load(i, lanes)
         both_k = jnp.concatenate([keys * low, keys * high], axis=0)
         both_v = jnp.concatenate([values * low, values * high], axis=0)
         scores = mm_nt(
             jnp.concatenate([both_k, extra_k[...]], axis=1),
-            jnp.concatenate([queries, extra_q[:rows]], axis=1),
+            jnp.concatenate([queries, extra_q[: queries.shape[0]]], axis=1),
         )
-        back = mm_nt(both_v, grads)
+        return queries, both_k, grads, scores, mm_nt(both_v, grads)
+
+    def finish(i, lanes, queries, both_k, grads, scores, back):
+        rows = queries.shape[0]
         soft, inner = [], []
         for half in (slice(0, rows), slice(rows, 2 * rows)):
             part = scores[half]
@@ -141,11 +163,14 @@
         soft = jnp.concatenate(soft, axis=0)
         inner = jnp.concatenate(inner, axis=0)
         store(
+            i,
             lanes,
             (mm_tn(inner, both_k) * HEAD_DIM ** (-0.5)).astype(bf16),
             pick_half(mm(inner, queries)).astype(bf16),
             pick_half(mm(soft, grads)).astype(bf16),
         )
+
+    in_flight(jobs_of(count), begin, finish)
 
 
 def project(hidden, rows, tiles):
@@ -190,8 +215,9 @@
         fetch(slots, gathered, joint, sems.at[1], lambda t: t + 1, True)
         fetch(slots, gathered, out, sems.at[2], lambda t: t + 4, False)
         arrive(embed, sems.at[0])
-        arrive(joint, sems.at[1])
-        arrive(out, sems.at[2])
+
+    def first(target, sem):
+        pl.when(pl.program_id(0) == 0)(lambda: arrive(target, sem))
 
     def work(count):
         cut = (frames, count * GROUP, width)
@@ -203,23 +229,24 @@
         base[: flat[0]] = stream
         rows_now = rows[...]
         unused, hidden = keep_norm(stream, rows_now, 0, hid_ref, hat_ref, rstd_ref, every, cut)
+        first(joint, sems.at[1])
         queries, keys, values = project(hidden, rows_now, joint)
         q_ref[:, here] = queries.reshape(cut)
         k_ref[:, here] = keys.reshape(cut)
         v_ref[:, here] = values.reshape(cut)
-        for g in range(count):
+
+        def load(g, lanes):
             part = slice(g * GROUP, (g + 1) * GROUP)
-
-            def load(lanes):
-                return tuple(
-                    ref[:, part, lanes].reshape(frames * GROUP, PAIR)
-                    for ref in (q_ref, k_ref, v_ref)
-                )
-
-            def store(lanes, merged):
-                o_ref[:, part, lanes] = merged.reshape(frames, GROUP, PAIR)
-
-            attend(load, store, extra_q, extra_k)
+            return tuple(
+                ref[:, part, lanes].reshape(frames * GROUP, PAIR) for ref in (q_ref, k_ref, v_ref)
+            )
+
+        def store(g, lanes, merged):
+            part = slice(g * GROUP, (g + 1) * GROUP)
+            o_ref[:, part, lanes] = merged.reshape(frames, GROUP, PAIR)
+
+        attend(count, load, store, extra_q, extra_k)
+        first(out, sems.at[2])
         merged = o_ref[:, here].reshape(flat)
         stream = base[: flat[0]] + mm(merged, out[...]) + rows_now[4:5]
         x1_ref[:, here] = stream.reshape(cut)
@@ -248,7 +275,6 @@
         fetch(slots, gathered, downs, sems.at[3], lambda t: 2 * t + 10, False)
         pool_ref[...] = jnp.zeros_like(pool_ref)
         arrive(joint, sems.at[0])
-        arrive(out, sems.at[1])
 
     rows_now = rows[...]
     unused, hidden = keep_norm(
@@ -258,15 +284,15 @@
     q_ref[...] = queries.reshape(cut)
     k_ref[...] = keys.reshape(cut)
     v_ref[...] = values.reshape(cut)
-    for f in range(span):
-
-        def load(lanes):
-            return q_ref[f, :, lanes], k_ref[f, :, lanes], v_ref[f, :, lanes]
-
-        def store(lanes, merged):
-            o_ref[f, :, lanes] = merged
-
-        attend(load, store, extra_q, extra_k)
+
+    def load(f, lanes):
+        return q_ref[f, :, lanes], k_ref[f, :, lanes], v_ref[f, :, lanes]
+
+    def store(f, lanes, merged):
+        o_ref[f, :, lanes] = merged
+
+    attend(span, load, store, extra_q, extra_k)
+    pl.when(step == 0)(lambda: arrive(out, sems.at[1]))
     merged = o_ref[...].reshape(flat)
     stream = x1[...].reshape(flat) + mm(merged, out[...]) + rows_now[4:5]
     low_now = low_rows[...]
@@ -277,16 +303,23 @@
         arrive(ups, sems.at[2])
         arrive(downs, sems.at[3])
 
-    for j in range(members):
-        lanes = slice(j * width, (j + 1) * width)
-        upper = mm(hidden, ups[:, lanes])
+    def begin(j, lanes):
+        return (mm(hidden, ups[:, lanes]),)
+
+    lowered = []
+
+    def finish(j, lanes, upper):
         cubic = gelu_a * gelu_b * (upper * upper)
         gate = 0.5 + 0.5 * jnp.tanh(upper * (gelu_a + cubic))
         active = upper * gate
         slope = gate + active * (1.0 - gate) * (2.0 * gelu_a + 6.0 * cubic)
         gp_ref[j] = slope.astype(bf16).reshape(cut)
         acts[:, lanes] = active.astype(bf16)
-        stream = stream + mm(acts[:, lanes], downs[lanes])
+        lowered.append(mm(acts[:, lanes], downs[lanes]))
+
+    in_flight([(j, slice(j * width, (j + 1) * width)) for j in range(members)], begin, finish)
+    for part in lowered:
+        stream = stream + part
     for i in range(2):
         own = pl.ds(pl.multiple_of((member[0] ^ i) * width, 128), width)
         act_ref[i] = acts[:, own].reshape(cut)
@@ -302,9 +335,9 @@
 
 
 def mlp_backward(
-    slots, frame_weight, member, patches, gathered, pool, pool_other, head, valid, targets, total,
+    slots, frame_weight, member, core, patches, gathered, pool, pool_other, head, valid, targets, total,
     hid2, hat2, rstd2, hat3, rstd3, gp, act, low_rows,
-    dx2_ref, own_ref, other_ref, rows_ref, small_ref,
+    dx2_ref, keep_ref, send_ref, rows_ref, small_ref,
     ups, downs, dus, spread, up_sum, down_sum, row_sums, sems,
 ):
     step = pl.program_id(0)
@@ -372,9 +405,10 @@
 
     @pl.when(step == pl.num_programs(0) - 1)
     def _():
-        for i, ref in enumerate((own_ref, other_ref)):
-            ref[0] = up_sum[i].astype(bf16)
-            ref[1] = down_sum[i].astype(bf16)
+        for ref, half in zip((keep_ref, send_ref), column_halves(core[0], width)):
+            for i in range(2):
+                ref[i, 0] = up_sum[i, :, half].astype(bf16)
+                ref[i, 1] = down_sum[i, :, half].astype(bf16)
         rows_ref[...] = jnp.zeros_like(rows_ref)
         for i in range(5):
             rows_ref[i : i + 1] = jnp.sum(row_sums[i], axis=0, keepdims=True)
@@ -400,19 +434,30 @@
     return jnp.where(row == picked.shape[0] - 16, 1.0, 0.0).astype(bf16)
 
 
+def column_halves(core, width):
+    middle = width // 2
+    keep = pl.ds(pl.multiple_of(core * middle, 128), middle)
+    send = pl.ds(pl.multiple_of((1 - core) * middle, 128), middle)
+    return keep, send
+
+
 def clear(*refs):
     for ref in refs:
         ref[...] = jnp.zeros_like(ref)
 
 
-def finish_attention(tile_refs, at, rows_ref, joint_sum, out_sum, row_sums):
-    share, width = tile_refs[0].shape[1:]
+def finish_attention(core, tile_refs, at, rows_ref, joint_sum, out_sum, row_sums):
+    share = tile_refs[0].shape[2]
+    width = out_sum.shape[1]
     rows_ref[...] = jnp.zeros_like(rows_ref)
-    for n, tile_ref in enumerate(tile_refs):
-        here = slice(n * share, (n + 1) * share)
-        for i in range(3):
-            tile_ref[at + i] = joint_sum[here, i * width : (i + 1) * width].astype(bf16)
-        tile_ref[at + 3] = out_sum[here].astype(bf16)
+    for tile_ref, half in zip(tile_refs, column_halves(core, width)):
+        for n in range(2):
+            here = slice(n * share, (n + 1) * share)
+            for i in range(3):
+                start = pl.multiple_of(i * width + half.start, 128)
+                columns = pl.ds(start, half.size)
+                tile_ref[n, at + i] = joint_sum[here, columns].astype(bf16)
+            tile_ref[n, at + 3] = out_sum[here, half].astype(bf16)
     last = slice(2 * share, 2 * share + 1)
     for i in range(2):
         rows_ref[i : i + 1] = jnp.sum(row_sums[i], axis=0, keepdims=True)
@@ -422,8 +467,8 @@
 
 
 def space_backward(
-    slots, gathered, dx2, hid1, hat1, rstd1, q, k, v, o, rows, picked, extra_q, extra_k,
-    g1_ref, own_ref, other_ref, rows_ref,
+    slots, core, gathered, dx2, hid1, hat1, rstd1, q, k, v, o, rows, picked, extra_q, extra_k,
+    g1_ref, keep_ref, send_ref, rows_ref,
     joint, out, joint_sum, out_sum, row_sums, grads, outer, sems,
 ):
     step = pl.program_id(0)
@@ -437,21 +482,21 @@
         fetch(slots, gathered, joint, sems.at[0], lambda t: t + 5, True)
         clear(joint_sum, out_sum, row_sums)
         arrive(out, sems.at[1])
-        arrive(joint, sems.at[0])
 
     grad_b = dx2[...].reshape(flat).astype(bf16)
     outer[...] = mm_nt(grad_b, out[...]).astype(bf16)
-    for f in range(span):
+
+    def load(f, lanes):
         here = slice(f * count, (f + 1) * count)
-
-        def load(lanes):
-            return q[f, :, lanes], k[f, :, lanes], v[f, :, lanes], outer[here, lanes]
-
-        def store(lanes, *parts):
-            for i, part in enumerate(parts):
-                grads[here, i * width + lanes.start : i * width + lanes.stop] = part
-
-        attend_back(load, store, extra_q, extra_k)
+        return q[f, :, lanes], k[f, :, lanes], v[f, :, lanes], outer[here, lanes]
+
+    def store(f, lanes, *parts):
+        here = slice(f * count, (f + 1) * count)
+        for i, part in enumerate(parts):
+            grads[here, i * width + lanes.start : i * width + lanes.stop] = part
+
+    attend_back(span, load, store, extra_q, extra_k)
+    pl.when(step == 0)(lambda: arrive(joint, sems.at[0]))
     picked_now = picked[...]
     g1_ref[...] = close_attention(
         dx2[...].reshape(flat), grad_b, hid1[...].reshape(flat), hat1[...].reshape(flat),
@@ -461,13 +506,15 @@
 
     @pl.when(step == pl.num_programs(0) - 1)
     def _():
-        finish_attention((own_ref, other_ref), 0, rows_ref, joint_sum, out_sum, row_sums)
+        finish_attention(
+            core[0], (keep_ref, send_ref), 0, rows_ref, joint_sum, out_sum, row_sums
+        )
 
 
 def time_backward(
-    rest, slots, member, gathered, near, far, hid0, hat0, rstd0, q, k, v, o, pixels, rows, picked,
+    rest, slots, member, core, gathered, near, far, hid0, hat0, rstd0, q, k, v, o, pixels, rows, picked,
     extra_q, extra_k,
-    own_ref, other_ref, rows_ref, pos_ref, frame_ref,
+    keep_ref, send_ref, rows_ref, pos_ref, frame_ref,
     joint, out, joint_sum, out_sum, embed_sum, row_sums, grads, outer, sems,
 ):
     step = pl.program_id(0)
@@ -479,7 +526,6 @@
         fetch(slots, gathered, joint, sems.at[0], lambda t: t + 1, True)
         clear(joint_sum, out_sum, embed_sum, row_sums, frame_ref)
         arrive(out, sems.at[1])
-        arrive(joint, sems.at[0])
 
     def work(groups):
         cut = (frames, groups * GROUP, width)
@@ -492,21 +538,21 @@
             [jnp.where(first, near_now, far_now), jnp.where(first, far_now, near_now)]
         ).reshape(flat)
         outer[:, here] = mm_nt(grad_b, out[...]).astype(bf16).reshape(cut)
-        for g in range(groups):
+
+        def load(g, lanes):
             part = slice(g * GROUP, (g + 1) * GROUP)
-
-            def load(lanes):
-                return tuple(
-                    ref[:, part, lanes].reshape(frames * GROUP, PAIR)
-                    for ref in (q, k, v, outer)
-                )
-
-            def store(lanes, *parts):
-                for i, value in enumerate(parts):
-                    span_now = slice(i * width + lanes.start, i * width + lanes.stop)
-                    grads[:, part, span_now] = value.reshape(small)
-
-            attend_back(load, store, extra_q, extra_k)
+            return tuple(
+                ref[:, part, lanes].reshape(frames * GROUP, PAIR) for ref in (q, k, v, outer)
+            )
+
+        def store(g, lanes, *parts):
+            part = slice(g * GROUP, (g + 1) * GROUP)
+            for i, value in enumerate(parts):
+                span_now = slice(i * width + lanes.start, i * width + lanes.stop)
+                grads[:, part, span_now] = value.reshape(small)
+
+        attend_back(groups, load, store, extra_q, extra_k)
+        pl.when(step == 0)(lambda: arrive(joint, sems.at[0]))
         picked_now = picked[...]
         grad = close_attention(
             grad_b.astype(f32), grad_b, hid0[:, here].reshape(flat),
@@ -534,36 +580,48 @@
 
     @pl.when(last)
     def _():
-        finish_attention((own_ref, other_ref), 1, rows_ref, joint_sum, out_sum, row_sums)
-        share = own_ref.shape[1]
-        own_ref[0] = embed_sum[:share].astype(bf16)
-        other_ref[0] = embed_sum[share : 2 * share].astype(bf16)
-
-
-def pack(dests, core, *refs):
-    count = (len(refs) - 3) // 3
-    owns, others, sums = refs[:count], refs[count : 2 * count], refs[-1 - count : -1]
-    keep_ref, send_ref, sems = refs[2 * count], refs[2 * count + 1], refs[-1]
+        finish_attention(
+            core[0], (keep_ref, send_ref), 1, rows_ref, joint_sum, out_sum, row_sums
+        )
+        share = keep_ref.shape[2]
+        for ref, half in zip((keep_ref, send_ref), column_halves(core[0], width)):
+            for n in range(2):
+                ref[n, 0] = embed_sum[n * share : (n + 1) * share, half].astype(bf16)
+
+
+def pack(bits, dests, place, *refs):
+    count = (len(refs) - 5) // 4
+    keeps, mets, fars = (refs[i * count : (i + 1) * count] for i in range(3))
+    (stay_a, go_a, stay_b, go_b), sems = refs[3 * count : 3 * count + 4], refs[-1]
+    sums = refs[-1 - count : -1]
     table_rows = sums[-1].shape[1]
-    slots = (keep_ref.shape[1] - table_rows) // BR
-
-    def route(source, chunk, place, sem):
-        mine = chunk % 2 == core[0]
-
-        @pl.when(mine)
-        def _():
-            pltpu.make_async_copy(source, keep_ref.at[chunk // 2, place], sem).start()
-
-        @pl.when(jnp.logical_not(mine))
-        def _():
-            pltpu.make_async_copy(source, send_ref.at[chunk // 2, place], sem).start()
+    slots = (stay_a.shape[1] - table_rows) // BR
+    top = bits - 1
+    rest = 2 ** (bits - 2) - 1
+
+    def route(source, chunk, rows, sem):
+        differs = chunk ^ place[0]
+        in_b = chunk % 2 == 1
+        index_a, index_b = chunk >> 2, (chunk >> 1) & rest
+        moves_a, moves_b = (differs >> 1) % 2 == 1, (differs >> top) % 2 == 1
+        for flag, target, index in (
+            (~in_b & ~moves_a, stay_a, index_a),
+            (~in_b & moves_a, go_a, index_a),
+            (in_b & ~moves_b, stay_b, index_b),
+            (in_b & moves_b, go_b, index_b),
+        ):
+
+            @pl.when(flag)
+            def _(target=target, index=index):
+                pltpu.make_async_copy(source, target.at[index, rows], sem).start()
 
     first = 0
-    for n, (own, other, source) in enumerate(zip(owns, others, sums)):
+    for n, (keep, met, far, source) in enumerate(zip(keeps, mets, fars, sums)):
         table = n == count - 1
 
-        def one(i, carry, own=own, other=other, source=source, first=first, n=n, table=table):
-            source[i] = (own[i].astype(f32) + other[i].astype(f32)).astype(bf16)
+        def one(i, carry, keep=keep, met=met, far=far, source=source, first=first, n=n, table=table):
+            total = keep[i].astype(f32) + met[i].astype(f32) + far[i].astype(f32)
+            source[i] = total.astype(bf16)
             if table:
                 route(source.at[i], i, pl.ds(slots * BR, table_rows), sems.at[n])
             else:
@@ -583,37 +641,47 @@
     return lax.ppermute(value, axis, [(i, i ^ hop) for i in range(size)])
 
 
-def halve(kept, sent, axis):
+def added(*parts):
+    total = parts[0].astype(f32)
+    for part in parts[1:]:
+        total = total + part.astype(f32)
+    return total
+
+
+def halve(stay_a, go_a, stay_b, go_b, axis):
+    bits = lax.axis_size(axis).bit_length() - 1
+    place = lax.axis_index(axis)
+    orders = [list(range(1, bits)), list(range(bits - 1, 0, -1))]
+    shape = (2,) * (bits - 2) + stay_a.shape[1:]
+    going, staying = [go_a, go_b], [stay_a, stay_b]
+    for stage in range(bits - 1):
+        met = [swap(value, axis, 1 << order[stage]) for value, order in zip(going, orders)]
+        values = [added(stay, come) for stay, come in zip(staying, met)]
+        if stage == bits - 2:
+            return values
+        going, staying = [], []
+        for value, order in zip(values, orders):
+            alive = sorted(order[stage + 1 :], reverse=True)
+            value = value.reshape(shape[stage:])
+            at = alive.index(order[stage + 1])
+            bit = (place >> order[stage + 1]) & 1
+            going.append(lax.dynamic_index_in_dim(value, 1 - bit, at, False).astype(bf16))
+            staying.append(lax.dynamic_index_in_dim(value, bit, at, False))
+
+
+def spread_four(value, axis):
     size = lax.axis_size(axis)
     place = lax.axis_index(axis)
-    bits = size.bit_length() - 1
-    rows, width = kept.shape[1:]
-    middle = (width // 256) * 128
-    met = swap(sent, axis, 1)
-    cut = (2,) * (bits - 1) + (rows, width)
-    kept, met = kept.reshape(cut), met.reshape(cut)
-    ascending = list(range(1, bits))
-    parts = [
-        [kept[..., :middle], met[..., :middle], ascending],
-        [kept[..., middle:], met[..., middle:], ascending[::-1]],
-    ]
-    parts = [(left.astype(f32) + right.astype(f32), order) for left, right, order in parts]
-    for stage in range(bits - 1):
-        outgoing, staying = [], []
-        for value, order in parts:
-            alive = sorted(order[stage:], reverse=True)
-            at = alive.index(order[stage])
-            bit = (place >> order[stage]) & 1
-            outgoing.append(lax.dynamic_index_in_dim(value, 1 - bit, at, False).astype(bf16))
-            staying.append(lax.dynamic_index_in_dim(value, bit, at, False))
-        arrived = [
-            swap(value, axis, 1 << order[stage]) for value, (unused, order) in zip(outgoing, parts)
-        ]
-        parts = [
-            (stay + come.astype(f32), order)
-            for stay, come, (unused, order) in zip(staying, arrived, parts)
-        ]
-    return jnp.concatenate([parts[0][0], parts[1][0]], axis=-1)
+    value = value[None]
+    hop = 1
+    while hop < size:
+        come = swap(value, axis, hop)
+        low = (place & hop) == 0
+        value = jnp.concatenate(
+            [jnp.where(low, value, come), jnp.where(low, come, value)], axis=0
+        )
+        hop *= 2
+    return value
 
 
 def block_ranks(owners):
@@ -706,6 +774,8 @@
     pix, label_total = lax.optimization_barrier((pix, label_total))
     share = width // mlp_count
     half = member % 2
+    place = lax.axis_index("dp").astype(jnp.int32)
+    core_s = (place % 2)[None]
     pick_row = jnp.arange(2 * share)
     pick_member = jnp.where(pick_row < share, member, member ^ 1)
     pick_row = pick_row % share
@@ -743,8 +813,8 @@
         ending = jnp.where(m[0] % 2 == 0, 2 * half_blocks, 2 * half_blocks - 1)
         return jnp.where(s < half_blocks, (m[0] % 2) * half_blocks + s, ending)
 
-    back_spec = pl.BlockSpec((frames, group_rows, width), lambda s, i, m: (0, half_index(s, m), 0))
-    back_thin = pl.BlockSpec((frames, group_rows, 128), lambda s, i, m: (0, half_index(s, m), 0))
+    back_spec = pl.BlockSpec((frames, group_rows, width), lambda s, i, m, c: (0, half_index(s, m), 0))
+    back_thin = pl.BlockSpec((frames, group_rows, 128), lambda s, i, m, c: (0, half_index(s, m), 0))
     near_spec = pl.BlockSpec((half_frames, group_rows, width), lambda s, *_: (0, s, 0))
     my_frame_spec = pl.BlockSpec(
         (FRAMES_AT_ONCE, padded, width),
@@ -828,12 +898,13 @@
     valid_p = jnp.pad(valid_f, ((0, 0), (0, class_pad - classes)))
     targets_p = jnp.pad(targets, ((0, 0), (0, class_pad - classes)))
     pool_other = swap(pool, "mlp", 1)
-    squares16 = jax.ShapeDtypeStruct((2, width, width), bf16)
-    dx2, own_mlp, other_mlp, rows_low, small = call(
-        lambda s, fw, m, *refs: mlp_backward(s, fw, m, patches, *refs),
+    middle = width // 2
+    squares16 = jax.ShapeDtypeStruct((2, 2, width, middle), bf16)
+    dx2, keep_mlp, send_mlp, rows_low, small = call(
+        lambda s, fw, m, c, *refs: mlp_backward(s, fw, m, c, patches, *refs),
         "mlp_backward",
         13,
-        [slot_index, frame_weight, member_s],
+        [slot_index, frame_weight, member_s, core_s],
         space_grid,
         [
             pool, pool_other, head_b, valid_p, targets_p, label_total[None],
@@ -846,7 +917,7 @@
             rows_spec,
         ],
         [half32, squares16, squares16, row32, row32],
-        [frame_spec, whole(2, width, width), whole(2, width, width), rows_spec, rows_spec],
+        [frame_spec] + [whole(2, 2, width, middle)] * 2 + [rows_spec, rows_spec],
         tile_bufs((1, mlp_count), (mlp_count, 1))
         + [
             pltpu.VMEM((frame_rows, mlp_count * width), bf16),
@@ -862,20 +933,20 @@
         pltpu.VMEM((2 * share + 16, 3 * width), f32),
         pltpu.VMEM((2 * share + 16, width), f32),
     ]
-    met_mlp = swap(other_mlp, "mlp", 1)
-    g1, own_space, other_space, rows_space = call(
+    met_mlp = swap(send_mlp, "dp", 1)
+    g1, keep_space, send_space, rows_space = call(
         space_backward,
         "space_backward",
         16,
-        [slot_index],
+        [slot_index, core_s],
         space_grid,
         [dx2, hid1, hat1, rstd1, q_s, k_s, v_s, o_s, space_rows, picked, space_q, space_k],
         [frame_spec] * 3
         + [frame_thin]
         + [frame_spec] * 4
         + [rows_spec, pick_spec, space_extra, space_extra],
-        [half16] + [jax.ShapeDtypeStruct((4, share, width), bf16)] * 2 + [row32],
-        [frame_spec] + [whole(4, share, width)] * 2 + [rows_spec],
+        [half16] + [jax.ShapeDtypeStruct((2, 4, share, middle), bf16)] * 2 + [row32],
+        [frame_spec] + [whole(2, 4, share, middle)] * 2 + [rows_spec],
         tile_bufs((1, 3), (1, 1))
         + sums
         + [
@@ -894,13 +965,17 @@
 
     far = swap(patches_of(1 - half), "mlp", 1)
     near = patches_of(half)
-    near, met_mlp = lax.optimization_barrier((near, met_mlp))
-    met_space = swap(other_space, "mlp", 1)
-    own_time, other_time, rows_time, grad_pos, grad_frames = call(
+    met_space = swap(send_space, "dp", 1)
+    chip_mlp = added(keep_mlp[1], met_mlp[1]).astype(bf16)
+    chip_space = added(keep_space[1], met_space[1]).astype(bf16)
+    far, chip_mlp, chip_space = lax.optimization_barrier((far, chip_mlp, chip_space))
+    far_mlp = swap(chip_mlp, "mlp", 1)
+    far_space = swap(chip_space, "mlp", 1)
+    keep_time, send_time, rows_time, grad_pos, grad_frames = call(
         partial(time_backward, rest),
         "time_backward",
         18,
-        [slot_index, member_s],
+        [slot_index, member_s, core_s],
         back_grid,
         [near, far, hid0, hat0, rstd0, q_t, k_t, v_t, o_t, pix, time_rows, picked, time_q, time_k],
         [near_spec] * 2
@@ -908,13 +983,13 @@
         + [back_thin]
         + [back_spec] * 5
         + [rows_spec, pick_spec, time_extra, time_extra],
-        [jax.ShapeDtypeStruct((5, share, width), bf16)] * 2
+        [jax.ShapeDtypeStruct((2, 5, share, middle), bf16)] * 2
         + [
             row32,
             jax.ShapeDtypeStruct((half_rows, width), f32),
             jax.ShapeDtypeStruct((frames, width), f32),
         ],
-        [whole(5, share, width)] * 2 + [rows_spec, patch_spec, whole(frames, width)],
+        [whole(2, 5, share, middle)] * 2 + [rows_spec, patch_spec, whole(frames, width)],
         tile_bufs((1, 3), (1, 1))
         + sums
         + [
@@ -927,8 +1002,10 @@
     )
 
     grad_time = jnp.einsum("ft,fd->td", time_hot, grad_frames, precision=highest)
-    other_time, met_space = lax.optimization_barrier((other_time, met_space))
-    met_time = swap(other_time, "mlp", 1)
+    send_time, far_mlp, far_space = lax.optimization_barrier((send_time, far_mlp, far_space))
+    met_time = swap(send_time, "dp", 1)
+    chip_time = added(keep_time[1], met_time[1]).astype(bf16)
+    far_time = swap(chip_time, "mlp", 1)
     main = half_blocks * group_rows
     all_pos = jnp.concatenate(
         [jnp.where(half == i, grad_pos[:main], 0.0) for i in range(2)] + [grad_pos[main:]]
@@ -953,13 +1030,23 @@
         rows_now = lax.dynamic_index_in_dim(table_part, which, 1, False).astype(bf16)
         return jnp.pad(rows_now, ((0, 0), (0, 16 - rows_each), (0, 0)))
 
-    met_table = swap(table_of(member ^ 1), "mlp", 1)
+    table_pair = jnp.stack([table_of(member), table_of(member ^ 1)])
+    columns = jnp.stack([table_pair[..., :middle], table_pair[..., middle:]])
+    keep_table = lax.dynamic_index_in_dim(columns, place % 2, 0, False)
+    met_table = swap(lax.dynamic_index_in_dim(columns, 1 - place % 2, 0, False), "dp", 1)
+    far_table = swap(added(keep_table[1], met_table[1]).astype(bf16), "mlp", 1)
 
     def blocks_of(*parts):
-        return [part.reshape(-1, BR, width) for part in parts]
-
-    sources = blocks_of(own_time, own_space, own_mlp) + [table_of(member)]
-    sources = sources + blocks_of(met_time, met_space, met_mlp) + [met_table]
+        return [part.reshape(-1, BR, middle) for part in parts]
+
+    sources = (
+        blocks_of(keep_time[0], keep_space[0], keep_mlp[0])
+        + [keep_table[0]]
+        + blocks_of(met_time[0], met_space[0], met_mlp[0])
+        + [met_table[0]]
+        + blocks_of(far_time, far_space, far_mlp)
+        + [far_table]
+    )
     shared_here = shared_blocks // mlp_count
     here_ids = jnp.arange(shared_here + 2 * per_tile)
     block_of = jnp.where(
@@ -969,23 +1056,27 @@
     )
     here_slots = slot_index[block_of]
     dests = (here_slots // (slots * mlp_count)) * slots + here_slots % slots
-    place = lax.axis_index("dp").astype(jnp.int32)
-    chunk = jax.ShapeDtypeStruct((dp_count // 2, slots * BR + 16, width), bf16)
-    kept, sent = pl.pallas_call(
-        pack,
+    bits = dp_count.bit_length() - 1
+    chunk = jax.ShapeDtypeStruct((dp_count // 4, slots * BR + 16, middle), bf16)
+    packed = pl.pallas_call(
+        partial(pack, bits),
         grid_spec=pltpu.PrefetchScalarGridSpec(
             num_scalar_prefetch=2,
             grid=(1,),
-            in_specs=[pl.BlockSpec(memory_space=pltpu.VMEM)] * 8,
-            out_specs=[any_spec] * 2,
+            in_specs=[pl.BlockSpec(memory_space=pltpu.VMEM)] * 12,
+            out_specs=[any_spec] * 4,
             scratch_shapes=[pltpu.VMEM(part.shape, bf16) for part in sources[:4]]
             + [pltpu.SemaphoreType.DMA((4,))],
         ),
-        out_shape=[chunk, chunk],
+        out_shape=[chunk] * 4,
         compiler_params=params,
         name="pack",
-    )(dests, (place % 2)[None], *sources)
-    summed = halve(kept, sent, "dp")
+    )(dests, place[None], *sources)
+    sum_a, sum_b = (value.reshape(value.shape[-2:]) for value in halve(*packed, "dp"))
+    even = place % 2 == 0
+    mine = jnp.where(even, sum_a, sum_b)
+    met = swap(jnp.where(even, sum_b, sum_a), "dp", 1)
+    summed = jnp.concatenate([jnp.where(even, mine, met), jnp.where(even, met, mine)], axis=1)
     my_slots = (place * mlp_count + member) * slots + jnp.arange(slots)
     filled = jnp.any(slot_index[:, None] == my_slots[None, :], axis=0)
     filled = jnp.repeat(filled, BR)[:, None]
@@ -999,7 +1090,7 @@
         ]
     )
     blocks = jnp.concatenate(
-        [lax.all_gather(block[:8], "mlp", axis=0), block[None, 8:]], axis=0
+        [spread_four(block[:8], "mlp"), block[None, 8:]], axis=0
     )
     blocks = lax.all_gather(blocks, "dp", axis=0)
     heads, blocks = blocks[:, mlp_count], blocks[:, :mlp_count]

time: 537 us -> 507 us (0.944)
  blocking collectives: 38.9 us -> 25.6 us
  Pallas kernels: 208 us -> 195 us
  waiting for transfers between devices: 186 us -> 176 us
    all_gather x1 -> x0, blocking collectives: 13.2 us -> none  [local(): lax.all_gather(block[:8], 'mlp', axis=0)]
    pallas_call x5, Pallas kernels: 201 us -> 188 us  [call(): pl.pallas_call(kernel, grid_spec=pltpu.PrefetchScalarGridSpec(num_scalar_...]
    ppermute x11 -> x17, waiting for transfers between devices: 76.7 us -> 66.5 us  [swap(): return lax.ppermute(value, axis, [(i, i ^ hop) for i in range(size)])]
    slice x0 -> x6, local copies, waits for them, and re-layouts: none -> 9.5 us  [the longest x1 2.45 us: local(): keep_mlp[0]]
    add x5 -> x2, other arithmetic: 8.12 us -> 2.54 us  [added(): total = total + part.astype(f32)]
    ppermute x11 -> x17, starting transfers between devices: 9.89 us -> 12.9 us  [swap(): return lax.ppermute(value, axis, [(i, i ^ hop) for i in range(size)])]
  transfers between devices with their start and end apart: 12 -> 18, of which waited for: 9 -> 10; matrix products, arithmetic and copies ran while one was open for 7% -> 9% of each run, Pallas kernels for 17% -> 15%
where the time goes in v3:
time: 507 us; the launch traced here: 500 us
  Pallas kernels  195 us (38%)
  waiting for transfers between devices  176 us (35%)
  other arithmetic  33.9 us (7%)
  local copies, waits for them, and re-layouts  33.8 us (7%)
  blocking collectives  25.6 us (5%)
  between operations  19.1 us (4%)
  starting transfers between devices  13 us (3%)
    pallas_call x5, Pallas kernels, call(): pl.pallas_call(kernel, grid_spec=pltpu.PrefetchScalarGridSpec(num_scalar_...  188 us
    all_gather x1, waiting for transfers between devices, local(): lax.all_gather(slot_weight.astype(bf16), ('dp', 'mlp'), axis=0, tiled=True)  110 us
    ppermute x17, waiting for transfers between devices, swap(): return lax.ppermute(value, axis, [(i, i ^ hop) for i in range(size)])  66.5 us
    psum x1, blocking collectives, local(): label_total = lax.psum(jnp.sum(valid_f), 'dp')  15.7 us
    ppermute x17, starting transfers between devices, swap(): return lax.ppermute(value, axis, [(i, i ^ hop) for i in range(size)])  12.9 us
  transfers between devices with their start and end apart: 18, of which 10 were waited for; matrix products, arithmetic and copies ran while one was open for 9% of the time, Pallas kernels for 15%

profile of v3, /device:TPU:0, one launch (start us, length us, event | category | flops | bytes accessed | tf_op | source)
XLA Modules:
  0.0 499.7 jit_solution(18256795692521672958)
XLA Ops:
  7.2 2.2 convert_element_type.156
  10.1 15.7 %psum.7 = f32[]{:T(128)} all-reduce(f32[]{:T(128)} %convert_reduce_fusion.1), channel_id=1, replica_groups=mesh['dp'=8,'mlp'=4] {'dp'}, use_global_device_ids=true, to_apply=%region_2.3 | all-reduce | flops 1 | bytes 8 | tf_op jit(solution)/shard_map/psum | solution.py:773
  28.5 4.2 pad.63.pixels
  40.3 109.7 %all-gather.3.cloned.1.call-done = bf16[13824,768]{1,0:T(8,128)(2,1)} async-done(((bf16[432,768]{1,0:T(8,128)(2,1)}), bf16[13824,768]{1,0:T(8,128)(2,1)}) %all-gather.3.cloned.1.call-update) | async-done | bytes 21233680 | tf_op jit(solution)/shard_map/all_gather | solution.py:736
  150.0 38.6 %time_forward.1 = (f32[12,208,768]{2,1,0:T(8,128)}, bf16[12,208,768]{2,1,0:T(8,128)(2,1)}, bf16[12,208,768]{2,1,0:T(8,128)(2,1)}, f32[12,208,128]{2,1,0:T(8,128)...) custom-call(s32[272]{0:T(512)} %multiply_add_fusion.3.slots.s, ...), custom_call_target="tpu_custom_call" | custom-call | flops 41221619712 | bytes 9437184 | tf_op jit(solution)/shard_map/time_forward/pallas_call | solution.py:838
  188.6 40.2 %space_forward.1 = (bf16[6,208,768]{2,1,0:T(8,128)(2,1)}, bf16[6,208,768]{2,1,0:T(8,128)(2,1)}, f32[6,208,128]{2,1,0:T(8,128)}, bf16[6,208,768]{2,1,0:T(8,128)(2...) custom-call(s32[272]{0:T(512)} %multiply_add_fusion.3.slots.s, ...), custom_call_target="tpu_custom_call" | custom-call | flops 44166021120 | bytes 9437184 | tf_op jit(solution)/shard_map/space_forward/pallas_call | solution.py:838
  233.5 34.7 %mlp_backward.1 = (f32[6,208,768]{2,1,0:T(8,128)}, bf16[2,2,768,384]{3,2,1,0:T(8,128)(2,1)}, bf16[2,2,768,384]{3,2,1,0:T(8,128)(2,1)}, f32[8,768]{1,0:T(8,128)}, f32[8,768]{1,0:T(8,128)}) custom-call(s32[272]{0:T(512)} %multiply_add_fusion.3.slots.s, f32[6]{0:T(128)} %dynamic_slice.36.fw, s32[1]{0:T(128)} %bitcast.2.m.member, s32[1]{0:T(128)} %bitcast.3.c.core, ...), custom_call_target="tpu_custom_call" | custom-call | flops 38277218304 | bytes 9437184 | tf_op jit(solution)/shard_map/mlp_backward/pallas_call | solution.py:838
  268.4 33.5 %space_backward.1 = (bf16[6,208,768]{2,1,0:T(8,128)(2,1)}, bf16[2,4,192,384]{3,2,1,0:T(8,128)(2,1)}, bf16[2,4,192,384]{3,2,1,0:T(8,128)(2,1)}, f32[8,768]{1,0:T(8,128)}) custom-call(s32[272]{0:T(512)} %multiply_add_fusion.3.slots.s, s32[1]{0:T(128)} %bitcast.3.c.core, bf16[288,48,768]{2,1,0:T(8,128)(2,1)} %bitcast.125, ...), custom_call_target="tpu_custom_call" | custom-call | flops 47110422528 | bytes 9437184 | tf_op jit(solution)/shard_map/space_backward/pallas_call | solution.py:838
  303.3 1.6 constant_dynamic-slice_fusion
  307.7 2.0 fusion.6
  309.7 1.6 fusion.3
  311.3 20.1 %collective-permute-done.1.far = bf16[6,112,768]{2,1,0:T(8,128)(2,1)} collective-permute-done((bf16[6,112,768]{2,1,0:T(8,128)(2,1)}, bf16[6,112,768]{2,1,0:T(8,128)(2,1)}, u32[]{:S(2)}, u32[]{:S(2)}) %collective-permute-start.1) | collective-permute-done | bytes 1032224 | tf_op jit(solution)/shard_map/ppermute | solution.py:641
  333.4 41.2 %time_backward.1 = (bf16[2,5,192,384]{3,2,1,0:T(8,128)(2,1)}, bf16[2,5,192,384]{3,2,1,0:T(8,128)(2,1)}, f32[8,768]{1,0:T(8,128)}, f32[112,768]{1,0:T(8,128)}, f32[12,768]{1,0:T(8,128)}) custom-call(s32[272]{0:T(512)} %multiply_add_fusion.3.slots.s, s32[1]{0:T(128)} %bitcast.2.m.member, s32[1]{0:T(128)} %bitcast.3.c.core, bf16[288,48,768]{2,1,0:T(8,128)(2,1)} %bitcast.126, ...), custom_call_target="tpu_custom_call" | custom-call | flops 52999225344 | bytes 9437184 | tf_op jit(solution)/shard_map/time_backward/pallas_call | solution.py:838
  378.5 2.5 slice.140
  381.0 2.0 slice.179
  390.2 1.8 collective-permute-start.9
  392.6 2.1 slice.178
  394.6 13.1 %collective-permute-done.9.refs_11_ = bf16[8,16,384]{2,1,0:T(8,128)(2,1)S(1)} collective-permute-done((bf16[8,16,384]{2,1,0:T(8,128)(2,1)S(1)}, bf16[8,16,384]{2,1,0:T(8,128)(2,1)S(1)}, u32[]{:S(2)}, u32[]{:S(2)}) %collective-permute-start.9) | collective-permute-done | bytes 98336 | tf_op jit(solution)/shard_map/ppermute | solution.py:641
  408.6 7.0 %pack.1 = (bf16[2,448,384]{2,1,0:T(8,128)(2,1)}, bf16[2,448,384]{2,1,0:T(8,128)(2,1)}, bf16[2,448,384]{2,1,0:T(8,128)(2,1)}, bf16[2,448,384]{2,1,0:T(8,128)(2,1)}) custom-call(s32[68]{0:T(128)} %fusion.46.dests, s32[1]{0:T(128)} %bitcast.1.place, bf16[20,48,384]{2,1,0:T(8,128)(2,1)} %bitcast.112, bf16[16,48,384]{2,1,0:T(8,128)(2,1)} %bitcast.114, ...), custom_call_target="tpu_custom_call" | custom-call | tf_op jit(solution)/shard_map/pack/pallas_call | solution.py:1061
  417.7 15.2 %collective-permute-done.12 = bf16[2,448,384]{2,1,0:T(8,128)(2,1)S(1)} collective-permute-done((bf16[2,448,384]{2,1,0:T(8,128)(2,1)}, bf16[2,448,384]{2,1,0:T(8,128)(2,1)S(1)}, u32[]{:S(2)}, u32[]{:S(2)}) %collective-permute-start.12) | collective-permute-done | bytes 688160 | tf_op jit(solution)/shard_map/ppermute | solution.py:641
  439.9 4.1 collective-permute-done.13
  444.0 4.1 collective-permute-done.11
  448.2 2.0 fusion.7
  450.5 2.1 collective-permute-done.14
  457.5 3.1 collective-permute-done.15
  460.7 1.6 collective-permute-start.16
  462.3 4.0 collective-permute-done.16
  466.3 9.9 %all-gather = f32[40,8,768]{2,1,0:T(8,128)S(1)} all-gather(f32[5,8,768]{2,1,0:T(8,128)S(1)} %pad_maximum_fusion.6), channel_id=2, replica_groups=mesh['dp'=8,'mlp'=4] {'dp'}, dimensions={0}, use_global_device_ids=true | all-gather | bytes 1105920 | tf_op jit(solution)/shard_map/all_gather | solution.py:1095
  478.4 1.9 multiply_reduce_fusion.1
  482.4 3.3 multiply_subtract_fusion.2
  485.7 2.8 multiply_subtract_fusion
  488.8 2.5 multiply_subtract_fusion.1
  (188 shorter events, 50.4 us)
Async XLA Ops:
  7.2 19.3 %copy-start.29 = (s32[1,12]{1,0:T(1,128)S(1)}, s32[1,12]{1,0:T(1,128)}, u32[]{:S(2)}) copy-start(s32[1,12]{1,0:T(1,128)} %param.18) | copy-start | bytes 148
  7.2 142.8 %all-gather.3.cloned.1.call-start = ((), (), s32[]{:S(2)}) async-start(), calls=%async_computation | async-start | bytes 21897216 | tf_op jit(solution)/shard_map/all_gather | solution.py:736
  28.5 4.2 copy-start.4
  33.5 5.0 copy-start.20
  33.5 5.8 %copy-start.26 = (s32[1,12]{1,0:T(1,128)S(1)}, s32[1,12]{1,0:T(1,128)}, u32[]{:S(2)}) copy-start(s32[1,12]{1,0:T(1,128)} %param.19) | copy-start | bytes 148
  188.6 41.2 %copy-start.2 = (f32[768,400]{0,1:T(8,128)S(1)}, f32[768,400]{0,1:T(8,128)}, u32[]{:S(2)}) copy-start(f32[768,400]{0,1:T(8,128)} %param.29) | copy-start | bytes 3686404
  228.8 4.1 collective-permute-start
  268.3 41.5 %collective-permute-start.2 = (bf16[2,2,768,384]{3,2,1,0:T(8,128)(2,1)}, bf16[2,2,768,384]{3,2,1,0:T(8,128)(2,1)S(1)}, u32[]{:S(2)}, u32[]{:S(2)}) collective-permute-start(bf16[2,2,768,384]{3,2,1,0:T(8,128)(2,1)} %get-tuple-element.82), channel_id=1, source_target_pairs={{0,4},{4,0},{8,12},{12,8},{16,20},{20,16},{24,28},{28,24},{1,5},{5... | collective-permute-start | bytes 7077896 | tf_op jit(solution)/shard_map/ppermute | solution.py:641
  301.9 5.8 %collective-permute-start.3 = (bf16[2,4,192,384]{3,2,1,0:T(8,128)(2,1)}, bf16[2,4,192,384]{3,2,1,0:T(8,128)(2,1)}, u32[]{:S(2)}, u32[]{:S(2)}) collective-permute-start(bf16[2,4,192,384]{3,2,1,0:T(8,128)(2,1)} %get-tuple-element.84), channel_id=1, source_target_pairs={{0,4},{4,0},{8,12},{12,8},{16,20},{20,16},{24,28},{28,24},{1,5},{5... | collective-permute-start | bytes 3538952 | tf_op jit(solution)/shard_map/ppermute | solution.py:641
  306.3 25.1 %collective-permute-start.1 = (bf16[6,112,768]{2,1,0:T(8,128)(2,1)}, bf16[6,112,768]{2,1,0:T(8,128)(2,1)}, u32[]{:S(2)}, u32[]{:S(2)}) collective-permute-start(bf16[6,112,768]{2,1,0:T(8,128)(2,1)} %get-tuple-element.134), channel_id=1, source_target_pairs={{0,1},{1,0},{2,3},{3,2},{4,5},{5,4},{6,7},{7,6},{8,9},{9,8},{10,11... | collective-permute-start | bytes 3096584 | tf_op jit(solution)/shard_map/ppermute | solution.py:641
  331.4 43.3 %collective-permute-start.4 = (bf16[2,768,384]{2,1,0:T(8,128)(2,1)S(1)}, bf16[2,768,384]{2,1,0:T(8,128)(2,1)S(1)}, u32[]{:S(2)}, u32[]{:S(2)}) collective-permute-start(bf16[2,768,384]{2,1,0:T(8,128)(2,1)S(1)} %fusion.3), channel_id=1, source_target_pairs={{0,1},{1,0},{2,3},{3,2},{4,5},{5,4},{6,7},{7,6},{8,9},{9,8},{10,11... | collective-permute-start | bytes 3538952 | tf_op jit(solution)/shard_map/ppermute | solution.py:641
  332.8 41.9 %collective-permute-start.5 = (bf16[4,192,384]{2,1,0:T(8,128)(2,1)}, bf16[4,192,384]{2,1,0:T(8,128)(2,1)}, u32[]{:S(2)}, u32[]{:S(2)}) collective-permute-start(bf16[4,192,384]{2,1,0:T(8,128)(2,1)} %fusion.6), channel_id=1, source_target_pairs={{0,1},{1,0},{2,3},{3,2},{4,5},{5,4},{6,7},{7,6},{8,9},{9,8},{10,11... | collective-permute-start | bytes 1769480 | tf_op jit(solution)/shard_map/ppermute | solution.py:641
  333.4 42.3 %copy-start = (s32[272]{0:T(512)S(1)}, s32[272]{0:T(512)}, u32[]{:S(2)}) copy-start(s32[272]{0:T(512)} %multiply_add_fusion.3.slots.s) | copy-start | bytes 3268
  375.7 8.4 %collective-permute-start.6 = (bf16[2,5,192,384]{3,2,1,0:T(8,128)(2,1)}, bf16[2,5,192,384]{3,2,1,0:T(8,128)(2,1)}, u32[]{:S(2)}, u32[]{:S(2)}) collective-permute-start(bf16[2,5,192,384]{3,2,1,0:T(8,128)(2,1)} %get-tuple-element.102), channel_id=1, source_target_pairs={{0,4},{4,0},{8,12},{12,8},{16,20},{20,16},{24,28},{28,24},{1,5},{5... | collective-permute-start | bytes 4423688 | tf_op jit(solution)/shard_map/ppermute | solution.py:641
  378.5 4.5 copy-start.17
  378.5 4.5 copy-start.24
  378.5 4.5 copy-start.18
  386.6 21.1 %collective-permute-start.8 = (bf16[5,192,384]{2,1,0:T(8,128)(2,1)S(1)}, bf16[5,192,384]{2,1,0:T(8,128)(2,1)S(1)}, u32[]{:S(2)}, u32[]{:S(2)}) collective-permute-start(bf16[5,192,384]{2,1,0:T(8,128)(2,1)S(1)} %fusion.4), channel_id=1, source_target_pairs={{0,1},{1,0},{2,3},{3,2},{4,5},{5,4},{6,7},{7,6},{8,9},{9,8},{10,11... | collective-permute-start | bytes 2211848 | tf_op jit(solution)/shard_map/ppermute | solution.py:641
  387.8 2.3 collective-permute-start.7
  390.2 17.5 %collective-permute-start.9 = (bf16[8,16,384]{2,1,0:T(8,128)(2,1)S(1)}, bf16[8,16,384]{2,1,0:T(8,128)(2,1)S(1)}, u32[]{:S(2)}, u32[]{:S(2)}) collective-permute-start(bf16[8,16,384]{2,1,0:T(8,128)(2,1)S(1)} %fusion.18), channel_id=1, source_target_pairs={{0,1},{1,0},{2,3},{3,2},{4,5},{5,4},{6,7},{7,6},{8,9},{9,8},{10,11... | collective-permute-start | bytes 294920 | tf_op jit(solution)/shard_map/ppermute | solution.py:641
  415.6 17.3 %collective-permute-start.12 = (bf16[2,448,384]{2,1,0:T(8,128)(2,1)}, bf16[2,448,384]{2,1,0:T(8,128)(2,1)S(1)}, u32[]{:S(2)}, u32[]{:S(2)}) collective-permute-start(bf16[2,448,384]{2,1,0:T(8,128)(2,1)} %get-tuple-element.108), channel_id=1, source_target_pairs={{0,16},{4,20},{8,24},{12,28},{16,0},{20,4},{24,8},{28,12},{1,17},{... | collective-permute-start | bytes 2064392 | tf_op jit(solution)/shard_map/ppermute | solution.py:641
  417.1 19.3 %collective-permute-start.10 = (bf16[2,448,384]{2,1,0:T(8,128)(2,1)}, bf16[2,448,384]{2,1,0:T(8,128)(2,1)S(1)}, u32[]{:S(2)}, u32[]{:S(2)}) collective-permute-start(bf16[2,448,384]{2,1,0:T(8,128)(2,1)} %get-tuple-element.106), channel_id=1, source_target_pairs={{0,8},{4,12},{8,0},{12,4},{16,24},{20,28},{24,16},{28,20},{1,9},{5... | collective-permute-start | bytes 2064392 | tf_op jit(solution)/shard_map/ppermute | solution.py:641
  432.9 4.4 copy-start.14
  435.0 9.0 %collective-permute-start.13 = (bf16[448,384]{1,0:T(8,128)(2,1)}, bf16[448,384]{1,0:T(8,128)(2,1)S(1)}, u32[]{:S(2)}, u32[]{:S(2)}) collective-permute-start(bf16[448,384]{1,0:T(8,128)(2,1)} %fusion.11), channel_id=1, source_target_pairs={{0,8},{4,12},{8,0},{12,4},{16,24},{20,28},{24,16},{28,20},{1,9},{5... | collective-permute-start | bytes 1032200 | tf_op jit(solution)/shard_map/ppermute | solution.py:641
  439.3 8.8 %collective-permute-start.11 = (bf16[448,384]{1,0:T(8,128)(2,1)}, bf16[448,384]{1,0:T(8,128)(2,1)}, u32[]{:S(2)}, u32[]{:S(2)}) collective-permute-start(bf16[448,384]{1,0:T(8,128)(2,1)} %fusion.10), channel_id=1, source_target_pairs={{0,16},{4,20},{8,24},{12,28},{16,0},{20,4},{24,8},{28,12},{1,17},{... | collective-permute-start | bytes 1032200 | tf_op jit(solution)/shard_map/ppermute | solution.py:641
  444.0 6.1 %copy-start.6 = (bf16[448,384]{1,0:T(8,128)(2,1)}, bf16[448,384]{1,0:T(8,128)(2,1)S(1)}, u32[]{:S(2)}) copy-start(bf16[448,384]{1,0:T(8,128)(2,1)S(1)} %collective-permute-done.13) | copy-start | bytes 1032196
  450.1 2.5 collective-permute-start.14
  455.0 11.2 %copy-start.19 = (f32[8,768]{1,0:T(8,128)S(1)}, f32[8,768]{1,0:T(8,128)}, u32[]{:S(2)}) copy-start(f32[8,768]{1,0:T(8,128)} %get-tuple-element.109) | copy-start | bytes 73732
  456.7 3.9 collective-permute-start.15
  460.7 5.6 %collective-permute-start.16 = (f32[2,8,768]{2,1,0:T(8,128)S(1)}, f32[2,8,768]{2,1,0:T(8,128)S(1)}, u32[]{:S(2)}, u32[]{:S(2)}) collective-permute-start(f32[2,8,768]{2,1,0:T(8,128)S(1)} %pad_maximum_fusion.11), channel_id=1, source_target_pairs={{0,2},{1,3},{2,0},{3,1},{4,6},{5,7},{6,4},{7,5},{8,10},{9,11},{10,... | collective-permute-start | bytes 147464 | tf_op jit(solution)/shard_map/ppermute | solution.py:641
  482.3 3.3 copy-start.1
  482.4 3.3 copy-start.7
  (16 other events, 31.6 us)
Sparse Core Ops, SparseCore 0:
  11.4 138.5 all-gather.2

commit v4 on v3

--- a/solution.py
+++ b/solution.py
@@ -105,6 +105,14 @@
     return [(i, lanes) for i in range(count) for lanes in pairs]
 
 
+def each_row(count, begin, finish):
+    def one(i, carry):
+        in_flight([(i, lanes) for unused, lanes in jobs_of(1)], begin, finish)
+        return carry
+
+    lax.fori_loop(0, count, one, 0)
+
+
 def in_flight(jobs, begin, finish):
     waiting = None
     for job in jobs:
@@ -137,7 +145,7 @@
     in_flight(jobs_of(count), begin, finish)
 
 
-def attend_back(count, load, store, extra_q, extra_k):
+def attend_back(count, load, store, extra_q, extra_k, looped=False):
     low, high = low_lanes()
 
     def begin(i, lanes):
@@ -170,7 +178,10 @@
             pick_half(mm(soft, grads)).astype(bf16),
         )
 
-    in_flight(jobs_of(count), begin, finish)
+    if looped:
+        each_row(count, begin, finish)
+    else:
+        in_flight(jobs_of(count), begin, finish)
 
 
 def project(hidden, rows, tiles):
@@ -335,14 +346,14 @@
 
 
 def mlp_backward(
-    slots, frame_weight, member, core, patches, gathered, pool, pool_other, head, valid, targets, total,
-    hid2, hat2, rstd2, hat3, rstd3, gp, act, low_rows,
-    dx2_ref, keep_ref, send_ref, rows_ref, small_ref,
-    ups, downs, dus, spread, up_sum, down_sum, row_sums, sems,
+    slots, frame_weight, member, patches, gathered, pool, pool_other, head, valid, targets, total,
+    hat2, rstd2, hat3, rstd3, gp, low_rows,
+    dx2_ref, g3_ref, du_ref, rows_ref, small_ref,
+    ups, downs, dus, spread, row_sums, sems,
 ):
     step = pl.program_id(0)
     members = gp.shape[0]
-    cut = hid2.shape
+    cut = hat2.shape
     span, count, width = cut
     flat = (span * count, width)
 
@@ -364,8 +375,6 @@
         small_ref[0:1, :] = pooled.astype(f32)
         small_ref[1:2, 0 : grad.shape[1]] = grad[0:1].astype(f32)
         small_ref[2:3, 0:128] = jnp.broadcast_to(loss[0:1], (1, 128))
-        up_sum[...] = jnp.zeros_like(up_sum)
-        down_sum[...] = jnp.zeros_like(down_sum)
         row_sums[...] = jnp.zeros_like(row_sums)
         arrive(downs, sems.at[1])
 
@@ -382,6 +391,7 @@
     grad_top = norm_back(grad_final, xhat, rstd, low_now[3:4])
     row_sums[2] += fold(grad_top)
     grad_b = grad_top.astype(bf16)
+    g3_ref[...] = grad_b.reshape(cut)
 
     for j in range(members):
         lanes = slice(j * width, (j + 1) * width)
@@ -395,8 +405,7 @@
     grad_hidden = mm_nt(dus[...], ups[...])
     for i in range(2):
         own = pl.ds(pl.multiple_of((member[0] ^ i) * width, 128), width)
-        up_sum[i] += mm_tn(hid2[...].reshape(flat), dus[:, own])
-        down_sum[i] += mm_tn(act[i].reshape(flat), grad_b)
+        du_ref[i] = dus[:, own].reshape(cut)
     xhat = hat2[...].reshape(flat).astype(f32)
     rstd = rstd2[...].reshape(flat[0], 128)[:, 0:1]
     row_sums[0] += fold(grad_hidden * xhat)
@@ -405,13 +414,36 @@
 
     @pl.when(step == pl.num_programs(0) - 1)
     def _():
-        for ref, half in zip((keep_ref, send_ref), column_halves(core[0], width)):
-            for i in range(2):
-                ref[i, 0] = up_sum[i, :, half].astype(bf16)
-                ref[i, 1] = down_sum[i, :, half].astype(bf16)
         rows_ref[...] = jnp.zeros_like(rows_ref)
         for i in range(5):
             rows_ref[i : i + 1] = jnp.sum(row_sums[i], axis=0, keepdims=True)
+
+
+def mlp_weights(core, hid2, g3, du, act, keep_ref, send_ref, sums):
+    rows, width = hid2.shape[0] * hid2.shape[1], hid2.shape[2]
+    sums[0] = mm_tn(hid2[...].reshape(rows, width), du[0].reshape(rows, width))
+    sums[1] = mm_tn(act[0].reshape(rows, width), g3[...].reshape(rows, width))
+    for ref, half in zip((keep_ref, send_ref), column_halves(core[0], width)):
+        for n in range(2):
+            ref[0, n] = sums[n, :, half].astype(bf16)
+
+
+def space_weights(core, picked, hid1, o, grads, keep_ref, send_ref, rows_ref, left, sums):
+    step = pl.program_id(0)
+    rows, width = hid1.shape[0] * hid1.shape[1], hid1.shape[2]
+    share = keep_ref.shape[2]
+
+    def select(source):
+        chosen = mm_nt(picked[...], source[...].reshape(rows, width)).astype(bf16)
+        left[...] = chosen + ones_row(picked)
+
+    pl.when(step == 0)(lambda: select(hid1))
+    pl.when(step == pl.num_programs(0) - 1)(lambda: select(o))
+    sums[...] = mm(left[...], grads[...].reshape(rows, width))
+    for ref, half in zip((keep_ref, send_ref), column_halves(core[0], width)):
+        for n in range(2):
+            ref[n, 0] = sums[n * share : (n + 1) * share, half].astype(bf16)
+    rows_ref[0] = sums[2 * share : 2 * share + 8]
 
 
 def close_attention(
@@ -467,12 +499,11 @@
 
 
 def space_backward(
-    slots, core, gathered, dx2, hid1, hat1, rstd1, q, k, v, o, rows, picked, extra_q, extra_k,
-    g1_ref, keep_ref, send_ref, rows_ref,
-    joint, out, joint_sum, out_sum, row_sums, grads, outer, sems,
+    slots, gathered, dx2, hat1, rstd1, q, k, v, rows, extra_q, extra_k,
+    g1_ref, grads_ref, rows_ref, joint, out, row_sums, outer, sems,
 ):
     step = pl.program_id(0)
-    cut = hid1.shape
+    cut = hat1.shape
     span, count, width = cut
     flat = (span * count, width)
 
@@ -480,35 +511,37 @@
     def _():
         fetch(slots, gathered, out, sems.at[1], lambda t: t + 8, False)
         fetch(slots, gathered, joint, sems.at[0], lambda t: t + 5, True)
-        clear(joint_sum, out_sum, row_sums)
+        clear(row_sums)
         arrive(out, sems.at[1])
 
     grad_b = dx2[...].reshape(flat).astype(bf16)
+    grads_ref[:, :, 3 * width :] = grad_b.reshape(cut)
     outer[...] = mm_nt(grad_b, out[...]).astype(bf16)
 
     def load(f, lanes):
-        here = slice(f * count, (f + 1) * count)
+        here = pl.ds(pl.multiple_of(f * count, 16), count)
         return q[f, :, lanes], k[f, :, lanes], v[f, :, lanes], outer[here, lanes]
 
     def store(f, lanes, *parts):
-        here = slice(f * count, (f + 1) * count)
         for i, part in enumerate(parts):
-            grads[here, i * width + lanes.start : i * width + lanes.stop] = part
-
-    attend_back(span, load, store, extra_q, extra_k)
+            grads_ref[f, :, i * width + lanes.start : i * width + lanes.stop] = part
+
+    attend_back(span, load, store, extra_q, extra_k, looped=True)
     pl.when(step == 0)(lambda: arrive(joint, sems.at[0]))
-    picked_now = picked[...]
-    g1_ref[...] = close_attention(
-        dx2[...].reshape(flat), grad_b, hid1[...].reshape(flat), hat1[...].reshape(flat),
-        rstd1[...].reshape(flat[0], 128), grads[...], o[...].reshape(flat), rows[...],
-        picked_now, ones_row(picked_now), joint, joint_sum, out_sum, row_sums,
-    ).astype(bf16).reshape(cut)
+    grads = grads_ref[:, :, : 3 * width].reshape(flat[0], 3 * width)
+    grad_hidden = mm_nt(grads, joint[...])
+    xhat = hat1[...].reshape(flat).astype(f32)
+    rstd = rstd1[...].reshape(flat[0], 128)[:, 0:1]
+    row_sums[0] += fold(grad_hidden * xhat)
+    row_sums[1] += fold(grad_hidden)
+    grad_stream = dx2[...].reshape(flat) + norm_back(grad_hidden, xhat, rstd, rows[0:1])
+    g1_ref[...] = grad_stream.astype(bf16).reshape(cut)
 
     @pl.when(step == pl.num_programs(0) - 1)
     def _():
-        finish_attention(
-            core[0], (keep_ref, send_ref), 0, rows_ref, joint_sum, out_sum, row_sums
-        )
+        rows_ref[...] = jnp.zeros_like(rows_ref)
+        for i in range(2):
+            rows_ref[i : i + 1] = jnp.sum(row_sums[i], axis=0, keepdims=True)
 
 
 def time_backward(
@@ -620,7 +653,7 @@
         table = n == count - 1
 
         def one(i, carry, keep=keep, met=met, far=far, source=source, first=first, n=n, table=table):
-            total = keep[i].astype(f32) + met[i].astype(f32) + far[i].astype(f32)
+            total = keep[0, i].astype(f32) + met[0, i].astype(f32) + far[i].astype(f32)
             source[i] = total.astype(bf16)
             if table:
                 route(source.at[i], i, pl.ds(slots * BR, table_rows), sems.at[n])
@@ -771,7 +804,9 @@
     ).astype(f32)
     valid_f = label_valid.astype(f32)
     label_total = lax.psum(jnp.sum(valid_f), "dp")
-    pix, label_total = lax.optimization_barrier((pix, label_total))
+    head_b = jnp.pad(head_weight.astype(bf16), ((0, 0), (0, class_pad - classes)))
+    valid_p = jnp.pad(valid_f, ((0, 0), (0, class_pad - classes)))
+    targets_p = jnp.pad(targets, ((0, 0), (0, class_pad - classes)))
     share = width // mlp_count
     half = member % 2
     place = lax.axis_index("dp").astype(jnp.int32)
@@ -787,6 +822,18 @@
     space_rows = jnp.pad(tables[6:11], ((0, 3), (0, 0)))
     low_rows = jnp.pad(tables[11:16], ((0, 3), (0, 0)))
 
+    shared_here = shared_blocks // mlp_count
+    here_ids = jnp.arange(shared_here + 2 * per_tile)
+    block_of = jnp.where(
+        here_ids < shared_here,
+        here_ids * mlp_count + member,
+        here_ids - shared_here + shared_blocks + member * 2 * per_tile,
+    )
+    here_slots = slot_index[block_of]
+    dests = (here_slots // (slots * mlp_count)) * slots + here_slots % slots
+    pix, label_total, head_b, valid_p, targets_p, picked, dests = lax.optimization_barrier(
+        (pix, label_total, head_b, valid_p, targets_p, picked, dests)
+    )
     cube32 = jax.ShapeDtypeStruct((frames, padded, width), f32)
     cube16 = jax.ShapeDtypeStruct((frames, padded, width), bf16)
     thin32 = jax.ShapeDtypeStruct((frames, padded, 128), f32)
@@ -834,13 +881,15 @@
     space_extra = whole(2 * padded, PAIR)
     pick_spec = whole(2 * share + 16, width)
 
-    def call(kernel, name, units, scalars, grid, ins, in_specs, outs, out_specs, scratch):
+    def call(
+        kernel, name, units, scalars, grid, ins, in_specs, outs, out_specs, scratch, tiles=True
+    ):
         return pl.pallas_call(
             kernel,
             grid_spec=pltpu.PrefetchScalarGridSpec(
                 num_scalar_prefetch=len(scalars),
                 grid=grid,
-                in_specs=[any_spec] + in_specs,
+                in_specs=([any_spec] if tiles else []) + in_specs,
                 out_specs=out_specs,
                 scratch_shapes=scratch,
             ),
@@ -852,7 +901,7 @@
                 transcendentals=0,
             ),
             name=name,
-        )(*scalars, gathered, *ins)
+        )(*scalars, *([gathered] if tiles else []), *ins)
 
     def tile_bufs(*shapes):
         return [pltpu.VMEM((rows * width, cols * width), bf16) for rows, cols in shapes]
@@ -894,77 +943,101 @@
         + [pltpu.VMEM((frame_rows, mlp_count * width), bf16), pltpu.SemaphoreType.DMA((4,))],
     )
 
-    head_b = jnp.pad(head_weight.astype(bf16), ((0, 0), (0, class_pad - classes)))
-    valid_p = jnp.pad(valid_f, ((0, 0), (0, class_pad - classes)))
-    targets_p = jnp.pad(targets, ((0, 0), (0, class_pad - classes)))
     pool_other = swap(pool, "mlp", 1)
     middle = width // 2
     squares16 = jax.ShapeDtypeStruct((2, 2, width, middle), bf16)
-    dx2, keep_mlp, send_mlp, rows_low, small = call(
-        lambda s, fw, m, c, *refs: mlp_backward(s, fw, m, c, patches, *refs),
+    pair16 = jax.ShapeDtypeStruct((2, half_frames, padded, width), bf16)
+    dx2, g3, du, rows_low, small = call(
+        lambda s, fw, m, *refs: mlp_backward(s, fw, m, patches, *refs),
         "mlp_backward",
-        13,
-        [slot_index, frame_weight, member_s, core_s],
+        9,
+        [slot_index, frame_weight, member_s],
         space_grid,
         [
             pool, pool_other, head_b, valid_p, targets_p, label_total[None],
-            hid2, hat2, rstd2, hat3, rstd3, gp, act, low_rows,
+            hat2, rstd2, hat3, rstd3, gp, low_rows,
         ],
         [
             rows_spec, rows_spec, whole(width, class_pad), whole(1, class_pad), whole(1, class_pad),
             pl.BlockSpec(memory_space=pltpu.SMEM),
-            frame_spec, frame_spec, frame_thin, frame_spec, frame_thin, gp_spec, act_spec,
-            rows_spec,
+            frame_spec, frame_thin, frame_spec, frame_thin, gp_spec, rows_spec,
         ],
-        [half32, squares16, squares16, row32, row32],
-        [frame_spec] + [whole(2, 2, width, middle)] * 2 + [rows_spec, rows_spec],
+        [half32, half16, pair16, row32, row32],
+        [frame_spec, frame_spec, act_spec, rows_spec, rows_spec],
         tile_bufs((1, mlp_count), (mlp_count, 1))
         + [
             pltpu.VMEM((frame_rows, mlp_count * width), bf16),
             pltpu.VMEM((8, width), f32),
-            pltpu.VMEM((2, width, width), f32),
-            pltpu.VMEM((2, width, width), f32),
             pltpu.VMEM((5, 8, width), f32),
             pltpu.SemaphoreType.DMA((2,)),
         ],
     )
 
-    sums = [
-        pltpu.VMEM((2 * share + 16, 3 * width), f32),
-        pltpu.VMEM((2 * share + 16, width), f32),
-    ]
-    met_mlp = swap(send_mlp, "dp", 1)
-    g1, keep_space, send_space, rows_space = call(
+    grads_spec = pl.BlockSpec((FRAMES_AT_ONCE, padded, 4 * width), lambda f, *_: (f, 0, 0))
+    g1, grads_space, norm_space = call(
         space_backward,
         "space_backward",
-        16,
-        [slot_index, core_s],
+        11,
+        [slot_index],
         space_grid,
-        [dx2, hid1, hat1, rstd1, q_s, k_s, v_s, o_s, space_rows, picked, space_q, space_k],
-        [frame_spec] * 3
-        + [frame_thin]
-        + [frame_spec] * 4
-        + [rows_spec, pick_spec, space_extra, space_extra],
-        [half16] + [jax.ShapeDtypeStruct((2, 4, share, middle), bf16)] * 2 + [row32],
-        [frame_spec] + [whole(2, 4, share, middle)] * 2 + [rows_spec],
+        [dx2, hat1, rstd1, q_s, k_s, v_s, space_rows, space_q, space_k],
+        [frame_spec] * 2 + [frame_thin] + [frame_spec] * 3 + [rows_spec, space_extra, space_extra],
+        [half16, jax.ShapeDtypeStruct((half_frames, padded, 4 * width), bf16), row32],
+        [frame_spec, grads_spec, rows_spec],
         tile_bufs((1, 3), (1, 1))
-        + sums
         + [
             pltpu.VMEM((2, 8, width), f32),
-            pltpu.VMEM((frame_rows, 3 * width), bf16),
             pltpu.VMEM((frame_rows, width), bf16),
             pltpu.SemaphoreType.DMA((2,)),
         ],
     )
 
-
-    def patches_of(which):
+    def patches_of(grad, which):
         main = half_blocks * group_rows
-        here = lax.dynamic_slice_in_dim(g1, which * main, main, 1)
-        return jnp.concatenate([here, g1[:, 2 * main :]], axis=1)
-
-    far = swap(patches_of(1 - half), "mlp", 1)
-    near = patches_of(half)
+        here = lax.dynamic_slice_in_dim(grad, which * main, main, 1)
+        return jnp.concatenate([here, grad[:, 2 * main :]], axis=1)
+
+    leaving, near, late_hid1, late_hid2 = lax.optimization_barrier(
+        (patches_of(g1, 1 - half), patches_of(g1, half), hid1, hid2)
+    )
+    far = swap(leaving, "mlp", 1)
+    clip_spec = whole(half_frames, padded, width)
+    one_spec = pl.BlockSpec((1, half_frames, padded, width), lambda i, c: (i, 0, 0, 0))
+    square_spec = pl.BlockSpec((1, 2, width, middle), lambda i, c: (i, 0, 0, 0))
+    keep_mlp, send_mlp = call(
+        mlp_weights,
+        "mlp_weights",
+        2,
+        [core_s],
+        (2,),
+        [late_hid2, g3, du, act],
+        [clip_spec, clip_spec, one_spec, one_spec],
+        [squares16] * 2,
+        [square_spec] * 2,
+        [pltpu.VMEM((2, width, width), f32)],
+        tiles=False,
+    )
+    met_mlp = swap(send_mlp, "dp", 1)
+    keep_space, send_space, sums_space = call(
+        space_weights,
+        "space_weights",
+        2,
+        [core_s],
+        (4,),
+        [picked, late_hid1, o_s, grads_space],
+        [
+            pick_spec, clip_spec, clip_spec,
+            pl.BlockSpec((half_frames, padded, width), lambda i, c: (0, 0, i)),
+        ],
+        [jax.ShapeDtypeStruct((2, 4, share, middle), bf16)] * 2
+        + [jax.ShapeDtypeStruct((4, 8, width), f32)],
+        [pl.BlockSpec((2, 1, share, middle), lambda i, c: (0, i, 0, 0))] * 2
+        + [pl.BlockSpec((1, 8, width), lambda i, c: (i, 0, 0))],
+        [pltpu.VMEM((2 * share + 16, half_frames * padded), bf16),
+         pltpu.VMEM((2 * share + 16, width), f32)],
+        tiles=False,
+    )
+    far, keep_space, send_space = lax.optimization_barrier((far, keep_space, send_space))
     met_space = swap(send_space, "dp", 1)
     chip_mlp = added(keep_mlp[1], met_mlp[1]).astype(bf16)
     chip_space = added(keep_space[1], met_space[1]).astype(bf16)
@@ -991,7 +1064,10 @@
         ],
         [whole(2, 5, share, middle)] * 2 + [rows_spec, patch_spec, whole(frames, width)],
         tile_bufs((1, 3), (1, 1))
-        + sums
+        + [
+            pltpu.VMEM((2 * share + 16, 3 * width), f32),
+            pltpu.VMEM((2 * share + 16, width), f32),
+        ]
         + [
             pltpu.VMEM((2 * share + 16, width), f32),
             pltpu.VMEM((2, 8, width), f32),
@@ -1015,7 +1091,10 @@
         [
             jnp.sum(grad_frames, axis=0, keepdims=True),
             rows_time[:5],
-            rows_space[:5],
+            norm_space[:2],
+            sums_space[0, :1],
+            sums_space[2, :1],
+            sums_space[3, :1],
             rows_low[:5],
             all_pos[:patches],
             grad_time,
@@ -1037,25 +1116,16 @@
     far_table = swap(added(keep_table[1], met_table[1]).astype(bf16), "mlp", 1)
 
     def blocks_of(*parts):
-        return [part.reshape(-1, BR, middle) for part in parts]
+        return [part.reshape(part.shape[0], -1, BR, middle) for part in parts]
 
     sources = (
-        blocks_of(keep_time[0], keep_space[0], keep_mlp[0])
-        + [keep_table[0]]
-        + blocks_of(met_time[0], met_space[0], met_mlp[0])
-        + [met_table[0]]
-        + blocks_of(far_time, far_space, far_mlp)
+        blocks_of(keep_time, keep_space, keep_mlp)
+        + [keep_table]
+        + blocks_of(met_time, met_space, met_mlp)
+        + [met_table]
+        + [part.reshape(-1, BR, middle) for part in (far_time, far_space, far_mlp)]
         + [far_table]
     )
-    shared_here = shared_blocks // mlp_count
-    here_ids = jnp.arange(shared_here + 2 * per_tile)
-    block_of = jnp.where(
-        here_ids < shared_here,
-        here_ids * mlp_count + member,
-        here_ids - shared_here + shared_blocks + member * 2 * per_tile,
-    )
-    here_slots = slot_index[block_of]
-    dests = (here_slots // (slots * mlp_count)) * slots + here_slots % slots
     bits = dp_count.bit_length() - 1
     chunk = jax.ShapeDtypeStruct((dp_count // 4, slots * BR + 16, middle), bf16)
     packed = pl.pallas_call(
@@ -1063,9 +1133,14 @@
         grid_spec=pltpu.PrefetchScalarGridSpec(
             num_scalar_prefetch=2,
             grid=(1,),
-            in_specs=[pl.BlockSpec(memory_space=pltpu.VMEM)] * 12,
+            in_specs=[
+                pl.BlockSpec((1,) + part.shape[1:], lambda i, *_: (0, 0, 0, 0))
+                if part.ndim == 4
+                else whole(*part.shape)
+                for part in sources
+            ],
             out_specs=[any_spec] * 4,
-            scratch_shapes=[pltpu.VMEM(part.shape, bf16) for part in sources[:4]]
+            scratch_shapes=[pltpu.VMEM(part.shape, bf16) for part in sources[8:]]
             + [pltpu.SemaphoreType.DMA((4,))],
         ),
         out_shape=[chunk] * 4,

time: 507 us -> 502 us (level)
  Pallas kernels: 195 us -> 209 us
  waiting for transfers between devices: 176 us -> 164 us
    pallas_call x5 -> x7, Pallas kernels: 188 us -> 202 us  [call(): pl.pallas_call(kernel, grid_spec=pltpu.PrefetchScalarGridSpec(num_scalar_...]
    slice x8 -> x2, local copies, waits for them, and re-layouts: 10.4 us -> 1.67 us  [the longest x1 0.93 us: patches_of(): return jnp.concatenate([here, grad[:, 2 * main:]], axis=1)]
    ppermute x17, waiting for transfers between devices: 66.5 us -> 59.3 us  [swap(): return lax.ppermute(value, axis, [(i, i ^ hop) for i in range(size)])]
  transfers between devices with their start and end apart: 18 -> 18, of which waited for: 10 -> 12; matrix products, arithmetic and copies ran while one was open for 9% -> 7% of each run, Pallas kernels for 15% -> 13%
where the time goes in v4:
time: 502 us; the launch traced here: 494 us
  Pallas kernels  209 us (42%)
  waiting for transfers between devices  164 us (33%)
  other arithmetic  32.8 us (7%)
  local copies, waits for them, and re-layouts  29.1 us (6%)
  blocking collectives  25.7 us (5%)
  between operations  18.8 us (4%)
  starting transfers between devices  10.4 us (2%)
    pallas_call x7, Pallas kernels, call(): pl.pallas_call(kernel, grid_spec=pltpu.PrefetchScalarGridSpec(num_scalar_...  202 us
    all_gather x1, waiting for transfers between devices, local(): lax.all_gather(slot_weight.astype(bf16), ('dp', 'mlp'), axis=0, tiled=True)  105 us
    ppermute x17, waiting for transfers between devices, swap(): return lax.ppermute(value, axis, [(i, i ^ hop) for i in range(size)])  59.3 us
    psum x1, blocking collectives, local(): label_total = lax.psum(jnp.sum(valid_f), 'dp')  15.7 us
    ppermute x17, starting transfers between devices, swap(): return lax.ppermute(value, axis, [(i, i ^ hop) for i in range(size)])  10.4 us
  transfers between devices with their start and end apart: 18, of which 12 were waited for; matrix products, arithmetic and copies ran while one was open for 7% of the time, Pallas kernels for 13%

profile of v4, /device:TPU:0, one launch (start us, length us, event | category | flops | bytes accessed | tf_op | source)
XLA Modules:
  0.0 493.9 jit_solution(15441645631599757147)
XLA Ops:
  7.2 2.3 convert_element_type.158
  10.2 15.7 %psum.7 = f32[]{:T(128)} all-reduce(f32[]{:T(128)} %convert_reduce_fusion.1), channel_id=1, replica_groups=mesh['dp'=8,'mlp'=4] {'dp'}, use_global_device_ids=true, to_apply=%region_1.2 | all-reduce | flops 1 | bytes 8 | tf_op jit(solution)/shard_map/psum | solution.py:806
  27.0 4.1 pad.64.pixels
  45.0 105.0 %all-gather.3.cloned.1.call-done = bf16[13824,768]{1,0:T(8,128)(2,1)} async-done(((bf16[432,768]{1,0:T(8,128)(2,1)}), bf16[13824,768]{1,0:T(8,128)(2,1)}) %all-gather.3.cloned.1.call-update) | async-done | bytes 21233680 | tf_op jit(solution)/shard_map/all_gather | solution.py:769
  150.0 38.6 %time_forward.1 = (f32[12,208,768]{2,1,0:T(8,128)}, bf16[12,208,768]{2,1,0:T(8,128)(2,1)}, bf16[12,208,768]{2,1,0:T(8,128)(2,1)}, f32[12,208,128]{2,1,0:T(8,128)...) custom-call(s32[272]{0:T(512)} %copy-done, ...), custom_call_target="tpu_custom_call" | custom-call | flops 41221619712 | bytes 9437184 | tf_op jit(solution)/shard_map/time_forward/pallas_call | solution.py:887
  188.6 40.0 %space_forward.1 = (bf16[6,208,768]{2,1,0:T(8,128)(2,1)}, bf16[6,208,768]{2,1,0:T(8,128)(2,1)}, f32[6,208,128]{2,1,0:T(8,128)}, bf16[6,208,768]{2,1,0:T(8,128)(2...) custom-call(s32[272]{0:T(512)} %copy-done, ...), custom_call_target="tpu_custom_call" | custom-call | flops 44166021120 | bytes 9437184 | tf_op jit(solution)/shard_map/space_forward/pallas_call | solution.py:887
  228.7 4.0 collective-permute-done.refs_2_
  233.3 29.3 %mlp_backward.1 = (f32[6,208,768]{2,1,0:T(8,128)}, bf16[6,208,768]{2,1,0:T(8,128)(2,1)}, bf16[2,6,208,768]{3,2,1,0:T(8,128)(2,1)}, f32[8,768]{1,0:T(8,128)}, f32[8,768]{1,0:T(8,128)}) custom-call(s32[272]{0:T(512)} %copy-done, f32[6]{0:T(128)} %dynamic_slice.36.fw, s32[1]{0:T(128)} %bitcast.3.m.member, bf16[288,48,768]{2,1,0:T(8,128)(2,1)} %bitcast.129, ...), custom_call_target="tpu_custom_call" | custom-call | flops 26499612672 | bytes 9437184 | tf_op jit(solution)/shard_map/mlp_backward/pallas_call | solution.py:887
  262.7 30.2 %space_backward.1 = (bf16[6,208,768]{2,1,0:T(8,128)(2,1)}, bf16[6,208,3072]{2,1,0:T(8,128)(2,1)}, f32[8,768]{1,0:T(8,128)}) custom-call(s32[272]{0:T(512)} %copy-done, bf16[288,48,768]{2,1,0:T(8,128)(2,1)} %bitcast.130, f32[6,208,768]{2,1,0:T(8,128)} %get-tuple-element.90.dx2, bf16[6,208,768]{2,1,0:T(8,128)(2,1)} %get-tuple-element.91.hat1, ...), custom_call_target="tpu_custom_call" | custom-call | flops 32388415488 | bytes 9437184 | tf_op jit(solution)/shard_map/space_backward/pallas_call | solution.py:887
  293.8 1.6 constant_dynamic-slice_fusion
  296.5 11.6 %mlp_weights.1 = (bf16[2,2,768,384]{3,2,1,0:T(8,128)(2,1)}, bf16[2,2,768,384]{3,2,1,0:T(8,128)(2,1)}) custom-call(s32[1]{0:T(128)} %bitcast.4.core, bf16[6,208,768]{2,1,0:T(8,128)(2,1)} %get-tuple-element.108.hid2, bf16[6,208,768]{2,1,0:T(8,128)(2,1)} %get-tuple-element.109.g3, bf16[2,6,208,768]{3,2,1,0:T(8,128)(2,1)} %get-tuple-element.110.du, ...), custom_call_target="tpu_custom_call" | custom-call | flops 5888802816 | bytes 9437184 | tf_op jit(solution)/shard_map/mlp_weights/pallas_call | solution.py:887
  308.1 10.9 %space_weights.1 = (bf16[2,4,192,384]{3,2,1,0:T(8,128)(2,1)}, bf16[2,4,192,384]{3,2,1,0:T(8,128)(2,1)}, f32[4,8,768]{2,1,0:T(8,128)}) custom-call(s32[1]{0:T(128)} %bitcast.4.core, bf16[400,768]{1,0:T(8,128)(2,1)} %pad_convert_fusion.picked, bf16[6,208,768]{2,1,0:T(8,128)(2,1)} %get-tuple-element.102.hid1, bf16[6,208,768]{2,1,0:T(8,128)(2,1)} %get-tuple-element.103.o, ...), custom_call_target="tpu_custom_call" | custom-call | flops 5888802816 | bytes 9437184 | tf_op jit(solution)/shard_map/space_weights/pallas_call | solution.py:887
  320.4 3.1 collective-permute-done.3
  323.5 2.4 fusion.6
  329.4 41.2 %time_backward.1 = (bf16[2,5,192,384]{3,2,1,0:T(8,128)(2,1)}, bf16[2,5,192,384]{3,2,1,0:T(8,128)(2,1)}, f32[8,768]{1,0:T(8,128)}, f32[112,768]{1,0:T(8,128)}, f32[12,768]{1,0:T(8,128)}) custom-call(s32[272]{0:T(512)} %copy-done, s32[1]{0:T(128)} %bitcast.3.m.member, s32[1]{0:T(128)} %bitcast.4.core, bf16[288,48,768]{2,1,0:T(8,128)(2,1)} %bitcast.131, ...), custom_call_target="tpu_custom_call" | custom-call | flops 52999225344 | bytes 9437184 | tf_op jit(solution)/shard_map/time_backward/pallas_call | solution.py:887
  384.9 17.1 %collective-permute-done.9.refs_11_ = bf16[8,16,384]{2,1,0:T(8,128)(2,1)S(1)} collective-permute-done((bf16[8,16,384]{2,1,0:T(8,128)(2,1)S(1)}, bf16[8,16,384]{2,1,0:T(8,128)(2,1)S(1)}, u32[]{:S(2)}, u32[]{:S(2)}) %collective-permute-start.9) | collective-permute-done | bytes 98336 | tf_op jit(solution)/shard_map/ppermute | solution.py:674
  402.9 7.0 %pack.1 = (bf16[2,448,384]{2,1,0:T(8,128)(2,1)}, bf16[2,448,384]{2,1,0:T(8,128)(2,1)}, bf16[2,448,384]{2,1,0:T(8,128)(2,1)}, bf16[2,448,384]{2,1,0:T(8,128)(2,1)}) custom-call(s32[68]{0:T(128)} %fusion.46.dests, s32[1]{0:T(128)} %bitcast.2.place, bf16[2,20,48,384]{3,2,1,0:T(8,128)(2,1)} %bitcast.115, bf16[2,16,48,384]{3,2,1,0:T(8,128)(2,1)} %bitcast.117, ...), custom_call_target="tpu_custom_call" | custom-call | tf_op jit(solution)/shard_map/pack/pallas_call | solution.py:1131
  409.9 1.5 collective-permute-start.12
  412.0 15.2 %collective-permute-done.12 = bf16[2,448,384]{2,1,0:T(8,128)(2,1)S(1)} collective-permute-done((bf16[2,448,384]{2,1,0:T(8,128)(2,1)}, bf16[2,448,384]{2,1,0:T(8,128)(2,1)S(1)}, u32[]{:S(2)}, u32[]{:S(2)}) %collective-permute-start.12) | collective-permute-done | bytes 688160 | tf_op jit(solution)/shard_map/ppermute | solution.py:674
  429.4 1.4 collective-permute-start.13
  434.3 4.1 collective-permute-done.13
  438.4 4.1 collective-permute-done.11
  442.5 2.0 fusion.7
  444.8 2.1 collective-permute-done.14
  451.9 3.1 collective-permute-done.15
  455.0 1.6 collective-permute-start.16
  456.6 4.0 collective-permute-done.16
  460.6 9.9 %all-gather = f32[40,8,768]{2,1,0:T(8,128)S(1)} all-gather(f32[5,8,768]{2,1,0:T(8,128)S(1)} %pad_maximum_fusion.6), channel_id=2, replica_groups=mesh['dp'=8,'mlp'=4] {'dp'}, dimensions={0}, use_global_device_ids=true | all-gather | bytes 1105920 | tf_op jit(solution)/shard_map/all_gather | solution.py:1170
  472.8 1.9 multiply_reduce_fusion.1
  476.7 3.3 multiply_subtract_fusion.2
  480.1 2.8 multiply_subtract_fusion
  483.2 2.5 multiply_subtract_fusion.1
  (189 shorter events, 51.2 us)
Async XLA Ops:
  7.2 19.4 %copy-start.5 = (f32[768,400]{0,1:T(8,128)S(1)}, f32[768,400]{0,1:T(8,128)}, u32[]{:S(2)}) copy-start(f32[768,400]{0,1:T(8,128)} %param.29) | copy-start | bytes 3686404
  7.2 142.8 %all-gather.3.cloned.1.call-start = ((), (), s32[]{:S(2)}) async-start(), calls=%async_computation | async-start | bytes 21897216 | tf_op jit(solution)/shard_map/all_gather | solution.py:769
  31.1 5.4 %copy-start.32 = (s32[1,12]{1,0:T(1,128)S(1)}, s32[1,12]{1,0:T(1,128)}, u32[]{:S(2)}) copy-start(s32[1,12]{1,0:T(1,128)} %param.18) | copy-start | bytes 148
  32.1 6.4 %copy-start.9 = (f32[220,768]{1,0:T(8,128)S(1)}, f32[220,768]{1,0:T(8,128)}, u32[]{:S(2)}) copy-start(f32[220,768]{1,0:T(8,128)} %param.26) | copy-start | bytes 2027524
  33.5 5.1 %copy-start = (s32[272]{0:T(512)}, s32[272]{0:T(512)S(1)}, u32[]{:S(2)}) copy-start(s32[272]{0:T(512)S(1)} %multiply_add_fusion.3.slots.s) | copy-start | bytes 3268
  39.2 4.9 copy-start.29
  228.6 4.1 collective-permute-start
  296.5 23.9 %collective-permute-start.1 = (bf16[6,112,768]{2,1,0:T(8,128)(2,1)S(1)}, bf16[6,112,768]{2,1,0:T(8,128)(2,1)}, u32[]{:S(2)}, u32[]{:S(2)}) collective-permute-start(bf16[6,112,768]{2,1,0:T(8,128)(2,1)S(1)} %get-tuple-element.100), channel_id=1, source_target_pairs={{0,1},{1,0},{2,3},{3,2},{4,5},{5,4},{6,7},{7,6},{8,9},{9,8},{10,11... | collective-permute-start | bytes 3096584 | tf_op jit(solution)/shard_map/ppermute | solution.py:674
  308.0 17.9 %collective-permute-start.2 = (bf16[2,2,768,384]{3,2,1,0:T(8,128)(2,1)}, bf16[2,2,768,384]{3,2,1,0:T(8,128)(2,1)S(1)}, u32[]{:S(2)}, u32[]{:S(2)}) collective-permute-start(bf16[2,2,768,384]{3,2,1,0:T(8,128)(2,1)} %get-tuple-element.113), channel_id=1, source_target_pairs={{0,4},{4,0},{8,12},{12,8},{16,20},{20,16},{24,28},{28,24},{1,5},{5... | collective-permute-start | bytes 7077896 | tf_op jit(solution)/shard_map/ppermute | solution.py:674
  308.1 17.9 %copy-start.2 = (bf16[2,2,768,384]{3,2,1,0:T(8,128)(2,1)S(1)}, bf16[2,2,768,384]{3,2,1,0:T(8,128)(2,1)}, u32[]{:S(2)}) copy-start(bf16[2,2,768,384]{3,2,1,0:T(8,128)(2,1)} %get-tuple-element.112) | copy-start | bytes 7077892
  320.4 3.1 collective-permute-start.3
  327.4 43.3 %collective-permute-start.4 = (bf16[2,768,384]{2,1,0:T(8,128)(2,1)S(1)}, bf16[2,768,384]{2,1,0:T(8,128)(2,1)S(1)}, u32[]{:S(2)}, u32[]{:S(2)}) collective-permute-start(bf16[2,768,384]{2,1,0:T(8,128)(2,1)S(1)} %fusion.3), channel_id=1, source_target_pairs={{0,1},{1,0},{2,3},{3,2},{4,5},{5,4},{6,7},{7,6},{8,9},{9,8},{10,11... | collective-permute-start | bytes 3538952 | tf_op jit(solution)/shard_map/ppermute | solution.py:674
  328.1 42.5 %collective-permute-start.5 = (bf16[4,192,384]{2,1,0:T(8,128)(2,1)}, bf16[4,192,384]{2,1,0:T(8,128)(2,1)S(1)}, u32[]{:S(2)}, u32[]{:S(2)}) collective-permute-start(bf16[4,192,384]{2,1,0:T(8,128)(2,1)} %fusion.6), channel_id=1, source_target_pairs={{0,1},{1,0},{2,3},{3,2},{4,5},{5,4},{6,7},{7,6},{8,9},{9,8},{10,11... | collective-permute-start | bytes 1769480 | tf_op jit(solution)/shard_map/ppermute | solution.py:674
  329.4 43.8 %copy-start.27 = (f32[8,768]{1,0:T(8,128)S(1)}, f32[8,768]{1,0:T(8,128)}, u32[]{:S(2)}) copy-start(f32[8,768]{1,0:T(8,128)} %get-tuple-element.129) | copy-start | bytes 73732
  329.4 48.0 %copy-start.30 = (s32[1,12]{1,0:T(1,128)S(1)}, s32[1,12]{1,0:T(1,128)}, u32[]{:S(2)}) copy-start(s32[1,12]{1,0:T(1,128)} %param.19) | copy-start | bytes 148
  372.5 8.3 %collective-permute-start.6 = (bf16[2,5,192,384]{3,2,1,0:T(8,128)(2,1)}, bf16[2,5,192,384]{3,2,1,0:T(8,128)(2,1)S(1)}, u32[]{:S(2)}, u32[]{:S(2)}) collective-permute-start(bf16[2,5,192,384]{3,2,1,0:T(8,128)(2,1)} %get-tuple-element.134), channel_id=1, source_target_pairs={{0,4},{4,0},{8,12},{12,8},{16,20},{20,16},{24,28},{28,24},{1,5},{5... | collective-permute-start | bytes 4423688 | tf_op jit(solution)/shard_map/ppermute | solution.py:674
  380.9 21.1 %collective-permute-start.8 = (bf16[5,192,384]{2,1,0:T(8,128)(2,1)S(1)}, bf16[5,192,384]{2,1,0:T(8,128)(2,1)S(1)}, u32[]{:S(2)}, u32[]{:S(2)}) collective-permute-start(bf16[5,192,384]{2,1,0:T(8,128)(2,1)S(1)} %fusion.4), channel_id=1, source_target_pairs={{0,1},{1,0},{2,3},{3,2},{4,5},{5,4},{6,7},{7,6},{8,9},{9,8},{10,11... | collective-permute-start | bytes 2211848 | tf_op jit(solution)/shard_map/ppermute | solution.py:674
  382.1 19.9 %copy-start.16 = (bf16[1,2,8,16,384]{4,3,2,1,0:T(8,128)(2,1)}, bf16[1,2,8,16,384]{4,3,2,1,0:T(8,128)(2,1)S(1)}, u32[]{:S(2)}) copy-start(bf16[1,2,8,16,384]{4,3,2,1,0:T(8,128)(2,1)S(1)} %get-tuple-element.159) | copy-start | bytes 589828
  382.1 1.6 collective-permute-start.7
  383.8 18.2 %copy-start.22 = (bf16[2,8,16,384]{3,2,1,0:T(8,128)(2,1)}, bf16[2,8,16,384]{3,2,1,0:T(8,128)(2,1)S(1)}, u32[]{:S(2)}) copy-start(bf16[2,8,16,384]{3,2,1,0:T(8,128)(2,1)S(1)} %collective-permute-done.7.refs_7_) | copy-start | bytes 589828
  383.8 18.2 %collective-permute-start.9 = (bf16[8,16,384]{2,1,0:T(8,128)(2,1)S(1)}, bf16[8,16,384]{2,1,0:T(8,128)(2,1)S(1)}, u32[]{:S(2)}, u32[]{:S(2)}) collective-permute-start(bf16[8,16,384]{2,1,0:T(8,128)(2,1)S(1)} %fusion.18), channel_id=1, source_target_pairs={{0,1},{1,0},{2,3},{3,2},{4,5},{5,4},{6,7},{7,6},{8,9},{9,8},{10,11... | collective-permute-start | bytes 294920 | tf_op jit(solution)/shard_map/ppermute | solution.py:674
  409.9 17.3 %collective-permute-start.12 = (bf16[2,448,384]{2,1,0:T(8,128)(2,1)}, bf16[2,448,384]{2,1,0:T(8,128)(2,1)S(1)}, u32[]{:S(2)}, u32[]{:S(2)}) collective-permute-start(bf16[2,448,384]{2,1,0:T(8,128)(2,1)} %get-tuple-element.140), channel_id=1, source_target_pairs={{0,16},{4,20},{8,24},{12,28},{16,0},{20,4},{24,8},{28,12},{1,17},{... | collective-permute-start | bytes 2064392 | tf_op jit(solution)/shard_map/ppermute | solution.py:674
  411.4 19.3 %collective-permute-start.10 = (bf16[2,448,384]{2,1,0:T(8,128)(2,1)}, bf16[2,448,384]{2,1,0:T(8,128)(2,1)S(1)}, u32[]{:S(2)}, u32[]{:S(2)}) collective-permute-start(bf16[2,448,384]{2,1,0:T(8,128)(2,1)} %get-tuple-element.138), channel_id=1, source_target_pairs={{0,8},{4,12},{8,0},{12,4},{16,24},{20,28},{24,16},{28,20},{1,9},{5... | collective-permute-start | bytes 2064392 | tf_op jit(solution)/shard_map/ppermute | solution.py:674
  427.3 4.4 copy-start.19
  429.4 9.0 %collective-permute-start.13 = (bf16[448,384]{1,0:T(8,128)(2,1)}, bf16[448,384]{1,0:T(8,128)(2,1)S(1)}, u32[]{:S(2)}, u32[]{:S(2)}) collective-permute-start(bf16[448,384]{1,0:T(8,128)(2,1)} %fusion.11), channel_id=1, source_target_pairs={{0,8},{4,12},{8,0},{12,4},{16,24},{20,28},{24,16},{28,20},{1,9},{5... | collective-permute-start | bytes 1032200 | tf_op jit(solution)/shard_map/ppermute | solution.py:674
  433.7 8.8 %collective-permute-start.11 = (bf16[448,384]{1,0:T(8,128)(2,1)}, bf16[448,384]{1,0:T(8,128)(2,1)}, u32[]{:S(2)}, u32[]{:S(2)}) collective-permute-start(bf16[448,384]{1,0:T(8,128)(2,1)} %fusion.10), channel_id=1, source_target_pairs={{0,16},{4,20},{8,24},{12,28},{16,0},{20,4},{24,8},{28,12},{1,17},{... | collective-permute-start | bytes 1032200 | tf_op jit(solution)/shard_map/ppermute | solution.py:674
  434.3 10.2 %copy-start.1 = (s32[272]{0:T(512)S(1)}, s32[272]{0:T(512)}, u32[]{:S(2)}) copy-start(s32[272]{0:T(512)} %copy-done) | copy-start | bytes 3268
  438.4 6.1 %copy-start.11 = (bf16[448,384]{1,0:T(8,128)(2,1)}, bf16[448,384]{1,0:T(8,128)(2,1)S(1)}, u32[]{:S(2)}) copy-start(bf16[448,384]{1,0:T(8,128)(2,1)S(1)} %collective-permute-done.13) | copy-start | bytes 1032196
  444.5 2.5 collective-permute-start.14
  449.4 11.2 %copy-start.24 = (f32[8,768]{1,0:T(8,128)S(1)}, f32[8,768]{1,0:T(8,128)}, u32[]{:S(2)}) copy-start(f32[8,768]{1,0:T(8,128)} %get-tuple-element.141) | copy-start | bytes 73732
  451.1 3.9 collective-permute-start.15
  455.0 5.6 %collective-permute-start.16 = (f32[2,8,768]{2,1,0:T(8,128)S(1)}, f32[2,8,768]{2,1,0:T(8,128)S(1)}, u32[]{:S(2)}, u32[]{:S(2)}) collective-permute-start(f32[2,8,768]{2,1,0:T(8,128)S(1)} %pad_maximum_fusion.11), channel_id=1, source_target_pairs={{0,2},{1,3},{2,0},{3,1},{4,6},{5,7},{6,4},{7,5},{8,10},{9,11},{10,... | collective-permute-start | bytes 147464 | tf_op jit(solution)/shard_map/ppermute | solution.py:674
  (19 other events, 36.7 us)
Sparse Core Ops, SparseCore 0:
  11.4 138.5 all-gather.2

commit v5 on v4

--- a/solution.py
+++ b/solution.py
@@ -214,11 +214,11 @@
 
 
 def time_forward(
-    total, slots, gathered, pixels, pos, trow, rows, extra_q, extra_k,
+    total, slots, member, gathered, pixels, pos, trow, rows, extra_q, extra_k,
     x1_ref, hid_ref, hat_ref, rstd_ref, q_ref, k_ref, v_ref, o_ref,
     embed, joint, out, base, sems,
 ):
-    frames, span, width = x1_ref.shape
+    frames, span, width = hid_ref.shape
 
     @pl.when(pl.program_id(0) == 0)
     def _():
@@ -258,9 +258,11 @@
 
         attend(count, load, store, extra_q, extra_k)
         first(out, sems.at[2])
-        merged = o_ref[:, here].reshape(flat)
-        stream = base[: flat[0]] + mm(merged, out[...]) + rows_now[4:5]
-        x1_ref[:, here] = stream.reshape(cut)
+        near, some = frames // 2, flat[0] // 2
+        late = member[0] % 2
+        merged = o_ref[pl.ds(late * near, near), here].reshape(some, width)
+        stream = base[pl.ds(pl.multiple_of(late * some, 16), some)] + mm(merged, out[...])
+        x1_ref[:, here] = (stream + rows_now[4:5]).reshape(near, count * GROUP, width)
 
     by_groups(span // GROUP, total, work)
 
@@ -863,10 +865,6 @@
     back_spec = pl.BlockSpec((frames, group_rows, width), lambda s, i, m, c: (0, half_index(s, m), 0))
     back_thin = pl.BlockSpec((frames, group_rows, 128), lambda s, i, m, c: (0, half_index(s, m), 0))
     near_spec = pl.BlockSpec((half_frames, group_rows, width), lambda s, *_: (0, s, 0))
-    my_frame_spec = pl.BlockSpec(
-        (FRAMES_AT_ONCE, padded, width),
-        lambda f, s, w, m: ((m[0] % 2) * (half_frames // FRAMES_AT_ONCE) + f, 0, 0),
-    )
     act_spec = pl.BlockSpec((2, FRAMES_AT_ONCE, padded, width), lambda f, *_: (0, f, 0, 0))
     half16 = jax.ShapeDtypeStruct((half_frames, padded, width), bf16)
     half32 = jax.ShapeDtypeStruct((half_frames, padded, width), f32)
@@ -910,12 +908,12 @@
         partial(time_forward, groups),
         "time_forward",
         14,
-        [slot_index],
+        [slot_index, member_s],
         time_grid,
         [pix, pos, trow, time_rows, time_q, time_k],
         [group_spec, patch_spec, whole(frames, width), rows_spec, time_extra, time_extra],
-        [cube32, cube16, cube16, thin32] + [cube16] * 4,
-        [group_spec] * 3 + [group_thin] + [group_spec] * 4,
+        [half32, cube16, cube16, thin32] + [cube16] * 4,
+        [near_spec] + [group_spec] * 2 + [group_thin] + [group_spec] * 4,
         tile_bufs((1, 1), (1, 3), (1, 1))
         + [pltpu.VMEM((frames * group_rows, width), f32), pltpu.SemaphoreType.DMA((3,))],
     )
@@ -926,7 +924,7 @@
         [slot_index, frame_weight, member_s],
         space_grid,
         [x1, space_rows, low_rows, space_q, space_k],
-        [my_frame_spec, rows_spec, rows_spec, space_extra, space_extra],
+        [frame_spec, rows_spec, rows_spec, space_extra, space_extra],
         [half16, half16, half_thin]
         + [half16] * 4
         + [half16, half16, half_thin, half16, half_thin]
@@ -1077,11 +1075,14 @@
         ],
     )
 
-    grad_time = jnp.einsum("ft,fd->td", time_hot, grad_frames, precision=highest)
     send_time, far_mlp, far_space = lax.optimization_barrier((send_time, far_mlp, far_space))
     met_time = swap(send_time, "dp", 1)
     chip_time = added(keep_time[1], met_time[1]).astype(bf16)
+    chip_time, grad_frames, grad_pos = lax.optimization_barrier(
+        (chip_time, grad_frames, grad_pos)
+    )
     far_time = swap(chip_time, "mlp", 1)
+    grad_time = jnp.einsum("ft,fd->td", time_hot, grad_frames, precision=highest)
     main = half_blocks * group_rows
     all_pos = jnp.concatenate(
         [jnp.where(half == i, grad_pos[:main], 0.0) for i in range(2)] + [grad_pos[main:]]

time: 502 us -> 499 us (level)
  transfers between devices with their start and end apart: 18 -> 18, of which waited for: 12 -> 13; matrix products, arithmetic and copies ran while one was open for 7% -> 6% of each run, Pallas kernels for 13% -> 13%
where the time goes in v5:
time: 499 us; the launch traced here: 491 us
  Pallas kernels  208 us (42%)
  waiting for transfers between devices  164 us (33%)
  other arithmetic  34.8 us (7%)
  blocking collectives  25.6 us (5%)
  local copies, waits for them, and re-layouts  24.8 us (5%)
  between operations  18.8 us (4%)
  starting transfers between devices  11.2 us (2%)
    pallas_call x7, Pallas kernels, call(): pl.pallas_call(kernel, grid_spec=pltpu.PrefetchScalarGridSpec(num_scalar_...  201 us
    all_gather x1, waiting for transfers between devices, local(): lax.all_gather(slot_weight.astype(bf16), ('dp', 'mlp'), axis=0, tiled=True)  105 us
    ppermute x17, waiting for transfers between devices, swap(): return lax.ppermute(value, axis, [(i, i ^ hop) for i in range(size)])  59.2 us
    psum x1, blocking collectives, local(): label_total = lax.psum(jnp.sum(valid_f), 'dp')  15.7 us
    ppermute x17, starting transfers between devices, swap(): return lax.ppermute(value, axis, [(i, i ^ hop) for i in range(size)])  11.2 us
  transfers between devices with their start and end apart: 18, of which 13 were waited for; matrix products, arithmetic and copies ran while one was open for 6% of the time, Pallas kernels for 13%

profile of v5, /device:TPU:0, one launch (start us, length us, event | category | flops | bytes accessed | tf_op | source)
XLA Modules:
  0.0 490.8 jit_solution(11472410773830581818)
XLA Ops:
  7.2 2.3 convert_element_type.158
  10.2 15.7 %psum.7 = f32[]{:T(128)} all-reduce(f32[]{:T(128)} %convert_reduce_fusion.1), channel_id=1, replica_groups=mesh['dp'=8,'mlp'=4] {'dp'}, use_global_device_ids=true, to_apply=%region_1.2 | all-reduce | flops 1 | bytes 8 | tf_op jit(solution)/shard_map/psum | solution.py:808
  27.0 4.2 pad.64.pixels
  45.0 105.0 %all-gather.3.cloned.1.call-done = bf16[13824,768]{1,0:T(8,128)(2,1)} async-done(((bf16[432,768]{1,0:T(8,128)(2,1)}), bf16[13824,768]{1,0:T(8,128)(2,1)}) %all-gather.3.cloned.1.call-update) | async-done | bytes 21233680 | tf_op jit(solution)/shard_map/all_gather | solution.py:771
  150.0 37.9 %time_forward.1 = (f32[6,208,768]{2,1,0:T(8,128)}, bf16[12,208,768]{2,1,0:T(8,128)(2,1)}, bf16[12,208,768]{2,1,0:T(8,128)(2,1)}, f32[12,208,128]{2,1,0:T(8,128)}...) custom-call(s32[272]{0:T(512)} %copy-done, ...), custom_call_target="tpu_custom_call" | custom-call | flops 41221619712 | bytes 9437184 | tf_op jit(solution)/shard_map/time_forward/pallas_call | solution.py:885
  187.8 40.0 %space_forward.1 = (bf16[6,208,768]{2,1,0:T(8,128)(2,1)}, bf16[6,208,768]{2,1,0:T(8,128)(2,1)}, f32[6,208,128]{2,1,0:T(8,128)}, bf16[6,208,768]{2,1,0:T(8,128)(2...) custom-call(s32[272]{0:T(512)} %copy-done, ...), custom_call_target="tpu_custom_call" | custom-call | flops 44166021120 | bytes 9437184 | tf_op jit(solution)/shard_map/space_forward/pallas_call | solution.py:885
  228.0 4.0 collective-permute-done.refs_2_
  232.6 29.3 %mlp_backward.1 = (f32[6,208,768]{2,1,0:T(8,128)}, bf16[6,208,768]{2,1,0:T(8,128)(2,1)}, bf16[2,6,208,768]{3,2,1,0:T(8,128)(2,1)}, f32[8,768]{1,0:T(8,128)}, f32[8,768]{1,0:T(8,128)}) custom-call(s32[272]{0:T(512)} %copy-done, f32[6]{0:T(128)} %dynamic_slice.36.fw, s32[1]{0:T(128)} %bitcast.3.member.m, bf16[288,48,768]{2,1,0:T(8,128)(2,1)} %bitcast.129, ...), custom_call_target="tpu_custom_call" | custom-call | flops 26499612672 | bytes 9437184 | tf_op jit(solution)/shard_map/mlp_backward/pallas_call | solution.py:885
  262.0 30.3 %space_backward.1 = (bf16[6,208,768]{2,1,0:T(8,128)(2,1)}, bf16[6,208,3072]{2,1,0:T(8,128)(2,1)}, f32[8,768]{1,0:T(8,128)}) custom-call(s32[272]{0:T(512)} %copy-done, bf16[288,48,768]{2,1,0:T(8,128)(2,1)} %bitcast.130, f32[6,208,768]{2,1,0:T(8,128)} %get-tuple-element.93.dx2, bf16[6,208,768]{2,1,0:T(8,128)(2,1)} %get-tuple-element.94.hat1, ...), custom_call_target="tpu_custom_call" | custom-call | flops 32388415488 | bytes 9437184 | tf_op jit(solution)/shard_map/space_backward/pallas_call | solution.py:885
  293.2 1.6 constant_dynamic-slice_fusion
  295.9 11.6 %mlp_weights.1 = (bf16[2,2,768,384]{3,2,1,0:T(8,128)(2,1)}, bf16[2,2,768,384]{3,2,1,0:T(8,128)(2,1)}) custom-call(s32[1]{0:T(128)} %bitcast.4.core, bf16[6,208,768]{2,1,0:T(8,128)(2,1)} %get-tuple-element.111.hid2, bf16[6,208,768]{2,1,0:T(8,128)(2,1)} %get-tuple-element.112.g3, bf16[2,6,208,768]{3,2,1,0:T(8,128)(2,1)} %get-tuple-element.113.du, ...), custom_call_target="tpu_custom_call" | custom-call | flops 5888802816 | bytes 9437184 | tf_op jit(solution)/shard_map/mlp_weights/pallas_call | solution.py:885
  307.5 10.9 %space_weights.1 = (bf16[2,4,192,384]{3,2,1,0:T(8,128)(2,1)}, bf16[2,4,192,384]{3,2,1,0:T(8,128)(2,1)}, f32[4,8,768]{2,1,0:T(8,128)}) custom-call(s32[1]{0:T(128)} %bitcast.4.core, bf16[400,768]{1,0:T(8,128)(2,1)} %pad_convert_fusion.picked, bf16[6,208,768]{2,1,0:T(8,128)(2,1)} %get-tuple-element.105.hid1, bf16[6,208,768]{2,1,0:T(8,128)(2,1)} %get-tuple-element.106.o, ...), custom_call_target="tpu_custom_call" | custom-call | flops 5888802816 | bytes 9437184 | tf_op jit(solution)/shard_map/space_weights/pallas_call | solution.py:885
  319.8 3.1 collective-permute-done.3
  322.8 2.4 fusion.6
  329.1 41.2 %time_backward.1 = (bf16[2,5,192,384]{3,2,1,0:T(8,128)(2,1)}, bf16[2,5,192,384]{3,2,1,0:T(8,128)(2,1)}, f32[8,768]{1,0:T(8,128)}, f32[112,768]{1,0:T(8,128)}, f32[12,768]{1,0:T(8,128)}) custom-call(s32[272]{0:T(512)} %copy-done, s32[1]{0:T(128)} %bitcast.3.member.m, s32[1]{0:T(128)} %bitcast.4.core, bf16[288,48,768]{2,1,0:T(8,128)(2,1)} %bitcast.131, ...), custom_call_target="tpu_custom_call" | custom-call | flops 52999225344 | bytes 9437184 | tf_op jit(solution)/shard_map/time_backward/pallas_call | solution.py:885
  374.6 1.8 fusion.4
  381.0 2.1 collective-permute-start.9
  383.1 16.8 %collective-permute-done.9.refs_11_ = bf16[8,16,384]{2,1,0:T(8,128)(2,1)S(1)} collective-permute-done((bf16[8,16,384]{2,1,0:T(8,128)(2,1)S(1)}, bf16[8,16,384]{2,1,0:T(8,128)(2,1)S(1)}, u32[]{:S(2)}, u32[]{:S(2)}) %collective-permute-start.9) | collective-permute-done | bytes 98336 | tf_op jit(solution)/shard_map/ppermute | solution.py:676
  400.8 7.0 %pack.1 = (bf16[2,448,384]{2,1,0:T(8,128)(2,1)}, bf16[2,448,384]{2,1,0:T(8,128)(2,1)}, bf16[2,448,384]{2,1,0:T(8,128)(2,1)}, bf16[2,448,384]{2,1,0:T(8,128)(2,1)}) custom-call(s32[68]{0:T(128)} %fusion.46.dests, s32[1]{0:T(128)} %bitcast.2.place, bf16[2,20,48,384]{3,2,1,0:T(8,128)(2,1)} %bitcast.115, bf16[2,16,48,384]{3,2,1,0:T(8,128)(2,1)} %bitcast.117, ...), custom_call_target="tpu_custom_call" | custom-call | tf_op jit(solution)/shard_map/pack/pallas_call | solution.py:1132
  409.9 14.8 %collective-permute-done.12 = bf16[2,448,384]{2,1,0:T(8,128)(2,1)S(1)} collective-permute-done((bf16[2,448,384]{2,1,0:T(8,128)(2,1)}, bf16[2,448,384]{2,1,0:T(8,128)(2,1)S(1)}, u32[]{:S(2)}, u32[]{:S(2)}) %collective-permute-start.12) | collective-permute-done | bytes 688160 | tf_op jit(solution)/shard_map/ppermute | solution.py:676
  431.7 3.7 collective-permute-done.13
  435.4 4.1 collective-permute-done.11
  439.5 1.9 fusion.7
  441.8 2.1 collective-permute-done.14
  449.1 2.9 collective-permute-done.15
  452.0 1.6 collective-permute-start.16
  453.6 4.0 collective-permute-done.16
  457.6 9.9 %all-gather = f32[40,8,768]{2,1,0:T(8,128)S(1)} all-gather(f32[5,8,768]{2,1,0:T(8,128)S(1)} %pad_maximum_fusion.6), channel_id=2, replica_groups=mesh['dp'=8,'mlp'=4] {'dp'}, dimensions={0}, use_global_device_ids=true | all-gather | bytes 1105920 | tf_op jit(solution)/shard_map/all_gather | solution.py:1171
  469.7 1.9 multiply_reduce_fusion.1
  473.7 3.3 multiply_subtract_fusion.2
  477.0 2.8 multiply_subtract_fusion
  480.1 2.5 multiply_subtract_fusion.1
  (189 shorter events, 49.2 us)
Async XLA Ops:
  7.2 19.4 %copy-start.5 = (f32[768,400]{0,1:T(8,128)S(1)}, f32[768,400]{0,1:T(8,128)}, u32[]{:S(2)}) copy-start(f32[768,400]{0,1:T(8,128)} %param.29) | copy-start | bytes 3686404
  7.2 142.8 %all-gather.3.cloned.1.call-start = ((), (), s32[]{:S(2)}) async-start(), calls=%async_computation | async-start | bytes 21897216 | tf_op jit(solution)/shard_map/all_gather | solution.py:771
  31.2 5.4 %copy-start.32 = (s32[1,12]{1,0:T(1,128)S(1)}, s32[1,12]{1,0:T(1,128)}, u32[]{:S(2)}) copy-start(s32[1,12]{1,0:T(1,128)} %param.18) | copy-start | bytes 148
  32.2 6.4 %copy-start.8 = (f32[220,768]{1,0:T(8,128)S(1)}, f32[220,768]{1,0:T(8,128)}, u32[]{:S(2)}) copy-start(f32[220,768]{1,0:T(8,128)} %param.26) | copy-start | bytes 2027524
  33.6 5.0 %copy-start = (s32[272]{0:T(512)}, s32[272]{0:T(512)S(1)}, u32[]{:S(2)}) copy-start(s32[272]{0:T(512)S(1)} %multiply_add_fusion.3.slots.s) | copy-start | bytes 3268
  227.9 4.1 collective-permute-start
  295.9 23.9 %collective-permute-start.1 = (bf16[6,112,768]{2,1,0:T(8,128)(2,1)S(1)}, bf16[6,112,768]{2,1,0:T(8,128)(2,1)}, u32[]{:S(2)}, u32[]{:S(2)}) collective-permute-start(bf16[6,112,768]{2,1,0:T(8,128)(2,1)S(1)} %get-tuple-element.103), channel_id=1, source_target_pairs={{0,1},{1,0},{2,3},{3,2},{4,5},{5,4},{6,7},{7,6},{8,9},{9,8},{10,11... | collective-permute-start | bytes 3096584 | tf_op jit(solution)/shard_map/ppermute | solution.py:676
  307.5 17.8 %collective-permute-start.2 = (bf16[2,2,768,384]{3,2,1,0:T(8,128)(2,1)}, bf16[2,2,768,384]{3,2,1,0:T(8,128)(2,1)S(1)}, u32[]{:S(2)}, u32[]{:S(2)}) collective-permute-start(bf16[2,2,768,384]{3,2,1,0:T(8,128)(2,1)} %get-tuple-element.116), channel_id=1, source_target_pairs={{0,4},{4,0},{8,12},{12,8},{16,20},{20,16},{24,28},{28,24},{1,5},{5... | collective-permute-start | bytes 7077896 | tf_op jit(solution)/shard_map/ppermute | solution.py:676
  307.5 17.8 %copy-start.2 = (bf16[2,2,768,384]{3,2,1,0:T(8,128)(2,1)S(1)}, bf16[2,2,768,384]{3,2,1,0:T(8,128)(2,1)}, u32[]{:S(2)}) copy-start(bf16[2,2,768,384]{3,2,1,0:T(8,128)(2,1)} %get-tuple-element.115) | copy-start | bytes 7077892
  319.8 3.1 collective-permute-start.3
  327.1 43.3 %collective-permute-start.4 = (bf16[2,768,384]{2,1,0:T(8,128)(2,1)}, bf16[2,768,384]{2,1,0:T(8,128)(2,1)S(1)}, u32[]{:S(2)}, u32[]{:S(2)}) collective-permute-start(bf16[2,768,384]{2,1,0:T(8,128)(2,1)} %fusion.3), channel_id=1, source_target_pairs={{0,1},{1,0},{2,3},{3,2},{4,5},{5,4},{6,7},{7,6},{8,9},{9,8},{10,11... | collective-permute-start | bytes 3538952 | tf_op jit(solution)/shard_map/ppermute | solution.py:676
  327.9 42.4 %collective-permute-start.5 = (bf16[4,192,384]{2,1,0:T(8,128)(2,1)}, bf16[4,192,384]{2,1,0:T(8,128)(2,1)S(1)}, u32[]{:S(2)}, u32[]{:S(2)}) collective-permute-start(bf16[4,192,384]{2,1,0:T(8,128)(2,1)} %fusion.6), channel_id=1, source_target_pairs={{0,1},{1,0},{2,3},{3,2},{4,5},{5,4},{6,7},{7,6},{8,9},{9,8},{10,11... | collective-permute-start | bytes 1769480 | tf_op jit(solution)/shard_map/ppermute | solution.py:676
  329.1 42.8 %copy-start.27 = (f32[8,768]{1,0:T(8,128)S(1)}, f32[8,768]{1,0:T(8,128)}, u32[]{:S(2)}) copy-start(f32[8,768]{1,0:T(8,128)} %get-tuple-element.138) | copy-start | bytes 73732
  370.3 6.2 %copy-start.23 = (f32[12,768]{1,0:T(8,128)S(1)}, f32[12,768]{1,0:T(8,128)}, u32[]{:S(2)}) copy-start(f32[12,768]{1,0:T(8,128)} %get-tuple-element.134) | copy-start | bytes 110596
  370.3 6.2 %copy-start.30 = (s32[1,12]{1,0:T(1,128)S(1)}, s32[1,12]{1,0:T(1,128)}, u32[]{:S(2)}) copy-start(s32[1,12]{1,0:T(1,128)} %param.19) | copy-start | bytes 148
  371.1 7.4 %copy-start.16 = (bf16[2,768,384]{2,1,0:T(8,128)(2,1)}, bf16[2,768,384]{2,1,0:T(8,128)(2,1)S(1)}, u32[]{:S(2)}) copy-start(bf16[2,768,384]{2,1,0:T(8,128)(2,1)S(1)} %collective-permute-done.4) | copy-start | bytes 3538948
  371.1 3.5 collective-permute-start.6
  379.2 20.7 %collective-permute-start.8 = (bf16[5,192,384]{2,1,0:T(8,128)(2,1)S(1)}, bf16[5,192,384]{2,1,0:T(8,128)(2,1)S(1)}, u32[]{:S(2)}, u32[]{:S(2)}) collective-permute-start(bf16[5,192,384]{2,1,0:T(8,128)(2,1)S(1)} %fusion.4), channel_id=1, source_target_pairs={{0,1},{1,0},{2,3},{3,2},{4,5},{5,4},{6,7},{7,6},{8,9},{9,8},{10,11... | collective-permute-start | bytes 2211848 | tf_op jit(solution)/shard_map/ppermute | solution.py:676
  379.5 20.4 %copy-start.15 = (bf16[1,2,8,16,384]{4,3,2,1,0:T(8,128)(2,1)}, bf16[1,2,8,16,384]{4,3,2,1,0:T(8,128)(2,1)S(1)}, u32[]{:S(2)}) copy-start(bf16[1,2,8,16,384]{4,3,2,1,0:T(8,128)(2,1)S(1)} %get-tuple-element.165) | copy-start | bytes 589828
  379.5 1.5 collective-permute-start.7
  381.0 18.9 %copy-start.21 = (bf16[2,8,16,384]{3,2,1,0:T(8,128)(2,1)}, bf16[2,8,16,384]{3,2,1,0:T(8,128)(2,1)S(1)}, u32[]{:S(2)}) copy-start(bf16[2,8,16,384]{3,2,1,0:T(8,128)(2,1)S(1)} %collective-permute-done.7.refs_7_) | copy-start | bytes 589828
  381.0 18.8 %collective-permute-start.9 = (bf16[8,16,384]{2,1,0:T(8,128)(2,1)S(1)}, bf16[8,16,384]{2,1,0:T(8,128)(2,1)S(1)}, u32[]{:S(2)}, u32[]{:S(2)}) collective-permute-start(bf16[8,16,384]{2,1,0:T(8,128)(2,1)S(1)} %fusion.18), channel_id=1, source_target_pairs={{0,1},{1,0},{2,3},{3,2},{4,5},{5,4},{6,7},{7,6},{8,9},{9,8},{10,11... | collective-permute-start | bytes 294920 | tf_op jit(solution)/shard_map/ppermute | solution.py:676
  407.8 16.9 %collective-permute-start.12 = (bf16[2,448,384]{2,1,0:T(8,128)(2,1)}, bf16[2,448,384]{2,1,0:T(8,128)(2,1)S(1)}, u32[]{:S(2)}, u32[]{:S(2)}) collective-permute-start(bf16[2,448,384]{2,1,0:T(8,128)(2,1)} %get-tuple-element.146), channel_id=1, source_target_pairs={{0,16},{4,20},{8,24},{12,28},{16,0},{20,4},{24,8},{28,12},{1,17},{... | collective-permute-start | bytes 2064392 | tf_op jit(solution)/shard_map/ppermute | solution.py:676
  409.3 18.9 %collective-permute-start.10 = (bf16[2,448,384]{2,1,0:T(8,128)(2,1)}, bf16[2,448,384]{2,1,0:T(8,128)(2,1)S(1)}, u32[]{:S(2)}, u32[]{:S(2)}) collective-permute-start(bf16[2,448,384]{2,1,0:T(8,128)(2,1)} %get-tuple-element.144), channel_id=1, source_target_pairs={{0,8},{4,12},{8,0},{12,4},{16,24},{20,28},{24,16},{28,20},{1,9},{5... | collective-permute-start | bytes 2064392 | tf_op jit(solution)/shard_map/ppermute | solution.py:676
  426.8 8.6 %collective-permute-start.13 = (bf16[448,384]{1,0:T(8,128)(2,1)}, bf16[448,384]{1,0:T(8,128)(2,1)S(1)}, u32[]{:S(2)}, u32[]{:S(2)}) collective-permute-start(bf16[448,384]{1,0:T(8,128)(2,1)} %fusion.11), channel_id=1, source_target_pairs={{0,8},{4,12},{8,0},{12,4},{16,24},{20,28},{24,16},{28,20},{1,9},{5... | collective-permute-start | bytes 1032200 | tf_op jit(solution)/shard_map/ppermute | solution.py:676
  431.1 8.4 %collective-permute-start.11 = (bf16[448,384]{1,0:T(8,128)(2,1)}, bf16[448,384]{1,0:T(8,128)(2,1)}, u32[]{:S(2)}, u32[]{:S(2)}) collective-permute-start(bf16[448,384]{1,0:T(8,128)(2,1)} %fusion.10), channel_id=1, source_target_pairs={{0,16},{4,20},{8,24},{12,28},{16,0},{20,4},{24,8},{28,12},{1,17},{... | collective-permute-start | bytes 1032200 | tf_op jit(solution)/shard_map/ppermute | solution.py:676
  431.7 9.7 %copy-start.1 = (s32[272]{0:T(512)S(1)}, s32[272]{0:T(512)}, u32[]{:S(2)}) copy-start(s32[272]{0:T(512)} %copy-done) | copy-start | bytes 3268
  435.4 6.1 %copy-start.10 = (bf16[448,384]{1,0:T(8,128)(2,1)}, bf16[448,384]{1,0:T(8,128)(2,1)S(1)}, u32[]{:S(2)}) copy-start(bf16[448,384]{1,0:T(8,128)(2,1)S(1)} %collective-permute-done.13) | copy-start | bytes 1032196
  441.4 2.5 collective-permute-start.14
  446.3 11.2 %copy-start.24 = (f32[8,768]{1,0:T(8,128)S(1)}, f32[8,768]{1,0:T(8,128)}, u32[]{:S(2)}) copy-start(f32[8,768]{1,0:T(8,128)} %get-tuple-element.147) | copy-start | bytes 73732
  448.0 3.9 collective-permute-start.15
  452.0 5.6 %collective-permute-start.16 = (f32[2,8,768]{2,1,0:T(8,128)S(1)}, f32[2,8,768]{2,1,0:T(8,128)S(1)}, u32[]{:S(2)}, u32[]{:S(2)}) collective-permute-start(f32[2,8,768]{2,1,0:T(8,128)S(1)} %pad_maximum_fusion.11), channel_id=1, source_target_pairs={{0,2},{1,3},{2,0},{3,1},{4,6},{5,7},{6,4},{7,5},{8,10},{9,11},{10,... | collective-permute-start | bytes 147464 | tf_op jit(solution)/shard_map/ppermute | solution.py:676
  (19 other events, 47.7 us)
Sparse Core Ops, SparseCore 0:
  11.4 138.5 all-gather.2

commit v6 on v5

--- a/solution.py
+++ b/solution.py
@@ -501,8 +501,8 @@
 
 
 def space_backward(
-    slots, gathered, dx2, hat1, rstd1, q, k, v, rows, extra_q, extra_k,
-    g1_ref, grads_ref, rows_ref, joint, out, row_sums, outer, sems,
+    main, slots, member, gathered, dx2, hat1, rstd1, q, k, v, rows, extra_q, extra_k,
+    near_ref, far_ref, grads_ref, rows_ref, joint, out, row_sums, outer, g1, sems,
 ):
     step = pl.program_id(0)
     cut = hat1.shape
@@ -537,7 +537,12 @@
     row_sums[0] += fold(grad_hidden * xhat)
     row_sums[1] += fold(grad_hidden)
     grad_stream = dx2[...].reshape(flat) + norm_back(grad_hidden, xhat, rstd, rows[0:1])
-    g1_ref[...] = grad_stream.astype(bf16).reshape(cut)
+    g1[...] = grad_stream.astype(bf16).reshape(cut)
+    late = member[0] % 2
+    for ref, which in ((near_ref, late), (far_ref, 1 - late)):
+        ref[:, :main] = g1[:, pl.ds(pl.multiple_of(which * main, 16), main)]
+        if ref.shape[1] > main:
+            ref[:, main:] = g1[:, 2 * main : main + ref.shape[1]]
 
     @pl.when(step == pl.num_programs(0) - 1)
     def _():
@@ -972,32 +977,30 @@
     )
 
     grads_spec = pl.BlockSpec((FRAMES_AT_ONCE, padded, 4 * width), lambda f, *_: (f, 0, 0))
-    g1, grads_space, norm_space = call(
-        space_backward,
+    main = half_blocks * group_rows
+    half_spec = pl.BlockSpec((FRAMES_AT_ONCE, half_rows, width), lambda f, *_: (f, 0, 0))
+    swapped16 = jax.ShapeDtypeStruct((half_frames, half_rows, width), bf16)
+    near, leaving, grads_space, norm_space = call(
+        partial(space_backward, main),
         "space_backward",
         11,
-        [slot_index],
+        [slot_index, member_s],
         space_grid,
         [dx2, hat1, rstd1, q_s, k_s, v_s, space_rows, space_q, space_k],
         [frame_spec] * 2 + [frame_thin] + [frame_spec] * 3 + [rows_spec, space_extra, space_extra],
-        [half16, jax.ShapeDtypeStruct((half_frames, padded, 4 * width), bf16), row32],
-        [frame_spec, grads_spec, rows_spec],
+        [swapped16] * 2
+        + [jax.ShapeDtypeStruct((half_frames, padded, 4 * width), bf16), row32],
+        [half_spec] * 2 + [grads_spec, rows_spec],
         tile_bufs((1, 3), (1, 1))
         + [
             pltpu.VMEM((2, 8, width), f32),
             pltpu.VMEM((frame_rows, width), bf16),
+            pltpu.VMEM((FRAMES_AT_ONCE, padded, width), bf16),
             pltpu.SemaphoreType.DMA((2,)),
         ],
     )
 
-    def patches_of(grad, which):
-        main = half_blocks * group_rows
-        here = lax.dynamic_slice_in_dim(grad, which * main, main, 1)
-        return jnp.concatenate([here, grad[:, 2 * main :]], axis=1)
-
-    leaving, near, late_hid1, late_hid2 = lax.optimization_barrier(
-        (patches_of(g1, 1 - half), patches_of(g1, half), hid1, hid2)
-    )
+    leaving, late_hid1, late_hid2 = lax.optimization_barrier((leaving, hid1, hid2))
     far = swap(leaving, "mlp", 1)
     clip_spec = whole(half_frames, padded, width)
     one_spec = pl.BlockSpec((1, half_frames, padded, width), lambda i, c: (i, 0, 0, 0))

time: 499 us -> 495 us (level)
  no operation moved by 1% of the time
where the time goes in v6:
time: 495 us; the launch traced here: 487 us
  Pallas kernels  208 us (42%)
  waiting for transfers between devices  163 us (33%)
  other arithmetic  33 us (7%)
  blocking collectives  25.6 us (5%)
  local copies, waits for them, and re-layouts  23.3 us (5%)
  between operations  18.8 us (4%)
  starting transfers between devices  11.3 us (2%)
    pallas_call x7, Pallas kernels, call(): pl.pallas_call(kernel, grid_spec=pltpu.PrefetchScalarGridSpec(num_scalar_...  201 us
    all_gather x1, waiting for transfers between devices, local(): lax.all_gather(slot_weight.astype(bf16), ('dp', 'mlp'), axis=0, tiled=True)  105 us
    ppermute x17, waiting for transfers between devices, swap(): return lax.ppermute(value, axis, [(i, i ^ hop) for i in range(size)])  58.4 us
    psum x1, blocking collectives, local(): label_total = lax.psum(jnp.sum(valid_f), 'dp')  15.7 us
    ppermute x17, starting transfers between devices, swap(): return lax.ppermute(value, axis, [(i, i ^ hop) for i in range(size)])  11.3 us
    all_gather x1, blocking collectives, local(): blocks = lax.all_gather(blocks, 'dp', axis=0)  9.91 us
  transfers between devices with their start and end apart: 18, of which 13 were waited for; matrix products, arithmetic and copies ran while one was open for 6% of the time, Pallas kernels for 13%

profile of v6, /device:TPU:0, one launch (start us, length us, event | category | flops | bytes accessed | tf_op | source)
XLA Modules:
  0.0 486.7 jit_solution(16707762638928689768)
XLA Ops:
  7.2 2.3 convert_element_type.158
  10.2 15.7 %psum.7 = f32[]{:T(128)} all-reduce(f32[]{:T(128)} %convert_reduce_fusion.1), channel_id=1, replica_groups=mesh['dp'=8,'mlp'=4] {'dp'}, use_global_device_ids=true, to_apply=%region_1.2 | all-reduce | flops 1 | bytes 8 | tf_op jit(solution)/shard_map/psum | solution.py:813
  27.0 4.2 pad.64.pixels
  45.2 104.8 %all-gather.3.cloned.1.call-done = bf16[13824,768]{1,0:T(8,128)(2,1)} async-done(((bf16[432,768]{1,0:T(8,128)(2,1)}), bf16[13824,768]{1,0:T(8,128)(2,1)}) %all-gather.3.cloned.1.call-update) | async-done | bytes 21233680 | tf_op jit(solution)/shard_map/all_gather | solution.py:776
  150.0 37.9 %time_forward.1 = (f32[6,208,768]{2,1,0:T(8,128)}, bf16[12,208,768]{2,1,0:T(8,128)(2,1)}, bf16[12,208,768]{2,1,0:T(8,128)(2,1)}, f32[12,208,128]{2,1,0:T(8,128)}...) custom-call(s32[272]{0:T(512)} %copy-done, ...), custom_call_target="tpu_custom_call" | custom-call | flops 41221619712 | bytes 9437184 | tf_op jit(solution)/shard_map/time_forward/pallas_call | solution.py:890
  187.9 40.0 %space_forward.1 = (bf16[6,208,768]{2,1,0:T(8,128)(2,1)}, bf16[6,208,768]{2,1,0:T(8,128)(2,1)}, f32[6,208,128]{2,1,0:T(8,128)}, bf16[6,208,768]{2,1,0:T(8,128)(2...) custom-call(s32[272]{0:T(512)} %copy-done, ...), custom_call_target="tpu_custom_call" | custom-call | flops 44166021120 | bytes 9437184 | tf_op jit(solution)/shard_map/space_forward/pallas_call | solution.py:890
  228.0 4.0 collective-permute-done.refs_2_
  232.6 29.3 %mlp_backward.1 = (f32[6,208,768]{2,1,0:T(8,128)}, bf16[6,208,768]{2,1,0:T(8,128)(2,1)}, bf16[2,6,208,768]{3,2,1,0:T(8,128)(2,1)}, f32[8,768]{1,0:T(8,128)}, f32[8,768]{1,0:T(8,128)}) custom-call(s32[272]{0:T(512)} %copy-done, f32[6]{0:T(128)} %dynamic_slice.30.fw, s32[1]{0:T(128)} %bitcast.3.member.m, bf16[288,48,768]{2,1,0:T(8,128)(2,1)} %bitcast.129, ...), custom_call_target="tpu_custom_call" | custom-call | flops 26499612672 | bytes 9437184 | tf_op jit(solution)/shard_map/mlp_backward/pallas_call | solution.py:890
  261.9 30.4 %space_backward.1 = (bf16[6,112,768]{2,1,0:T(8,128)(2,1)}, bf16[6,112,768]{2,1,0:T(8,128)(2,1)}, bf16[6,208,3072]{2,1,0:T(8,128)(2,1)}, f32[8,768]{1,0:T(8,128)}) custom-call(s32[272]{0:T(512)} %copy-done, s32[1]{0:T(128)} %bitcast.3.member.m, bf16[288,48,768]{2,1,0:T(8,128)(2,1)} %bitcast.130, f32[6,208,768]{2,1,0:T(8,128)} %get-tuple-element.93.dx2, ...), custom_call_target="tpu_custom_call" | custom-call | flops 32388415488 | bytes 9437184 | tf_op jit(solution)/shard_map/space_backward/pallas_call | solution.py:890
  292.4 11.7 %mlp_weights.1 = (bf16[2,2,768,384]{3,2,1,0:T(8,128)(2,1)}, bf16[2,2,768,384]{3,2,1,0:T(8,128)(2,1)}) custom-call(s32[1]{0:T(128)} %bitcast.4.core, bf16[6,208,768]{2,1,0:T(8,128)(2,1)} %get-tuple-element.111.hid2, bf16[6,208,768]{2,1,0:T(8,128)(2,1)} %get-tuple-element.112.g3, bf16[2,6,208,768]{3,2,1,0:T(8,128)(2,1)} %get-tuple-element.113.du, ...), custom_call_target="tpu_custom_call" | custom-call | flops 5888802816 | bytes 9437184 | tf_op jit(solution)/shard_map/mlp_weights/pallas_call | solution.py:890
  304.1 10.9 %space_weights.1 = (bf16[2,4,192,384]{3,2,1,0:T(8,128)(2,1)}, bf16[2,4,192,384]{3,2,1,0:T(8,128)(2,1)}, f32[4,8,768]{2,1,0:T(8,128)}) custom-call(s32[1]{0:T(128)} %bitcast.4.core, bf16[400,768]{1,0:T(8,128)(2,1)} %pad_convert_fusion.picked, bf16[6,208,768]{2,1,0:T(8,128)(2,1)} %get-tuple-element.105.hid1, bf16[6,208,768]{2,1,0:T(8,128)(2,1)} %get-tuple-element.106.o, ...), custom_call_target="tpu_custom_call" | custom-call | flops 5888802816 | bytes 9437184 | tf_op jit(solution)/shard_map/space_weights/pallas_call | solution.py:890
  317.4 2.1 collective-permute-done.3
  319.5 1.6 fusion.6
  321.2 1.5 fusion.3
  325.0 41.1 %time_backward.1 = (bf16[2,5,192,384]{3,2,1,0:T(8,128)(2,1)}, bf16[2,5,192,384]{3,2,1,0:T(8,128)(2,1)}, f32[8,768]{1,0:T(8,128)}, f32[112,768]{1,0:T(8,128)}, f32[12,768]{1,0:T(8,128)}) custom-call(s32[272]{0:T(512)} %copy-done, s32[1]{0:T(128)} %bitcast.3.member.m, s32[1]{0:T(128)} %bitcast.4.core, bf16[288,48,768]{2,1,0:T(8,128)(2,1)} %bitcast.131, ...), custom_call_target="tpu_custom_call" | custom-call | flops 52999225344 | bytes 9437184 | tf_op jit(solution)/shard_map/time_backward/pallas_call | solution.py:890
  370.5 1.8 fusion.4
  376.9 2.1 collective-permute-start.9
  379.0 16.8 %collective-permute-done.9.refs_11_ = bf16[8,16,384]{2,1,0:T(8,128)(2,1)S(1)} collective-permute-done((bf16[8,16,384]{2,1,0:T(8,128)(2,1)S(1)}, bf16[8,16,384]{2,1,0:T(8,128)(2,1)S(1)}, u32[]{:S(2)}, u32[]{:S(2)}) %collective-permute-start.9) | collective-permute-done | bytes 98336 | tf_op jit(solution)/shard_map/ppermute | solution.py:681
  396.6 7.0 %pack.1 = (bf16[2,448,384]{2,1,0:T(8,128)(2,1)}, bf16[2,448,384]{2,1,0:T(8,128)(2,1)}, bf16[2,448,384]{2,1,0:T(8,128)(2,1)}, bf16[2,448,384]{2,1,0:T(8,128)(2,1)}) custom-call(s32[68]{0:T(128)} %fusion.46.dests, s32[1]{0:T(128)} %bitcast.2.place, bf16[2,20,48,384]{3,2,1,0:T(8,128)(2,1)} %bitcast.115, bf16[2,16,48,384]{3,2,1,0:T(8,128)(2,1)} %bitcast.117, ...), custom_call_target="tpu_custom_call" | custom-call | tf_op jit(solution)/shard_map/pack/pallas_call | solution.py:1135
  405.7 14.8 %collective-permute-done.12 = bf16[2,448,384]{2,1,0:T(8,128)(2,1)S(1)} collective-permute-done((bf16[2,448,384]{2,1,0:T(8,128)(2,1)}, bf16[2,448,384]{2,1,0:T(8,128)(2,1)S(1)}, u32[]{:S(2)}, u32[]{:S(2)}) %collective-permute-start.12) | collective-permute-done | bytes 688160 | tf_op jit(solution)/shard_map/ppermute | solution.py:681
  427.6 3.7 collective-permute-done.13
  431.2 4.1 collective-permute-done.11
  435.3 1.9 fusion.7
  437.7 2.1 collective-permute-done.14
  444.9 2.9 collective-permute-done.15
  447.8 1.6 collective-permute-start.16
  449.4 4.0 collective-permute-done.16
  453.4 9.9 %all-gather = f32[40,8,768]{2,1,0:T(8,128)S(1)} all-gather(f32[5,8,768]{2,1,0:T(8,128)S(1)} %pad_maximum_fusion.4), channel_id=2, replica_groups=mesh['dp'=8,'mlp'=4] {'dp'}, dimensions={0}, use_global_device_ids=true | all-gather | bytes 1105920 | tf_op jit(solution)/shard_map/all_gather | solution.py:1174
  465.6 1.9 multiply_reduce_fusion.1
  469.5 3.3 multiply_subtract_fusion.2
  472.9 2.8 multiply_subtract_fusion
  476.0 2.5 multiply_subtract_fusion.1
  (188 shorter events, 47.0 us)
Async XLA Ops:
  7.2 19.4 %copy-start.5 = (f32[768,400]{0,1:T(8,128)S(1)}, f32[768,400]{0,1:T(8,128)}, u32[]{:S(2)}) copy-start(f32[768,400]{0,1:T(8,128)} %param.29) | copy-start | bytes 3686404
  7.2 142.8 %all-gather.3.cloned.1.call-start = ((), (), s32[]{:S(2)}) async-start(), calls=%async_computation | async-start | bytes 21897216 | tf_op jit(solution)/shard_map/all_gather | solution.py:776
  31.2 5.5 %copy-start.33 = (s32[1,12]{1,0:T(1,128)S(1)}, s32[1,12]{1,0:T(1,128)}, u32[]{:S(2)}) copy-start(s32[1,12]{1,0:T(1,128)} %param.18) | copy-start | bytes 148
  32.2 6.5 %copy-start.8 = (f32[220,768]{1,0:T(8,128)S(1)}, f32[220,768]{1,0:T(8,128)}, u32[]{:S(2)}) copy-start(f32[220,768]{1,0:T(8,128)} %param.26) | copy-start | bytes 2027524
  33.6 5.1 %copy-start = (s32[272]{0:T(512)}, s32[272]{0:T(512)S(1)}, u32[]{:S(2)}) copy-start(s32[272]{0:T(512)S(1)} %multiply_add_fusion.3.slots.s) | copy-start | bytes 3268
  227.9 4.1 collective-permute-start
  292.3 24.1 %collective-permute-start.1 = (bf16[6,112,768]{2,1,0:T(8,128)(2,1)}, bf16[6,112,768]{2,1,0:T(8,128)(2,1)S(1)}, u32[]{:S(2)}, u32[]{:S(2)}) collective-permute-start(bf16[6,112,768]{2,1,0:T(8,128)(2,1)} %get-tuple-element.103), channel_id=1, source_target_pairs={{0,1},{1,0},{2,3},{3,2},{4,5},{5,4},{6,7},{7,6},{8,9},{9,8},{10,11... | collective-permute-start | bytes 3096584 | tf_op jit(solution)/shard_map/ppermute | solution.py:681
  304.1 17.1 %collective-permute-start.2 = (bf16[2,2,768,384]{3,2,1,0:T(8,128)(2,1)}, bf16[2,2,768,384]{3,2,1,0:T(8,128)(2,1)S(1)}, u32[]{:S(2)}, u32[]{:S(2)}) collective-permute-start(bf16[2,2,768,384]{3,2,1,0:T(8,128)(2,1)} %get-tuple-element.116), channel_id=1, source_target_pairs={{0,4},{4,0},{8,12},{12,8},{16,20},{20,16},{24,28},{28,24},{1,5},{5... | collective-permute-start | bytes 7077896 | tf_op jit(solution)/shard_map/ppermute | solution.py:681
  304.1 17.1 %copy-start.2 = (bf16[2,2,768,384]{3,2,1,0:T(8,128)(2,1)S(1)}, bf16[2,2,768,384]{3,2,1,0:T(8,128)(2,1)}, u32[]{:S(2)}) copy-start(bf16[2,2,768,384]{3,2,1,0:T(8,128)(2,1)} %get-tuple-element.115) | copy-start | bytes 7077892
  316.4 3.1 collective-permute-start.3
  323.0 43.2 %collective-permute-start.4 = (bf16[2,768,384]{2,1,0:T(8,128)(2,1)}, bf16[2,768,384]{2,1,0:T(8,128)(2,1)S(1)}, u32[]{:S(2)}, u32[]{:S(2)}) collective-permute-start(bf16[2,768,384]{2,1,0:T(8,128)(2,1)} %fusion.3), channel_id=1, source_target_pairs={{0,1},{1,0},{2,3},{3,2},{4,5},{5,4},{6,7},{7,6},{8,9},{9,8},{10,11... | collective-permute-start | bytes 3538952 | tf_op jit(solution)/shard_map/ppermute | solution.py:681
  323.7 42.5 %collective-permute-start.5 = (bf16[4,192,384]{2,1,0:T(8,128)(2,1)S(1)}, bf16[4,192,384]{2,1,0:T(8,128)(2,1)S(1)}, u32[]{:S(2)}, u32[]{:S(2)}) collective-permute-start(bf16[4,192,384]{2,1,0:T(8,128)(2,1)S(1)} %fusion.6), channel_id=1, source_target_pairs={{0,1},{1,0},{2,3},{3,2},{4,5},{5,4},{6,7},{7,6},{8,9},{9,8},{10,11... | collective-permute-start | bytes 1769480 | tf_op jit(solution)/shard_map/ppermute | solution.py:681
  325.0 42.8 %copy-start.27 = (f32[8,768]{1,0:T(8,128)S(1)}, f32[8,768]{1,0:T(8,128)}, u32[]{:S(2)}) copy-start(f32[8,768]{1,0:T(8,128)} %get-tuple-element.138) | copy-start | bytes 73732
  366.1 6.2 %copy-start.23 = (f32[12,768]{1,0:T(8,128)S(1)}, f32[12,768]{1,0:T(8,128)}, u32[]{:S(2)}) copy-start(f32[12,768]{1,0:T(8,128)} %get-tuple-element.134) | copy-start | bytes 110596
  366.2 6.2 %copy-start.30 = (s32[1,12]{1,0:T(1,128)S(1)}, s32[1,12]{1,0:T(1,128)}, u32[]{:S(2)}) copy-start(s32[1,12]{1,0:T(1,128)} %param.19) | copy-start | bytes 148
  367.0 7.4 %copy-start.16 = (bf16[2,768,384]{2,1,0:T(8,128)(2,1)}, bf16[2,768,384]{2,1,0:T(8,128)(2,1)S(1)}, u32[]{:S(2)}) copy-start(bf16[2,768,384]{2,1,0:T(8,128)(2,1)S(1)} %collective-permute-done.4) | copy-start | bytes 3538948
  367.0 3.5 collective-permute-start.6
  375.0 20.7 %collective-permute-start.8 = (bf16[5,192,384]{2,1,0:T(8,128)(2,1)S(1)}, bf16[5,192,384]{2,1,0:T(8,128)(2,1)S(1)}, u32[]{:S(2)}, u32[]{:S(2)}) collective-permute-start(bf16[5,192,384]{2,1,0:T(8,128)(2,1)S(1)} %fusion.4), channel_id=1, source_target_pairs={{0,1},{1,0},{2,3},{3,2},{4,5},{5,4},{6,7},{7,6},{8,9},{9,8},{10,11... | collective-permute-start | bytes 2211848 | tf_op jit(solution)/shard_map/ppermute | solution.py:681
  375.3 20.4 %copy-start.15 = (bf16[1,2,8,16,384]{4,3,2,1,0:T(8,128)(2,1)}, bf16[1,2,8,16,384]{4,3,2,1,0:T(8,128)(2,1)S(1)}, u32[]{:S(2)}) copy-start(bf16[1,2,8,16,384]{4,3,2,1,0:T(8,128)(2,1)S(1)} %get-tuple-element.163) | copy-start | bytes 589828
  375.4 1.5 collective-permute-start.7
  376.9 18.9 %copy-start.21 = (bf16[2,8,16,384]{3,2,1,0:T(8,128)(2,1)}, bf16[2,8,16,384]{3,2,1,0:T(8,128)(2,1)S(1)}, u32[]{:S(2)}) copy-start(bf16[2,8,16,384]{3,2,1,0:T(8,128)(2,1)S(1)} %collective-permute-done.7.refs_7_) | copy-start | bytes 589828
  376.9 18.8 %collective-permute-start.9 = (bf16[8,16,384]{2,1,0:T(8,128)(2,1)S(1)}, bf16[8,16,384]{2,1,0:T(8,128)(2,1)S(1)}, u32[]{:S(2)}, u32[]{:S(2)}) collective-permute-start(bf16[8,16,384]{2,1,0:T(8,128)(2,1)S(1)} %fusion.18), channel_id=1, source_target_pairs={{0,1},{1,0},{2,3},{3,2},{4,5},{5,4},{6,7},{7,6},{8,9},{9,8},{10,11... | collective-permute-start | bytes 294920 | tf_op jit(solution)/shard_map/ppermute | solution.py:681
  403.6 16.9 %collective-permute-start.12 = (bf16[2,448,384]{2,1,0:T(8,128)(2,1)}, bf16[2,448,384]{2,1,0:T(8,128)(2,1)S(1)}, u32[]{:S(2)}, u32[]{:S(2)}) collective-permute-start(bf16[2,448,384]{2,1,0:T(8,128)(2,1)} %get-tuple-element.146), channel_id=1, source_target_pairs={{0,16},{4,20},{8,24},{12,28},{16,0},{20,4},{24,8},{28,12},{1,17},{... | collective-permute-start | bytes 2064392 | tf_op jit(solution)/shard_map/ppermute | solution.py:681
  405.2 18.9 %collective-permute-start.10 = (bf16[2,448,384]{2,1,0:T(8,128)(2,1)}, bf16[2,448,384]{2,1,0:T(8,128)(2,1)S(1)}, u32[]{:S(2)}, u32[]{:S(2)}) collective-permute-start(bf16[2,448,384]{2,1,0:T(8,128)(2,1)} %get-tuple-element.144), channel_id=1, source_target_pairs={{0,8},{4,12},{8,0},{12,4},{16,24},{20,28},{24,16},{28,20},{1,9},{5... | collective-permute-start | bytes 2064392 | tf_op jit(solution)/shard_map/ppermute | solution.py:681
  422.7 8.6 %collective-permute-start.13 = (bf16[448,384]{1,0:T(8,128)(2,1)}, bf16[448,384]{1,0:T(8,128)(2,1)S(1)}, u32[]{:S(2)}, u32[]{:S(2)}) collective-permute-start(bf16[448,384]{1,0:T(8,128)(2,1)} %fusion.11), channel_id=1, source_target_pairs={{0,8},{4,12},{8,0},{12,4},{16,24},{20,28},{24,16},{28,20},{1,9},{5... | collective-permute-start | bytes 1032200 | tf_op jit(solution)/shard_map/ppermute | solution.py:681
  427.0 8.4 %collective-permute-start.11 = (bf16[448,384]{1,0:T(8,128)(2,1)}, bf16[448,384]{1,0:T(8,128)(2,1)}, u32[]{:S(2)}, u32[]{:S(2)}) collective-permute-start(bf16[448,384]{1,0:T(8,128)(2,1)} %fusion.10), channel_id=1, source_target_pairs={{0,16},{4,20},{8,24},{12,28},{16,0},{20,4},{24,8},{28,12},{1,17},{... | collective-permute-start | bytes 1032200 | tf_op jit(solution)/shard_map/ppermute | solution.py:681
  427.6 9.7 %copy-start.1 = (s32[272]{0:T(512)S(1)}, s32[272]{0:T(512)}, u32[]{:S(2)}) copy-start(s32[272]{0:T(512)} %copy-done) | copy-start | bytes 3268
  431.2 6.1 %copy-start.10 = (bf16[448,384]{1,0:T(8,128)(2,1)}, bf16[448,384]{1,0:T(8,128)(2,1)S(1)}, u32[]{:S(2)}) copy-start(bf16[448,384]{1,0:T(8,128)(2,1)S(1)} %collective-permute-done.13) | copy-start | bytes 1032196
  437.3 2.5 collective-permute-start.14
  442.2 11.2 %copy-start.24 = (f32[8,768]{1,0:T(8,128)S(1)}, f32[8,768]{1,0:T(8,128)}, u32[]{:S(2)}) copy-start(f32[8,768]{1,0:T(8,128)} %get-tuple-element.147) | copy-start | bytes 73732
  443.9 3.9 collective-permute-start.15
  447.8 5.6 %collective-permute-start.16 = (f32[2,8,768]{2,1,0:T(8,128)S(1)}, f32[2,8,768]{2,1,0:T(8,128)S(1)}, u32[]{:S(2)}, u32[]{:S(2)}) collective-permute-start(f32[2,8,768]{2,1,0:T(8,128)S(1)} %pad_maximum_fusion.9), channel_id=1, source_target_pairs={{0,2},{1,3},{2,0},{3,1},{4,6},{5,7},{6,4},{7,5},{8,10},{9,11},{10,... | collective-permute-start | bytes 147464 | tf_op jit(solution)/shard_map/ppermute | solution.py:681
  (20 other events, 48.0 us)
Sparse Core Ops, SparseCore 0:
  11.4 138.5 all-gather.2

commit v7 on v6

--- a/solution.py
+++ b/solution.py
@@ -81,19 +81,15 @@
     width = source.shape[2]
     per_tile = width // BR
 
-    def one(i, carry):
-        tile, row = i // per_tile, pl.multiple_of((i % per_tile) * BR, 16)
-        place = pl.ds(row, BR)
-        if across:
-            into = target.at[place, pl.ds(pl.multiple_of(tile * width, width), width)]
-        else:
-            into = target.at[pl.ds(pl.multiple_of(tile * width, 16) + row, BR)]
-        block = first(tile) * per_tile + i % per_tile
-        pltpu.make_async_copy(source.at[slots_ref[block]], into, sem).start()
-        return carry
-
     count = target.shape[0] * target.shape[1] // (width * width)
-    lax.fori_loop(0, count * per_tile, one, 0)
+    for tile in range(count):
+        for i in range(per_tile):
+            if across:
+                into = target.at[pl.ds(i * BR, BR), pl.ds(tile * width, width)]
+            else:
+                into = target.at[pl.ds(tile * width + i * BR, BR)]
+            block = first(tile) * per_tile + i
+            pltpu.make_async_copy(source.at[slots_ref[block]], into, sem).start()
 
 
 def arrive(target, sem):

time: 495 us -> 494 us (level)
  no operation moved by 1% of the time
where the time goes in v7:
time: 494 us; the launch traced here: 486 us
  Pallas kernels  208 us (42%)
  waiting for transfers between devices  163 us (33%)
  other arithmetic  33 us (7%)
  blocking collectives  25.6 us (5%)
  local copies, waits for them, and re-layouts  23.3 us (5%)
  between operations  18.8 us (4%)
  starting transfers between devices  11.3 us (2%)
    pallas_call x7, Pallas kernels, call(): pl.pallas_call(kernel, grid_spec=pltpu.PrefetchScalarGridSpec(num_scalar_...  201 us
    all_gather x1, waiting for transfers between devices, local(): lax.all_gather(slot_weight.astype(bf16), ('dp', 'mlp'), axis=0, tiled=True)  105 us
    ppermute x17, waiting for transfers between devices, swap(): return lax.ppermute(value, axis, [(i, i ^ hop) for i in range(size)])  58.4 us
    psum x1, blocking collectives, local(): label_total = lax.psum(jnp.sum(valid_f), 'dp')  15.7 us
    ppermute x17, starting transfers between devices, swap(): return lax.ppermute(value, axis, [(i, i ^ hop) for i in range(size)])  11.3 us
    all_gather x1, blocking collectives, local(): blocks = lax.all_gather(blocks, 'dp', axis=0)  9.91 us
  transfers between devices with their start and end apart: 18, of which 13 were waited for; matrix products, arithmetic and copies ran while one was open for 6% of the time, Pallas kernels for 13%

profile of v7, /device:TPU:0, one launch (start us, length us, event | category | flops | bytes accessed | tf_op | source)
XLA Modules:
  0.0 486.3 jit_solution(9606842085668761995)
XLA Ops:
  7.2 2.3 convert_element_type.158
  10.2 15.7 %psum.7 = f32[]{:T(128)} all-reduce(f32[]{:T(128)} %convert_reduce_fusion.1), channel_id=1, replica_groups=mesh['dp'=8,'mlp'=4] {'dp'}, use_global_device_ids=true, to_apply=%region_1.2 | all-reduce | flops 1 | bytes 8 | tf_op jit(solution)/shard_map/psum | solution.py:809
  27.0 4.2 pad.64.pixels
  45.2 104.8 %all-gather.3.cloned.1.call-done = bf16[13824,768]{1,0:T(8,128)(2,1)} async-done(((bf16[432,768]{1,0:T(8,128)(2,1)}), bf16[13824,768]{1,0:T(8,128)(2,1)}) %all-gather.3.cloned.1.call-update) | async-done | bytes 21233680 | tf_op jit(solution)/shard_map/all_gather | solution.py:772
  150.0 37.8 %time_forward.1 = (f32[6,208,768]{2,1,0:T(8,128)}, bf16[12,208,768]{2,1,0:T(8,128)(2,1)}, bf16[12,208,768]{2,1,0:T(8,128)(2,1)}, f32[12,208,128]{2,1,0:T(8,128)}...) custom-call(s32[272]{0:T(512)} %copy-done, ...), custom_call_target="tpu_custom_call" | custom-call | flops 41221619712 | bytes 9437184 | tf_op jit(solution)/shard_map/time_forward/pallas_call | solution.py:886
  187.7 39.8 %space_forward.1 = (bf16[6,208,768]{2,1,0:T(8,128)(2,1)}, bf16[6,208,768]{2,1,0:T(8,128)(2,1)}, f32[6,208,128]{2,1,0:T(8,128)}, bf16[6,208,768]{2,1,0:T(8,128)(2...) custom-call(s32[272]{0:T(512)} %copy-done, ...), custom_call_target="tpu_custom_call" | custom-call | flops 44166021120 | bytes 9437184 | tf_op jit(solution)/shard_map/space_forward/pallas_call | solution.py:886
  227.7 4.0 collective-permute-done.refs_2_
  232.3 29.1 %mlp_backward.1 = (f32[6,208,768]{2,1,0:T(8,128)}, bf16[6,208,768]{2,1,0:T(8,128)(2,1)}, bf16[2,6,208,768]{3,2,1,0:T(8,128)(2,1)}, f32[8,768]{1,0:T(8,128)}, f32[8,768]{1,0:T(8,128)}) custom-call(s32[272]{0:T(512)} %copy-done, f32[6]{0:T(128)} %dynamic_slice.30.fw, s32[1]{0:T(128)} %bitcast.3.member.m, bf16[288,48,768]{2,1,0:T(8,128)(2,1)} %bitcast.129, ...), custom_call_target="tpu_custom_call" | custom-call | flops 26499612672 | bytes 9437184 | tf_op jit(solution)/shard_map/mlp_backward/pallas_call | solution.py:886
  261.3 30.4 %space_backward.1 = (bf16[6,112,768]{2,1,0:T(8,128)(2,1)}, bf16[6,112,768]{2,1,0:T(8,128)(2,1)}, bf16[6,208,3072]{2,1,0:T(8,128)(2,1)}, f32[8,768]{1,0:T(8,128)}) custom-call(s32[272]{0:T(512)} %copy-done, s32[1]{0:T(128)} %bitcast.3.member.m, bf16[288,48,768]{2,1,0:T(8,128)(2,1)} %bitcast.130, f32[6,208,768]{2,1,0:T(8,128)} %get-tuple-element.93.dx2, ...), custom_call_target="tpu_custom_call" | custom-call | flops 32388415488 | bytes 9437184 | tf_op jit(solution)/shard_map/space_backward/pallas_call | solution.py:886
  291.9 11.7 %mlp_weights.1 = (bf16[2,2,768,384]{3,2,1,0:T(8,128)(2,1)}, bf16[2,2,768,384]{3,2,1,0:T(8,128)(2,1)}) custom-call(s32[1]{0:T(128)} %bitcast.4.core, bf16[6,208,768]{2,1,0:T(8,128)(2,1)} %get-tuple-element.111.hid2, bf16[6,208,768]{2,1,0:T(8,128)(2,1)} %get-tuple-element.112.g3, bf16[2,6,208,768]{3,2,1,0:T(8,128)(2,1)} %get-tuple-element.113.du, ...), custom_call_target="tpu_custom_call" | custom-call | flops 5888802816 | bytes 9437184 | tf_op jit(solution)/shard_map/mlp_weights/pallas_call | solution.py:886
  303.5 10.9 %space_weights.1 = (bf16[2,4,192,384]{3,2,1,0:T(8,128)(2,1)}, bf16[2,4,192,384]{3,2,1,0:T(8,128)(2,1)}, f32[4,8,768]{2,1,0:T(8,128)}) custom-call(s32[1]{0:T(128)} %bitcast.4.core, bf16[400,768]{1,0:T(8,128)(2,1)} %pad_convert_fusion.picked, bf16[6,208,768]{2,1,0:T(8,128)(2,1)} %get-tuple-element.105.hid1, bf16[6,208,768]{2,1,0:T(8,128)(2,1)} %get-tuple-element.106.o, ...), custom_call_target="tpu_custom_call" | custom-call | flops 5888802816 | bytes 9437184 | tf_op jit(solution)/shard_map/space_weights/pallas_call | solution.py:886
  316.8 2.1 collective-permute-done.3
  318.9 1.6 fusion.6
  320.6 1.5 fusion.3
  324.4 41.3 %time_backward.1 = (bf16[2,5,192,384]{3,2,1,0:T(8,128)(2,1)}, bf16[2,5,192,384]{3,2,1,0:T(8,128)(2,1)}, f32[8,768]{1,0:T(8,128)}, f32[112,768]{1,0:T(8,128)}, f32[12,768]{1,0:T(8,128)}) custom-call(s32[272]{0:T(512)} %copy-done, s32[1]{0:T(128)} %bitcast.3.member.m, s32[1]{0:T(128)} %bitcast.4.core, bf16[288,48,768]{2,1,0:T(8,128)(2,1)} %bitcast.131, ...), custom_call_target="tpu_custom_call" | custom-call | flops 52999225344 | bytes 9437184 | tf_op jit(solution)/shard_map/time_backward/pallas_call | solution.py:886
  370.1 1.8 fusion.4
  376.5 2.1 collective-permute-start.9
  378.6 16.8 %collective-permute-done.9.refs_11_ = bf16[8,16,384]{2,1,0:T(8,128)(2,1)S(1)} collective-permute-done((bf16[8,16,384]{2,1,0:T(8,128)(2,1)S(1)}, bf16[8,16,384]{2,1,0:T(8,128)(2,1)S(1)}, u32[]{:S(2)}, u32[]{:S(2)}) %collective-permute-start.9) | collective-permute-done | bytes 98336 | tf_op jit(solution)/shard_map/ppermute | solution.py:677
  396.3 7.0 %pack.1 = (bf16[2,448,384]{2,1,0:T(8,128)(2,1)}, bf16[2,448,384]{2,1,0:T(8,128)(2,1)}, bf16[2,448,384]{2,1,0:T(8,128)(2,1)}, bf16[2,448,384]{2,1,0:T(8,128)(2,1)}) custom-call(s32[68]{0:T(128)} %fusion.46.dests, s32[1]{0:T(128)} %bitcast.2.place, bf16[2,20,48,384]{3,2,1,0:T(8,128)(2,1)} %bitcast.115, bf16[2,16,48,384]{3,2,1,0:T(8,128)(2,1)} %bitcast.117, ...), custom_call_target="tpu_custom_call" | custom-call | tf_op jit(solution)/shard_map/pack/pallas_call | solution.py:1131
  405.4 14.8 %collective-permute-done.12 = bf16[2,448,384]{2,1,0:T(8,128)(2,1)S(1)} collective-permute-done((bf16[2,448,384]{2,1,0:T(8,128)(2,1)}, bf16[2,448,384]{2,1,0:T(8,128)(2,1)S(1)}, u32[]{:S(2)}, u32[]{:S(2)}) %collective-permute-start.12) | collective-permute-done | bytes 688160 | tf_op jit(solution)/shard_map/ppermute | solution.py:677
  427.2 3.7 collective-permute-done.13
  430.8 4.1 collective-permute-done.11
  435.0 1.9 fusion.7
  437.3 2.1 collective-permute-done.14
  444.5 2.9 collective-permute-done.15
  447.4 1.6 collective-permute-start.16
  449.0 4.0 collective-permute-done.16
  453.1 9.9 %all-gather = f32[40,8,768]{2,1,0:T(8,128)S(1)} all-gather(f32[5,8,768]{2,1,0:T(8,128)S(1)} %pad_maximum_fusion.4), channel_id=2, replica_groups=mesh['dp'=8,'mlp'=4] {'dp'}, dimensions={0}, use_global_device_ids=true | all-gather | bytes 1105920 | tf_op jit(solution)/shard_map/all_gather | solution.py:1170
  465.2 1.9 multiply_reduce_fusion.1
  469.2 3.3 multiply_subtract_fusion.2
  472.5 2.8 multiply_subtract_fusion
  475.6 2.5 multiply_subtract_fusion.1
  (188 shorter events, 46.9 us)
Async XLA Ops:
  7.2 19.4 %copy-start.5 = (f32[768,400]{0,1:T(8,128)S(1)}, f32[768,400]{0,1:T(8,128)}, u32[]{:S(2)}) copy-start(f32[768,400]{0,1:T(8,128)} %param.29) | copy-start | bytes 3686404
  7.2 142.8 %all-gather.3.cloned.1.call-start = ((), (), s32[]{:S(2)}) async-start(), calls=%async_computation | async-start | bytes 21897216 | tf_op jit(solution)/shard_map/all_gather | solution.py:772
  31.2 5.5 %copy-start.33 = (s32[1,12]{1,0:T(1,128)S(1)}, s32[1,12]{1,0:T(1,128)}, u32[]{:S(2)}) copy-start(s32[1,12]{1,0:T(1,128)} %param.18) | copy-start | bytes 148
  32.2 6.5 %copy-start.8 = (f32[220,768]{1,0:T(8,128)S(1)}, f32[220,768]{1,0:T(8,128)}, u32[]{:S(2)}) copy-start(f32[220,768]{1,0:T(8,128)} %param.26) | copy-start | bytes 2027524
  33.6 5.1 %copy-start = (s32[272]{0:T(512)}, s32[272]{0:T(512)S(1)}, u32[]{:S(2)}) copy-start(s32[272]{0:T(512)S(1)} %multiply_add_fusion.3.slots.s) | copy-start | bytes 3268
  227.6 4.1 collective-permute-start
  291.8 24.1 %collective-permute-start.1 = (bf16[6,112,768]{2,1,0:T(8,128)(2,1)}, bf16[6,112,768]{2,1,0:T(8,128)(2,1)S(1)}, u32[]{:S(2)}, u32[]{:S(2)}) collective-permute-start(bf16[6,112,768]{2,1,0:T(8,128)(2,1)} %get-tuple-element.103), channel_id=1, source_target_pairs={{0,1},{1,0},{2,3},{3,2},{4,5},{5,4},{6,7},{7,6},{8,9},{9,8},{10,11... | collective-permute-start | bytes 3096584 | tf_op jit(solution)/shard_map/ppermute | solution.py:677
  303.5 17.0 %collective-permute-start.2 = (bf16[2,2,768,384]{3,2,1,0:T(8,128)(2,1)}, bf16[2,2,768,384]{3,2,1,0:T(8,128)(2,1)S(1)}, u32[]{:S(2)}, u32[]{:S(2)}) collective-permute-start(bf16[2,2,768,384]{3,2,1,0:T(8,128)(2,1)} %get-tuple-element.116), channel_id=1, source_target_pairs={{0,4},{4,0},{8,12},{12,8},{16,20},{20,16},{24,28},{28,24},{1,5},{5... | collective-permute-start | bytes 7077896 | tf_op jit(solution)/shard_map/ppermute | solution.py:677
  303.5 17.1 %copy-start.2 = (bf16[2,2,768,384]{3,2,1,0:T(8,128)(2,1)S(1)}, bf16[2,2,768,384]{3,2,1,0:T(8,128)(2,1)}, u32[]{:S(2)}) copy-start(bf16[2,2,768,384]{3,2,1,0:T(8,128)(2,1)} %get-tuple-element.115) | copy-start | bytes 7077892
  315.9 3.1 collective-permute-start.3
  322.4 43.4 %collective-permute-start.4 = (bf16[2,768,384]{2,1,0:T(8,128)(2,1)}, bf16[2,768,384]{2,1,0:T(8,128)(2,1)S(1)}, u32[]{:S(2)}, u32[]{:S(2)}) collective-permute-start(bf16[2,768,384]{2,1,0:T(8,128)(2,1)} %fusion.3), channel_id=1, source_target_pairs={{0,1},{1,0},{2,3},{3,2},{4,5},{5,4},{6,7},{7,6},{8,9},{9,8},{10,11... | collective-permute-start | bytes 3538952 | tf_op jit(solution)/shard_map/ppermute | solution.py:677
  323.2 42.6 %collective-permute-start.5 = (bf16[4,192,384]{2,1,0:T(8,128)(2,1)S(1)}, bf16[4,192,384]{2,1,0:T(8,128)(2,1)S(1)}, u32[]{:S(2)}, u32[]{:S(2)}) collective-permute-start(bf16[4,192,384]{2,1,0:T(8,128)(2,1)S(1)} %fusion.6), channel_id=1, source_target_pairs={{0,1},{1,0},{2,3},{3,2},{4,5},{5,4},{6,7},{7,6},{8,9},{9,8},{10,11... | collective-permute-start | bytes 1769480 | tf_op jit(solution)/shard_map/ppermute | solution.py:677
  324.4 42.9 %copy-start.27 = (f32[8,768]{1,0:T(8,128)S(1)}, f32[8,768]{1,0:T(8,128)}, u32[]{:S(2)}) copy-start(f32[8,768]{1,0:T(8,128)} %get-tuple-element.138) | copy-start | bytes 73732
  365.8 6.2 %copy-start.23 = (f32[12,768]{1,0:T(8,128)S(1)}, f32[12,768]{1,0:T(8,128)}, u32[]{:S(2)}) copy-start(f32[12,768]{1,0:T(8,128)} %get-tuple-element.134) | copy-start | bytes 110596
  365.8 6.2 %copy-start.30 = (s32[1,12]{1,0:T(1,128)S(1)}, s32[1,12]{1,0:T(1,128)}, u32[]{:S(2)}) copy-start(s32[1,12]{1,0:T(1,128)} %param.19) | copy-start | bytes 148
  366.6 7.4 %copy-start.16 = (bf16[2,768,384]{2,1,0:T(8,128)(2,1)}, bf16[2,768,384]{2,1,0:T(8,128)(2,1)S(1)}, u32[]{:S(2)}) copy-start(bf16[2,768,384]{2,1,0:T(8,128)(2,1)S(1)} %collective-permute-done.4) | copy-start | bytes 3538948
  366.6 3.5 collective-permute-start.6
  374.7 20.7 %collective-permute-start.8 = (bf16[5,192,384]{2,1,0:T(8,128)(2,1)S(1)}, bf16[5,192,384]{2,1,0:T(8,128)(2,1)S(1)}, u32[]{:S(2)}, u32[]{:S(2)}) collective-permute-start(bf16[5,192,384]{2,1,0:T(8,128)(2,1)S(1)} %fusion.4), channel_id=1, source_target_pairs={{0,1},{1,0},{2,3},{3,2},{4,5},{5,4},{6,7},{7,6},{8,9},{9,8},{10,11... | collective-permute-start | bytes 2211848 | tf_op jit(solution)/shard_map/ppermute | solution.py:677
  375.0 20.4 %copy-start.15 = (bf16[1,2,8,16,384]{4,3,2,1,0:T(8,128)(2,1)}, bf16[1,2,8,16,384]{4,3,2,1,0:T(8,128)(2,1)S(1)}, u32[]{:S(2)}) copy-start(bf16[1,2,8,16,384]{4,3,2,1,0:T(8,128)(2,1)S(1)} %get-tuple-element.163) | copy-start | bytes 589828
  375.0 1.5 collective-permute-start.7
  376.5 18.9 %copy-start.21 = (bf16[2,8,16,384]{3,2,1,0:T(8,128)(2,1)}, bf16[2,8,16,384]{3,2,1,0:T(8,128)(2,1)S(1)}, u32[]{:S(2)}) copy-start(bf16[2,8,16,384]{3,2,1,0:T(8,128)(2,1)S(1)} %collective-permute-done.7.refs_7_) | copy-start | bytes 589828
  376.5 18.8 %collective-permute-start.9 = (bf16[8,16,384]{2,1,0:T(8,128)(2,1)S(1)}, bf16[8,16,384]{2,1,0:T(8,128)(2,1)S(1)}, u32[]{:S(2)}, u32[]{:S(2)}) collective-permute-start(bf16[8,16,384]{2,1,0:T(8,128)(2,1)S(1)} %fusion.18), channel_id=1, source_target_pairs={{0,1},{1,0},{2,3},{3,2},{4,5},{5,4},{6,7},{7,6},{8,9},{9,8},{10,11... | collective-permute-start | bytes 294920 | tf_op jit(solution)/shard_map/ppermute | solution.py:677
  403.3 16.9 %collective-permute-start.12 = (bf16[2,448,384]{2,1,0:T(8,128)(2,1)}, bf16[2,448,384]{2,1,0:T(8,128)(2,1)S(1)}, u32[]{:S(2)}, u32[]{:S(2)}) collective-permute-start(bf16[2,448,384]{2,1,0:T(8,128)(2,1)} %get-tuple-element.146), channel_id=1, source_target_pairs={{0,16},{4,20},{8,24},{12,28},{16,0},{20,4},{24,8},{28,12},{1,17},{... | collective-permute-start | bytes 2064392 | tf_op jit(solution)/shard_map/ppermute | solution.py:677
  404.8 18.9 %collective-permute-start.10 = (bf16[2,448,384]{2,1,0:T(8,128)(2,1)}, bf16[2,448,384]{2,1,0:T(8,128)(2,1)S(1)}, u32[]{:S(2)}, u32[]{:S(2)}) collective-permute-start(bf16[2,448,384]{2,1,0:T(8,128)(2,1)} %get-tuple-element.144), channel_id=1, source_target_pairs={{0,8},{4,12},{8,0},{12,4},{16,24},{20,28},{24,16},{28,20},{1,9},{5... | collective-permute-start | bytes 2064392 | tf_op jit(solution)/shard_map/ppermute | solution.py:677
  422.3 8.6 %collective-permute-start.13 = (bf16[448,384]{1,0:T(8,128)(2,1)}, bf16[448,384]{1,0:T(8,128)(2,1)S(1)}, u32[]{:S(2)}, u32[]{:S(2)}) collective-permute-start(bf16[448,384]{1,0:T(8,128)(2,1)} %fusion.11), channel_id=1, source_target_pairs={{0,8},{4,12},{8,0},{12,4},{16,24},{20,28},{24,16},{28,20},{1,9},{5... | collective-permute-start | bytes 1032200 | tf_op jit(solution)/shard_map/ppermute | solution.py:677
  426.6 8.4 %collective-permute-start.11 = (bf16[448,384]{1,0:T(8,128)(2,1)}, bf16[448,384]{1,0:T(8,128)(2,1)}, u32[]{:S(2)}, u32[]{:S(2)}) collective-permute-start(bf16[448,384]{1,0:T(8,128)(2,1)} %fusion.10), channel_id=1, source_target_pairs={{0,16},{4,20},{8,24},{12,28},{16,0},{20,4},{24,8},{28,12},{1,17},{... | collective-permute-start | bytes 1032200 | tf_op jit(solution)/shard_map/ppermute | solution.py:677
  427.2 9.7 %copy-start.1 = (s32[272]{0:T(512)S(1)}, s32[272]{0:T(512)}, u32[]{:S(2)}) copy-start(s32[272]{0:T(512)} %copy-done) | copy-start | bytes 3268
  430.8 6.1 %copy-start.10 = (bf16[448,384]{1,0:T(8,128)(2,1)}, bf16[448,384]{1,0:T(8,128)(2,1)S(1)}, u32[]{:S(2)}) copy-start(bf16[448,384]{1,0:T(8,128)(2,1)S(1)} %collective-permute-done.13) | copy-start | bytes 1032196
  436.9 2.5 collective-permute-start.14
  441.8 11.2 %copy-start.24 = (f32[8,768]{1,0:T(8,128)S(1)}, f32[8,768]{1,0:T(8,128)}, u32[]{:S(2)}) copy-start(f32[8,768]{1,0:T(8,128)} %get-tuple-element.147) | copy-start | bytes 73732
  443.5 3.9 collective-permute-start.15
  447.4 5.6 %collective-permute-start.16 = (f32[2,8,768]{2,1,0:T(8,128)S(1)}, f32[2,8,768]{2,1,0:T(8,128)S(1)}, u32[]{:S(2)}, u32[]{:S(2)}) collective-permute-start(f32[2,8,768]{2,1,0:T(8,128)S(1)} %pad_maximum_fusion.9), channel_id=1, source_target_pairs={{0,2},{1,3},{2,0},{3,1},{4,6},{5,7},{6,4},{7,5},{8,10},{9,11},{10,... | collective-permute-start | bytes 147464 | tf_op jit(solution)/shard_map/ppermute | solution.py:677
  (20 other events, 48.0 us)
Sparse Core Ops, SparseCore 0:
  11.4 138.5 all-gather.2
